TPU v7x, 256 devices: a whole 4x4x8 slice. The times are simulated.
256 devices in a mesh: ctx: 64 (over z, y, core), tp: 4 (over x).
Axes of the slice: x: 4, y: 4, z: 8, core: 2. Of those that a mesh axis runs over, the one named last changes fastest.
Arguments:
- tokens: bfloat16 [32768, 5376], P(('ctx', 'tp')), may hold values from -8 to 8
- positions: int32 [32768], replicated, may hold values from 0 to 131071, as said below
- w_query: bfloat16 [5376, 2048], P('ctx', 'tp'), may hold values from -1 to 1
- key_matrix: bfloat16 [5376, 1024], P('ctx', 'tp'), may hold values from -1 to 1
- value_matrix: bfloat16 [5376, 1024], P('ctx', 'tp'), may hold values from -0.078125 to 0.078125
- w_out: bfloat16 [2048, 5376], P('tp', 'ctx'), may hold values from -0.125 to 0.125
- gain_in: float32 [5376], replicated, may hold values from 0.1 to 1.9
- gain_query: float32 [128], replicated, may hold values from 0.5 to 14
- gain_key: float32 [128], replicated, may hold values from 0.5 to 14
- gain_post: float32 [5376], replicated, may hold values from 0.1 to 1.9
Outputs:
- layer_out: bfloat16 [32768, 5376], P(('ctx', 'tp'))
Inputs may be any that keep to these rules, and one draw needn't show every extreme that they name: (positions) rise strictly along the tokens, by 1 to 4 from one token to the next, and the last token stands at 131071.
All inputs are finite; a program needn't handle non-finite values.
Results may differ from a plain program's by a relative error of at most 0.013.
The roundings to bfloat16 on the way count: a program that leaves them out, or rounds other values in their place, can miss the bound.
Values may be sent and summed in bfloat16 or wider, within the bound.
No kernel may reach another device: no remote copies, remote signals or barrier semaphores. Data moves between devices by JAX's collectives and lax.ppermute only.
A program may use at most 128 MiB of HBM per device.

v0:
```python
import jax
import jax.numpy as jnp
from jax import lax
from jax.sharding import PartitionSpec as P

HEAD_SIZE = 128
QS = 168
LOOKBACK_WINDOW = 1024


EPSILON = 1e-06
ROPE_BASE = 10000.0


def shifted(value, axis, steps):
    count = lax.axis_size(axis)
    leading, last = (max(0, -steps), min(count, count - steps))
    return lax.ppermute(value, axis, [(source, source + steps) for source in range(leading, last)])


def row_norm(values, scales):
    mean_square = jnp.mean(values * values, axis=-1, keepdims=True)
    return values * lax.rsqrt(mean_square + EPSILON) * scales


def rotate(head_rows, offsets):
    half_dim = head_rows.shape[-1] // 2
    frequency = ROPE_BASE ** (
        -(jnp.arange(half_dim, dtype=jnp.float32) * 2.0) / head_rows.shape[-1]
    )
    angles = offsets.astype(jnp.float32)[:, None] * frequency[None, :]
    cosine = jnp.cos(angles)[:, None, :]
    sine_wave = jnp.sin(angles)[:, None, :]
    first_half = head_rows[..., :half_dim]
    second_half = head_rows[..., half_dim:]
    return jnp.concatenate(
        [
            first_half * cosine - second_half * sine_wave,
            second_half * cosine + first_half * sine_wave,
        ],
        axis=-1,
    )


def attend(query_matrix, projected_keys, projected_values, query_offsets, key_offsets, key_valid):
    scores = jnp.einsum(
        "qkgd,skd->kgqs", query_matrix, projected_keys, preferred_element_type=jnp.float32
    ) * QS ** (-0.5)
    position_gap = query_offsets[:, None] - key_offsets[None, :]
    allowed = key_valid[None, :] & (position_gap >= 0) & (position_gap < LOOKBACK_WINDOW)
    scores = jnp.where(allowed[None, None], scores, -1e30)
    row_max = jnp.max(scores, axis=-1, keepdims=True)
    weights = jnp.where(allowed[None, None], jnp.exp(scores - row_max), 0.0)
    totals = jnp.sum(weights, axis=-1, keepdims=True)
    rounded = weights.astype(jnp.bfloat16)
    mixed = jnp.einsum(
        "kgqs,skd->qkgd", rounded, projected_values, preferred_element_type=jnp.float32
    )
    mixed = mixed / jnp.transpose(totals, (2, 0, 1, 3))
    return mixed.astype(jnp.bfloat16).reshape(query_matrix.shape[0], -1)


def shards(
    tokens,
    positions,
    w_query,
    key_matrix,
    value_matrix,
    w_out,
    gain_in,
    gain_query,
    gain_key,
    gain_post,
):
    gathered = lax.all_gather(tokens, "tp", axis=0, tiled=True)
    normalized_rows = row_norm(gathered.astype(jnp.float32), gain_in).astype(jnp.bfloat16)
    row_count = normalized_rows.shape[0]
    block_start = lax.axis_index("ctx") * row_count
    offsets_all = positions - positions[0]
    query_offsets = lax.dynamic_slice_in_dim(offsets_all, block_start, row_count, 0)

    def add_rows(weight_rows):
        return jnp.dot(normalized_rows, weight_rows, preferred_element_type=jnp.float32)

    query_raw = add_rows(lax.all_gather(w_query, "ctx", axis=0, tiled=True))
    unnormed_keys = add_rows(lax.all_gather(key_matrix, "ctx", axis=0, tiled=True))
    value_raw = add_rows(lax.all_gather(value_matrix, "ctx", axis=0, tiled=True))
    key_heads = key_matrix.shape[1] // HEAD_SIZE
    projected_keys = rotate(
        row_norm(unnormed_keys.reshape(row_count, key_heads, HEAD_SIZE), gain_key), query_offsets
    ).astype(jnp.bfloat16)
    projected_values = value_raw.astype(jnp.bfloat16).reshape(row_count, key_heads, HEAD_SIZE)
    own_pair = jnp.stack([projected_keys, projected_values])
    window_blocks = LOOKBACK_WINDOW // row_count
    earlier = []
    carried = own_pair
    for relay_step in range(window_blocks):
        carried = shifted(carried, "ctx", 1)
        earlier.insert(0, carried)
    window_pair = jnp.concatenate(earlier + [own_pair], axis=1)
    query_heads = w_query.shape[1] // HEAD_SIZE
    query_matrix = rotate(
        row_norm(query_raw.reshape(row_count, query_heads, HEAD_SIZE), gain_query), query_offsets
    ).astype(jnp.bfloat16)
    query_matrix = query_matrix.reshape(row_count, key_heads, query_heads // key_heads, HEAD_SIZE)
    padded_offsets = jnp.concatenate(
        [jnp.zeros((LOOKBACK_WINDOW,), jnp.int32), offsets_all], axis=0
    )
    key_offsets = lax.dynamic_slice_in_dim(
        padded_offsets, block_start, LOOKBACK_WINDOW + row_count, 0
    )
    key_valid = (
        block_start + jnp.arange(LOOKBACK_WINDOW + row_count, dtype=jnp.int32) >= LOOKBACK_WINDOW
    )
    attended = attend(
        query_matrix, window_pair[0], window_pair[1], query_offsets, key_offsets, key_valid
    )
    projected = jnp.dot(
        attended,
        lax.all_gather(w_out, "ctx", axis=1, tiled=True),
        preferred_element_type=jnp.float32,
    )
    summed = lax.psum_scatter(
        projected.astype(jnp.bfloat16), "tp", scatter_dimension=0, tiled=True
    ).astype(jnp.float32)
    return (tokens.astype(jnp.float32) + row_norm(summed, gain_post)).astype(jnp.bfloat16)


def solution(mesh):
    in_specs = (
        P(("ctx", "tp"), None),
        P(),
        P("ctx", "tp"),
        P("ctx", "tp"),
        P("ctx", "tp"),
        P("tp", "ctx"),
        P(),
        P(),
        P(),
        P(),
    )
    out_specs = P(("ctx", "tp"), None)
    return jax.shard_map(shards, mesh=mesh, in_specs=in_specs, out_specs=out_specs, check_vma=False)
```

profile of v0, /device:TPU:25, one launch (start us, length us, event | category | flops | bytes accessed | tf_op | source)
XLA Modules:
  0.0 478.7 jit_solution(11651452583727154229)
XLA Ops:
  6.5 0.7 all-gather.12.cloned.1.call-update
  7.3 0.7 all-gather.14.cloned.1.call-update
  8.1 0.7 all-gather.10.cloned.1.call-update
  8.8 0.5 all-gather.16.cloned.1.call-update
  9.4 0.5 all-gather.18.cloned.1.call-update
  9.9 0.0 reduce-scatter.2.cloned.1.call-start
  10.0 1.2 slice.22
  11.2 1.6 broadcast_subtract_fusion
  12.7 0.1 fusion.41
  12.8 0.5 multiply_cosine_fusion
  13.4 0.1 copy.36
  13.5 0.1 copy.37
  13.6 76.5 %all-gather.12.cloned.1.call-done = bf16[64,84,256]{2,1,0:T(8,128)(2,1)} async-done(((bf16[1,84,256]{2,1,0:T(8,128)(2,1)}), bf16[64,84,256]{2,1,0:T(8,128)(2,1)}) %all-gather.12.cloned.1.call-update) | async-done | bytes 2752528 | tf_op jit(solution)/shard_map/all_gather | solution.py:86
  90.2 3.6 reshape.188
  93.7 74.7 %all-gather.14.cloned.1.call-done = bf16[64,84,256]{2,1,0:T(8,128)(2,1)} async-done(((bf16[1,84,256]{2,1,0:T(8,128)(2,1)}), bf16[64,84,256]{2,1,0:T(8,128)(2,1)}) %all-gather.14.cloned.1.call-update) | async-done | bytes 2752528 | tf_op jit(solution)/shard_map/all_gather | solution.py:87
  168.4 5.1 %reshape.190 = bf16[5376,256]{1,0:T(8,128)(2,1)} reshape(bf16[64,84,256]{2,1,0:T(8,128)(2,1)} %all-gather.14.cloned.1.call-done) | data formatting | bytes 5505024
  173.6 56.5 %all-gather.10.cloned.1.call-done = bf16[512,5376]{1,0:T(8,128)(2,1)} async-done(((bf16[128,5376]{1,0:T(8,128)(2,1)}), bf16[512,5376]{1,0:T(8,128)(2,1)}) %all-gather.10.cloned.1.call-update) | async-done | bytes 5505040 | tf_op jit(solution)/shard_map/all_gather | solution.py:75
  230.1 3.9 fusion.1
  234.0 0.3 copy-done
  234.3 3.6 multiply_reduce_fusion.1
  237.8 1.2 copy.35
  239.1 5.4 %convolution_convert_fusion.1 = bf16[512,256]{0,1:T(8,128)(2,1)S(1)} fusion(bf16[5376,256]{1,0:T(8,128)(2,1)} %reshape.190, bf16[512,5376]{1,0:T(8,128)(2,1)} %all-gather.10.cloned.1.call-done, f32[5376]{0:T(1024)} %param.16, f32[512]{0:T(512)S(1)} %add_rsqrt_fusion.2), kind=kOutput, calls=%fused_computation.30 | convolution fusion | flops 1420427264 | bytes 8543232 | tf_op jit(solution)/shard_map/dot_general | solution.py:83
  244.5 0.2 copy.38
  244.7 0.2 multiply_multiply_fusion.1
  244.9 0.2 fusion.28
  245.2 0.2 pad_maximum_fusion
  245.3 3.7 collective-permute-start
  249.0 0.1 pad_dynamic-slice_fusion
  249.1 6.7 %collective-permute-done = bf16[2,512,2,128]{3,1,2,0:T(8,128)(2,1)S(1)} collective-permute-done((bf16[2,512,2,128]{3,1,2,0:T(8,128)(2,1)S(1)}, bf16[2,512,2,128]{3,1,2,0:T(8,128)(2,1)S(1)}, u32[]{:S(2)}, u32[]{:S(2)}) %collective-permute-start) | collective-permute-done | bytes 524320 | tf_op jit(solution)/shard_map/ppermute | solution.py:18
  255.9 6.8 %collective-permute-start.1 = (bf16[2,512,2,128]{3,1,2,0:T(8,128)(2,1)S(1)}, bf16[2,512,2,128]{3,1,2,0:T(8,128)(2,1)S(1)}, u32[]{:S(2)}, u32[]{:S(2)}) collective-permute-start(bf16[2,512,2,128]{3,1,2,0:T(8,128)(2,1)S(1)} %collective-permute-done), channel_id=1, source_target_pairs={{0,4},{4,8},{8,12},{12,16},{16,20},{20,24},{24,28},{28,32},{32,36}... | collective-permute-start | bytes 1572872 | tf_op jit(solution)/shard_map/ppermute | solution.py:18
  262.7 2.0 fusion.11
  264.7 4.5 collective-permute-done.1
  269.2 0.2 maximum_maximum_fusion
  269.4 43.3 %all-gather.16.cloned.1.call-done = bf16[64,84,512]{2,1,0:T(8,128)(2,1)} async-done(((bf16[1,84,512]{2,1,0:T(8,128)(2,1)}), bf16[64,84,512]{2,1,0:T(8,128)(2,1)}) %all-gather.16.cloned.1.call-update) | async-done | bytes 5505040 | tf_op jit(solution)/shard_map/all_gather | solution.py:85
  312.7 8.9 %reshape.192 = bf16[5376,512]{1,0:T(8,128)(2,1)} reshape(bf16[64,84,512]{2,1,0:T(8,128)(2,1)} %all-gather.16.cloned.1.call-done) | data formatting | bytes 11010048
  321.6 8.0 %multiply_reduce_fusion = (f32[512,4]{0,1:T(4,128)S(1)}, f32[512,512]{0,1:T(8,128)S(1)}) fusion(bf16[5376,512]{1,0:T(8,128)(2,1)} %reshape.192, bf16[512,5376]{1,0:T(8,128)(2,1)} %all-gather.10.cloned.1.call-done, f32[5376]{0:T(1024)S(1)} %copy-done.7, f32[512]{0:T(512)S(1)} %add_rsqrt_fusion.2), kind=kOutput, calls=%fused_computation.32 | convolution fusion | flops 2830104576 | bytes 12090368 | tf_op jit(solution)/shard_map/dot_general | solution.py:83
  329.7 0.2 multiply_multiply_fusion
  329.9 0.2 subtract_convert_fusion
  330.0 0.3 copy.39
  330.3 0.3 copy.40
  330.6 9.2 %fusion.42 = (f32[2,2,512]{2,1,0:T(2,128)S(1)}, bf16[2,2,512,1536]{2,3,1,0:T(8,128)(2,1)}) fusion(pred[512,1536]{0,1:T(8,128)(4,1)} %fusion.11, bf16[2,1536,2,128]{3,1,2,0:T(8,128)(2,1)S(1)} %maximum_maximum_fusion, bf16[512,2,2,64]{3,0,2,1:T(8,128)(2,1)S(1)} %bitcast.71, bf16[512,2,2,64]{3,0,2,1:T(8,128)(2,1)S(1)} %bitcast.70), kind=kOutput, calls=%fused_computation.63 | convolution fusion | flops 825230848 | bytes 9707520 | tf_op jit(solution)/shard_map/sub | solution.py:53
  339.8 3.9 fusion.24
  343.7 48.9 %all-gather.18.cloned.1.call-done = bf16[64,84,512]{2,1,0:T(8,128)(2,1)} async-done(((bf16[1,84,512]{2,1,0:T(8,128)(2,1)}), bf16[64,84,512]{2,1,0:T(8,128)(2,1)}) %all-gather.18.cloned.1.call-update) | async-done | bytes 5505040 | tf_op jit(solution)/shard_map/all_gather | solution.py:120
  392.6 8.9 %reshape.194 = bf16[5376,512]{1,0:T(8,128)(2,1)} reshape(bf16[64,84,512]{2,1,0:T(8,128)(2,1)} %all-gather.18.cloned.1.call-done) | data formatting | bytes 11010048
  401.5 7.5 %convolution_convert_fusion = bf16[512,5376]{1,0:T(8,128)(2,1)} fusion(bf16[512,512]{0,1:T(8,128)(2,1)S(1)} %bitcast.78, bf16[5376,512]{1,0:T(8,128)(2,1)} %reshape.194), kind=kOutput, calls=%fused_computation.9 | convolution fusion | flops 2821324800 | bytes 11534336 | tf_op jit(solution)/shard_map/dot_general | solution.py:118
  409.0 58.1 %reduce-scatter.2.cloned.1.call-done = bf16[128,5376]{1,0:T(8,128)(2,1)} async-done(((bf16[512,5376]{1,0:T(8,128)(2,1)}), bf16[128,5376]{1,0:T(8,128)(2,1)}) %reduce-scatter.2.cloned.1.call-update) | async-done | bytes 1376272 | tf_op jit(solution)/shard_map/reduce_scatter | solution.py:123
  467.1 1.7 fusion.12
  468.8 3.0 fusion.15
  (27 shorter events, 0.3 us)
Async XLA Ops:
  6.5 83.6 %all-gather.12.cloned.1.call-start = ((), (), s32[]{:S(2)}) async-start(), calls=%async_computation.3 | async-start | bytes 2928640 | tf_op jit(solution)/shard_map/all_gather | solution.py:86
  7.3 161.2 %all-gather.14.cloned.1.call-start = ((), (), s32[]{:S(2)}) async-start(), calls=%async_computation.4 | async-start | bytes 2928640 | tf_op jit(solution)/shard_map/all_gather | solution.py:87
  8.0 222.1 %all-gather.10.cloned.1.call-start = ((), (), s32[]{:S(2)}) async-start(), calls=%async_computation.1 | async-start | bytes 6881280 | tf_op jit(solution)/shard_map/all_gather | solution.py:75
  8.7 304.0 %all-gather.16.cloned.1.call-start = ((), (), s32[]{:S(2)}) async-start(), calls=%async_computation.5 | async-start | bytes 5857280 | tf_op jit(solution)/shard_map/all_gather | solution.py:85
  9.3 383.3 %all-gather.18.cloned.1.call-start = ((), (), s32[]{:S(2)}) async-start(), calls=%async_computation.6 | async-start | bytes 5857280 | tf_op jit(solution)/shard_map/all_gather | solution.py:120
  9.9 457.2 %reduce-scatter.2.cloned.1.call-start = ((), (), s32[]{:S(2)}) async-start(), calls=%async_computation.2 | async-start | bytes 6881280 | tf_op jit(solution)/shard_map/reduce_scatter | solution.py:123
  12.7 0.6 copy-start.2
  230.1 4.2 copy-start
  239.1 5.6 %copy-start.5 = (f32[128]{0:T(128)S(1)}, f32[128]{0:T(128)}, u32[]{:S(2)}) copy-start(f32[128]{0:T(128)} %param.18) | copy-start | bytes 1540
  239.1 10.0 %copy-start.3 = (s32[32768]{0:T(1024)S(1)}, s32[32768]{0:T(1024)}, u32[]{:S(2)}) copy-start(s32[32768]{0:T(1024)} %copy-done.2) | copy-start | bytes 393220
  245.3 10.5 %collective-permute-start = (bf16[2,512,2,128]{3,1,2,0:T(8,128)(2,1)S(1)}, bf16[2,512,2,128]{3,1,2,0:T(8,128)(2,1)S(1)}, u32[]{:S(2)}, u32[]{:S(2)}) collective-permute-start(bf16[2,512,2,128]{3,1,2,0:T(8,128)(2,1)S(1)} %pad_maximum_fusion), channel_id=1, source_target_pairs={{0,4},{4,8},{8,12},{12,16},{16,20},{20,24},{24,28},{28,32},{32,36}... | collective-permute-start | bytes 1572872 | tf_op jit(solution)/shard_map/ppermute | solution.py:18
  255.9 13.3 %collective-permute-start.1 = (bf16[2,512,2,128]{3,1,2,0:T(8,128)(2,1)S(1)}, bf16[2,512,2,128]{3,1,2,0:T(8,128)(2,1)S(1)}, u32[]{:S(2)}, u32[]{:S(2)}) collective-permute-start(bf16[2,512,2,128]{3,1,2,0:T(8,128)(2,1)S(1)} %collective-permute-done), channel_id=1, source_target_pairs={{0,4},{4,8},{8,12},{12,16},{16,20},{20,24},{24,28},{28,32},{32,36}... | collective-permute-start | bytes 1572872 | tf_op jit(solution)/shard_map/ppermute | solution.py:18
  269.4 52.2 %copy-start.7 = (f32[5376]{0:T(1024)S(1)}, f32[5376]{0:T(1024)}, u32[]{:S(2)}) copy-start(f32[5376]{0:T(1024)} %param.16) | copy-start | bytes 64516
  321.6 8.0 %copy-start.6 = (f32[128]{0:T(128)S(1)}, f32[128]{0:T(128)}, u32[]{:S(2)}) copy-start(f32[128]{0:T(128)} %param.17) | copy-start | bytes 1540
  409.0 59.8 %copy-start.1 = (bf16[128,5376]{1,0:T(8,128)(2,1)S(1)}, bf16[128,5376]{1,0:T(8,128)(2,1)}, u32[]{:S(2)}) copy-start(bf16[128,5376]{1,0:T(8,128)(2,1)} %param.10) | copy-start | bytes 4128772
  409.0 59.8 %copy-start.4 = (f32[5376]{0:T(1024)S(1)}, f32[5376]{0:T(1024)}, u32[]{:S(2)}) copy-start(f32[5376]{0:T(1024)} %param.19) | copy-start | bytes 64516
Sparse Core Ops, SparseCore 0:
  10.0 80.0 all-gather.11
  92.9 75.5 all-gather.13
  170.2 59.8 all-gather.9
  232.7 79.9 all-gather.15
  315.3 77.2 all-gather.17
  409.1 57.9 reduce-scatter.1
where the time goes:
time: 481 us; the launch traced here: 479 us
  waiting for transfers between devices  373 us (78%)
  matrix products  37.5 us (8%)
  local copies, waits for them, and re-layouts  30.3 us (6%)
  other arithmetic  13.9 us (3%)
  between operations  13.7 us (3%)
  starting transfers between devices  10.7 us (2%)
    all_gather x1, waiting for transfers between devices, shards(): lax.all_gather(key_matrix, 'ctx', axis=0, tiled=True)  76.5 us
    all_gather x1, waiting for transfers between devices, shards(): lax.all_gather(value_matrix, 'ctx', axis=0, tiled=True)  74.7 us
    reduce_scatter x1, waiting for transfers between devices, shards(): lax.psum_scatter(projected.astype(jnp.bfloat16), 'tp', scatter_dimension=...  58.1 us
    all_gather x1, waiting for transfers between devices, shards(): gathered = lax.all_gather(tokens, 'tp', axis=0, tiled=True)  56.5 us
    all_gather x1, waiting for transfers between devices, shards(): lax.all_gather(w_out, 'ctx', axis=1, tiled=True)  48.9 us
    all_gather x1, waiting for transfers between devices, shards(): query_raw = add_rows(lax.all_gather(w_query, 'ctx', axis=0, tiled=True))  43.3 us
    unnamed x20, local copies, waits for them, and re-layouts  26.8 us
    dot_general x3, matrix products, add_rows(): jnp.dot(normalized_rows, weight_rows, preferred_element_type=jnp.float32)  17 us
  transfers between devices with their start and end apart: 8, of which 8 were waited for; matrix products, arithmetic and copies ran while one was open for 13% of the time, Pallas kernels for 0%

commit v1 on v0

v1 whole, which is shorter than its diff:
```python
import functools

import jax
import jax.numpy as jnp
from jax import lax
from jax.experimental import pallas as pl
from jax.experimental.pallas import tpu as pltpu
from jax.sharding import PartitionSpec as P

HEAD_SIZE = 128
QS = 168
LOOKBACK_WINDOW = 1024
EPSILON = 1e-06
ROPE_BASE = 10000.0
Z, Y, C, X = 8, 4, 2, 4
BLOCK = 512
PAIR = 1024
VMEM = pltpu.VMEM
MIB = 1024 * 1024


def ctx_pairs(move):
    pairs = []
    for source in range(Z * Y * C):
        target = move(source // (Y * C), source // C % Y, source % C)
        if target is not None:
            z, y, c = target
            pairs.append((source, (z % Z) * Y * C + (y % Y) * C + c))
    return pairs


def swap_cores(value):
    return lax.ppermute(value, "ctx", ctx_pairs(lambda z, y, c: (z, y, 1 - c)))


def shift_x(value, steps):
    return lax.ppermute(value, "tp", [(x, (x + steps) % X) for x in range(X)])


def next_pair(value):
    pairs = [(source, source + C) for source in range(Z * Y * C - C)]
    return lax.ppermute(value, "ctx", pairs)


PLANES = [[z * Y * C + y * C + c for z in range(Z) for y in range(Y)] for c in range(C)]


def norm_body(rows_ref, gain_ref, out_ref):
    rows = rows_ref[...].astype(jnp.float32)
    scale = lax.rsqrt(jnp.mean(rows * rows, axis=-1, keepdims=True) + EPSILON)
    out_ref[...] = (rows * scale * gain_ref[...]).astype(jnp.bfloat16)


def input_norm(rows, gain):
    count, width = rows.shape
    step = 32
    return pl.pallas_call(
        norm_body,
        grid=(count // step,),
        in_specs=[
            pl.BlockSpec((step, width), lambda i: (i, 0)),
            pl.BlockSpec((1, width), lambda i: (0, 0)),
        ],
        out_specs=pl.BlockSpec((step, width), lambda i: (i, 0)),
        out_shape=jax.ShapeDtypeStruct(rows.shape, jnp.bfloat16),
        name="input_norm",
    )(rows, gain.reshape(1, width))


def head_norm_rope(raw, gain, cosine, sine):
    scale = lax.rsqrt(jnp.mean(raw * raw, axis=-1, keepdims=True) + EPSILON)
    normed = raw * scale * gain
    return normed * cosine + pltpu.roll(normed, HEAD_SIZE // 2, 1) * sine


def project_body(kinds, place_ref, *refs):
    pieces = refs[:10]
    weight_ref, gain_ref, cos_ref, sin_ref, out_ref, rows_ref, sems = refs[10:]
    x, c = place_ref[0], place_ref[1]
    quarter, half = BLOCK // X, BLOCK // X // 2
    copies = []
    for side in range(2):
        core = c if side == 0 else 1 - c
        own = pieces[5 * side : 5 * side + 5]
        for k, (piece, rel, shift, size) in enumerate(
            [
                (own[0], 0, 0, quarter),
                (own[1], 1, 0, quarter),
                (own[2], 2, 0, half),
                (own[3], 2, half, half),
                (own[4], 3, 0, quarter),
            ]
        ):
            start = pl.multiple_of(core * BLOCK + lax.rem(x + rel, X) * quarter + shift, half)
            copies.append(
                pltpu.make_async_copy(piece, rows_ref.at[pl.ds(start, size)], sems.at[5 * side + k])
            )
    for copy in copies:
        copy.start()
    for side in range(2):
        for copy in copies[5 * side : 5 * side + 5]:
            copy.wait()
        core = c if side == 0 else 1 - c
        start = pl.multiple_of(core * BLOCK, BLOCK)
        raw = jnp.dot(
            rows_ref[pl.ds(start, BLOCK), :], weight_ref[...], preferred_element_type=jnp.float32
        )
        for h, kind in enumerate(kinds):
            head = raw[:, h * HEAD_SIZE : (h + 1) * HEAD_SIZE]
            if kind == "rope":
                head = head_norm_rope(
                    head, gain_ref[...], cos_ref[pl.ds(start, BLOCK), :], sin_ref[pl.ds(start, BLOCK), :]
                )
            out_ref[h, pl.ds(start, BLOCK), :] = head.astype(jnp.bfloat16)


def project(kinds, place, pieces, gathered, column, gain, cosine, sine, name):
    width = gathered.shape[0]
    whole = lambda shape: pl.BlockSpec(shape, lambda i, p: (0,) * len(shape))
    return pl.pallas_call(
        functools.partial(project_body, kinds),
        grid_spec=pltpu.PrefetchScalarGridSpec(
            num_scalar_prefetch=1,
            grid=(1,),
            in_specs=[pl.BlockSpec(memory_space=pl.ANY)] * 10
            + [
                pl.BlockSpec((width, 2 * HEAD_SIZE), lambda i, p: (0, column)),
                whole((1, HEAD_SIZE)),
                whole((PAIR, HEAD_SIZE)),
                whole((PAIR, HEAD_SIZE)),
            ],
            out_specs=whole((2, PAIR, HEAD_SIZE)),
            scratch_shapes=[
                pltpu.VMEM((PAIR, width), jnp.bfloat16),
                pltpu.SemaphoreType.DMA((10,)),
            ],
        ),
        out_shape=jax.ShapeDtypeStruct((2, PAIR, HEAD_SIZE), jnp.bfloat16),
        compiler_params=pltpu.CompilerParams(vmem_limit_bytes=40 * MIB),
        cost_estimate=pl.CostEstimate(
            flops=2 * PAIR * width * 256, bytes_accessed=14 * MIB, transcendentals=0
        ),
        name=name,
    )(place, *pieces, gathered, gain.reshape(1, HEAD_SIZE), cosine, sine)


TILE = 256


def attend_body(q_ref, own_ref, prev_ref, qoff_ref, koff_ref, out_ref):
    for tile in range(PAIR // TILE):
        first, last = tile * TILE, (tile + 1) * TILE
        keys = jnp.concatenate([prev_ref[0, first:], own_ref[0, :last]], axis=0)
        values = jnp.concatenate([prev_ref[1, first:], own_ref[1, :last]], axis=0)
        span = PAIR + TILE
        gap = qoff_ref[first:last, :] - koff_ref[:, first : first + span]
        allowed = (gap >= 0) & (gap < LOOKBACK_WINDOW)
        for h in range(2):
            scores = lax.dot_general(
                q_ref[h, first:last],
                keys,
                (((1,), (1,)), ((), ())),
                preferred_element_type=jnp.float32,
            ) * QS ** (-0.5)
            scores = jnp.where(allowed, scores, -1e30)
            row_max = jnp.max(scores, axis=-1, keepdims=True)
            weights = jnp.exp(scores - row_max)
            totals = jnp.sum(weights, axis=-1, keepdims=True)
            mixed = jnp.dot(
                weights.astype(jnp.bfloat16), values, preferred_element_type=jnp.float32
            )
            out_ref[first:last, h * HEAD_SIZE : (h + 1) * HEAD_SIZE] = (mixed / totals).astype(
                jnp.bfloat16
            )


def attend(queries, own, prev, query_offsets, key_offsets):
    return pl.pallas_call(
        attend_body,
        out_shape=jax.ShapeDtypeStruct((PAIR, 2 * HEAD_SIZE), jnp.bfloat16),
        compiler_params=pltpu.CompilerParams(vmem_limit_bytes=32 * MIB),
        cost_estimate=pl.CostEstimate(
            flops=4 * PAIR * 1280 * 256, bytes_accessed=3 * MIB, transcendentals=2 * PAIR * 1280
        ),
        name="attend",
    )(queries, own, prev, query_offsets, key_offsets)


def out_body(low_ref, high_ref, wlow_ref, whigh_ref, out_ref):
    nt = (((1,), (1,)), ((), ()))
    total = lax.dot_general(low_ref[...], wlow_ref[...], nt, preferred_element_type=jnp.float32)
    total += lax.dot_general(high_ref[...], whigh_ref[...], nt, preferred_element_type=jnp.float32)
    out_ref[...] = total.astype(jnp.bfloat16)


def out_project(own, other, own_weights, other_weights):
    width = own_weights.shape[0]
    step = 768
    return pl.pallas_call(
        out_body,
        grid=(width // step,),
        in_specs=[
            pl.BlockSpec((BLOCK, 256), lambda i: (0, 0)),
            pl.BlockSpec((BLOCK, 256), lambda i: (0, 0)),
            pl.BlockSpec((step, 256), lambda i: (i, 0)),
            pl.BlockSpec((step, 256), lambda i: (i, 0)),
        ],
        out_specs=pl.BlockSpec((BLOCK, step), lambda i: (0, i)),
        out_shape=jax.ShapeDtypeStruct((BLOCK, width), jnp.bfloat16),
        cost_estimate=pl.CostEstimate(
            flops=2 * BLOCK * width * 512, bytes_accessed=12 * MIB, transcendentals=0
        ),
        name="out_project",
    )(own, other, own_weights, other_weights)


def final_body(sum_ref, rows_ref, gain_ref, out_ref):
    summed = sum_ref[...].astype(jnp.float32)
    scale = lax.rsqrt(jnp.mean(summed * summed, axis=-1, keepdims=True) + EPSILON)
    out = rows_ref[...].astype(jnp.float32) + summed * scale * gain_ref[...]
    out_ref[...] = out.astype(jnp.bfloat16)


def final_norm(summed, rows, gain):
    count, width = rows.shape
    step = 32
    block = pl.BlockSpec((step, width), lambda i: (i, 0))
    return pl.pallas_call(
        final_body,
        grid=(count // step,),
        in_specs=[block, block, pl.BlockSpec((1, width), lambda i: (0, 0))],
        out_specs=block,
        out_shape=jax.ShapeDtypeStruct(rows.shape, jnp.bfloat16),
        name="final_norm",
    )(summed, rows, gain.reshape(1, width))


def core_order(first, second, c):
    low = jnp.where(c == 0, first, second)
    high = jnp.where(c == 0, second, first)
    return low, high


def shards(
    tokens,
    positions,
    w_query,
    key_matrix,
    value_matrix,
    w_out,
    gain_in,
    gain_query,
    gain_key,
    gain_post,
):
    ctx = lax.axis_index("ctx")
    c, pair = ctx % C, ctx // C
    x = lax.axis_index("tp")
    place = jnp.stack([x, c]).astype(jnp.int32)

    out_rows = w_out.T
    sides = [
        jnp.concatenate(
            [
                w_query[:, side * 256 : side * 256 + 256],
                key_matrix[:, side * 128 : side * 128 + 128],
                value_matrix[:, side * 128 : side * 128 + 128],
                out_rows[:, side * 256 : side * 256 + 256],
            ],
            axis=1,
        )
        for side in range(2)
    ]
    mine, theirs = core_order(sides[0], sides[1], c)
    received = swap_cores(theirs)
    stacked = jnp.concatenate(core_order(mine, received, c), axis=0)
    gathered = lax.all_gather(stacked, "ctx", axis=0, tiled=True, axis_index_groups=PLANES)

    rows = input_norm(tokens, gain_in)
    from_low, from_high = shift_x(rows, 1), shift_x(rows, -1)
    half = rows.shape[0] // 2
    far_low = shift_x(from_low[:half], 1)
    far_high = shift_x(from_high[half:], -1)
    pieces = [rows, from_high, far_low, far_high, from_low]
    pieces = pieces + [swap_cores(piece) for piece in pieces]

    offsets = positions - positions[0]
    start = pair * PAIR
    query_offsets = lax.dynamic_slice_in_dim(offsets, start, PAIR, 0)
    padded = jnp.concatenate([jnp.full((PAIR,), -(2**30), jnp.int32), offsets])
    key_offsets = lax.dynamic_slice_in_dim(padded, start, 2 * PAIR, 0)
    half_dim = HEAD_SIZE // 2
    frequency = ROPE_BASE ** (-(jnp.arange(half_dim, dtype=jnp.float32) * 2.0) / HEAD_SIZE)
    angles = query_offsets.astype(jnp.float32)[:, None] * frequency[None, :]
    cosine, sine = jnp.cos(angles), jnp.sin(angles)
    cosine = jnp.concatenate([cosine, cosine], axis=1)
    sine = jnp.concatenate([-sine, sine], axis=1)

    own = project(
        ("rope", "plain"), place, pieces, gathered, 1, gain_key, cosine, sine, "kv_project"
    )
    prev = next_pair(own)
    queries = project(
        ("rope", "rope"), place, pieces, gathered, 0, gain_query, cosine, sine, "q_project"
    )
    own_weights = gathered[:, 512:]
    other_weights = swap_cores(own_weights)
    attended = attend(queries, own, prev, query_offsets[:, None], key_offsets[None, :])
    keep = lax.dynamic_slice_in_dim(attended, c * BLOCK, BLOCK, 0)
    give = lax.dynamic_slice_in_dim(attended, (1 - c) * BLOCK, BLOCK, 0)
    other = swap_cores(give)
    projected = out_project(keep, other, own_weights, other_weights)
    summed = lax.psum_scatter(projected, "tp", scatter_dimension=0, tiled=True)
    return final_norm(summed, tokens, gain_post)


def solution(mesh):
    in_specs = (
        P(("ctx", "tp"), None),
        P(),
        P("ctx", "tp"),
        P("ctx", "tp"),
        P("ctx", "tp"),
        P("tp", "ctx"),
        P(),
        P(),
        P(),
        P(),
    )
    out_specs = P(("ctx", "tp"), None)
    return jax.shard_map(shards, mesh=mesh, in_specs=in_specs, out_specs=out_specs, check_vma=False)
```

time: 481 us -> 247 us (0.51)
  waiting for transfers between devices: 373 us -> 146 us
  Pallas kernels: 0 us -> 47.8 us
  matrix products: 37.5 us -> 0 us
  local copies, waits for them, and re-layouts: 30.3 us -> 18.7 us
  other arithmetic: 13.9 us -> 3.84 us
    all_gather x5 -> x1, waiting for transfers between devices: 300 us -> 54.4 us  [shards(): lax.all_gather(stacked, 'ctx', axis=0, tiled=True, axis_index_groups=PLANES)]
    pallas_call x0 -> x6, Pallas kernels: none -> 47.8 us  [the longest x2 23.7 us: project(): pl.pallas_call(functools.partial(project_body, kinds), grid_spec=pltpu.Pr...]
    dot_general x5 -> x0, matrix products: 28.3 us -> none  [the longest x3 17 us: add_rows(): jnp.dot(normalized_rows, weight_rows, preferred_element_type=jnp.float32)]
    ppermute x2 -> x13, waiting for transfers between devices: 11.2 us -> 33.4 us  [the longest x4 28 us: shift_x(): return lax.ppermute(value, 'tp', [(x, (x + steps) % X) for x in range(X)])]
    unnamed x20 -> x38, local copies, waits for them, and re-layouts: 26.8 us -> 7.13 us
    sub x1 -> x0, matrix products: 9.2 us -> none  [attend(): weights = jnp.where(allowed[None, None], jnp.exp(scores - row_max), 0.0)]
    slice x1 -> x6, local copies, waits for them, and re-layouts: 1.2 us -> 8.51 us  [the longest x1 3.56 us: shards(): own_weights = gathered[:, 512:]]
    reduce_sum x2 -> x0, other arithmetic: 5.55 us -> none  [row_norm(): mean_square = jnp.mean(values * values, axis=-1, keepdims=True)]
  transfers between devices with their start and end apart: 8 -> 15, of which waited for: 8 -> 7; matrix products, arithmetic and copies ran while one was open for 13% -> 5% of each run, Pallas kernels for 0% -> 14%
where the time goes in v1:
time: 247 us; the launch traced here: 245 us
  waiting for transfers between devices  146 us (59%)
  Pallas kernels  47.8 us (19%)
  local copies, waits for them, and re-layouts  18.7 us (8%)
  starting transfers between devices  14.7 us (6%)
  between operations  13.7 us (6%)
  other arithmetic  3.84 us (2%)
    reduce_scatter x1, waiting for transfers between devices, shards(): summed = lax.psum_scatter(projected, 'tp', scatter_dimension=0, tiled=True)  58.6 us
    all_gather x1, waiting for transfers between devices, shards(): lax.all_gather(stacked, 'ctx', axis=0, tiled=True, axis_index_groups=PLANES)  54.4 us
    ppermute x4, waiting for transfers between devices, shift_x(): return lax.ppermute(value, 'tp', [(x, (x + steps) % X) for x in range(X)])  28 us
    pallas_call x2, Pallas kernels, project(): pl.pallas_call(functools.partial(project_body, kinds), grid_spec=pltpu.Pr...  23.7 us
    pallas_call x1, Pallas kernels, out_project(): pl.pallas_call(out_body, grid=(width // step,), in_specs=[pl.BlockSpec((B...  8.9 us
    unnamed x38, local copies, waits for them, and re-layouts  7.13 us
    pallas_call x1, Pallas kernels, attend(): pl.pallas_call(attend_body, out_shape=jax.ShapeDtypeStruct((PAIR, 2 * HEA...  7.1 us
    ppermute x8, starting transfers between devices, swap_cores(): return lax.ppermute(value, 'ctx', ctx_pairs(lambda z, y, c: (z, y, 1 - c)))  5.76 us
  transfers between devices with their start and end apart: 15, of which 7 were waited for; matrix products, arithmetic and copies ran while one was open for 5% of the time, Pallas kernels for 14%

profile of v1, /device:TPU:25, one launch (start us, length us, event | category | flops | bytes accessed | tf_op | source)
XLA Modules:
  0.0 245.1 jit_solution(475609086814408448)
XLA Ops:
  6.5 0.9 fusion.2
  7.4 0.8 fusion.4
  8.3 0.8 collective-permute-start.9
  9.0 1.0 collective-permute-done.9
  10.0 0.1 broadcast_select_fusion.1
  10.1 0.8 pad_maximum_fusion.2
  10.9 0.0 reduce-scatter.2.cloned.1.call-start
  10.9 0.6 reshape.20.gain_ref
  11.6 3.9 %input_norm.1.refs_0_ = bf16[128,5376]{1,0:T(8,128)(2,1)} custom-call(bf16[128,5376]{1,0:T(8,128)(2,1)} %rows_ref.3, f32[1,5376]{1,0:T(1,128)} %reshape.20.gain_ref), custom_call_target="tpu_custom_call" | custom-call | tf_op jit(solution)/shard_map/input_norm/pallas_call | solution.py:57
  15.4 1.2 collective-permute-start.1
  16.6 1.5 collective-permute-start
  18.1 0.9 collective-permute-start.4
  19.0 1.2 slice.46
  20.2 28.0 %collective-permute-done.1.refs_4_ = bf16[128,5376]{1,0:T(8,128)(2,1)S(1)} collective-permute-done((bf16[128,5376]{1,0:T(8,128)(2,1)}, bf16[128,5376]{1,0:T(8,128)(2,1)S(1)}, u32[]{:S(2)}, u32[]{:S(2)}) %collective-permute-start.1) | collective-permute-done | bytes 1376288 | tf_op jit(solution)/shard_map/ppermute | solution.py:37
  48.3 0.2 collective-permute-start.2
  48.5 2.0 slice.49
  50.5 2.6 %collective-permute-start.3 = (bf16[64,5376]{1,0:T(8,128)(2,1)}, bf16[64,5376]{1,0:T(8,128)(2,1)}, u32[]{:S(2)}, u32[]{:S(2)}) collective-permute-start(bf16[64,5376]{1,0:T(8,128)(2,1)} %slice.49), channel_id=1, source_target_pairs={{0,3},{1,0},{2,1},{3,2},{4,7},{5,4},{6,5},{7,6},{8,11},{9,8},{10,9... | collective-permute-start | bytes 2064392 | tf_op jit(solution)/shard_map/ppermute | solution.py:37
  53.1 1.8 collective-permute-start.5
  54.8 54.4 %all-gather.2.cloned.1.call-done.refs_10_ = bf16[5376,768]{1,0:T(8,128)(2,1)} async-done(((bf16[168,768]{1,0:T(8,128)(2,1)}), bf16[5376,768]{1,0:T(8,128)(2,1)}) %all-gather.2.cloned.1.call-update) | async-done | bytes 8257552 | tf_op jit(solution)/shard_map/all_gather | solution.py:277
  109.2 3.6 %slice.52.wlow_ref = bf16[5376,256]{1,0:T(8,128)(2,1)} slice(bf16[5376,768]{1,0:T(8,128)(2,1)} %all-gather.2.cloned.1.call-done.refs_10_), slice={[0:5376], [512:768]} | slice | bytes 5505024 | tf_op jit(solution)/shard_map/slice | solution.py:306
  112.8 1.1 copy-done.1
  113.9 1.1 collective-permute-start.12
  114.9 0.6 broadcast_subtract_fusion
  115.6 0.1 collective-permute-start.6
  115.7 0.5 collective-permute-start.7
  116.2 0.1 pad_add_fusion.place_ref
  116.3 1.9 fusion
  118.2 0.3 pad_maximum_fusion
  118.6 2.3 collective-permute-done.6.refs_7_
  120.9 1.0 collective-permute-done.7.refs_8_
  121.9 11.9 %kv_project.1.own_ref = bf16[2,1024,128]{2,1,0:T(8,128)(2,1)} custom-call(s32[2]{0:T(128)S(1)} %pad_add_fusion.place_ref, bf16[128,5376]{1,0:T(8,128)(2,1)S(1)} %copy-done, bf16[128,5376]{1,0:T(8,128)(2,1)} %collective-permute-done.refs_1_, bf16[64,5376]{1,0:T(8,128)(2,1)} %collective-permute-done.2.refs_2_, ...), custom_call_target="tpu_custom_call" | custom-call | flops 2818572288 | bytes 14680064 | tf_op jit(solution)/shard_map/kv_project/pallas_call | solution.py:120
  133.8 3.5 %collective-permute-start.10 = (bf16[2,1024,128]{2,1,0:T(8,128)(2,1)}, bf16[2,1024,128]{2,1,0:T(8,128)(2,1)}, u32[]{:S(2)}, u32[]{:S(2)}) collective-permute-start(bf16[2,1024,128]{2,1,0:T(8,128)(2,1)} %kv_project.1.own_ref), channel_id=1, source_target_pairs={{0,8},{4,12},{8,16},{12,20},{16,24},{20,28},{24,32},{28,36},{32,40... | collective-permute-start | bytes 1572872 | tf_op jit(solution)/shard_map/ppermute | solution.py:42
  137.3 1.0 copy.11.qoff_ref
  138.4 1.3 copy-done.3
  139.7 1.0 copy-done.5
  140.8 1.1 copy-done.7
  141.9 1.1 copy-done.9
  143.0 11.8 %q_project.1.q_ref = bf16[2,1024,128]{2,1,0:T(8,128)(2,1)S(1)} custom-call(s32[2]{0:T(128)S(1)} %pad_add_fusion.place_ref, bf16[128,5376]{1,0:T(8,128)(2,1)S(1)} %copy-done, bf16[128,5376]{1,0:T(8,128)(2,1)} %collective-permute-done.refs_1_, bf16[64,5376]{1,0:T(8,128)(2,1)} %collective-permute-done.2.refs_2_, ...), custom_call_target="tpu_custom_call" | custom-call | flops 2818572288 | bytes 14680064 | tf_op jit(solution)/shard_map/q_project/pallas_call | solution.py:120
  154.8 7.1 %attend.1 = bf16[1024,256]{1,0:T(8,128)(2,1)S(1)} custom-call(bf16[2,1024,128]{2,1,0:T(8,128)(2,1)S(1)} %q_project.1.q_ref, bf16[2,1024,128]{2,1,0:T(8,128)(2,1)} %kv_project.1.own_ref, bf16[2,1024,128]{2,1,0:T(8,128)(2,1)} %collective-permute-done.10.prev_ref, s32[1024,1]{1,0:T(8,128)S(1)} %copy-done.10, s32[1,2048]{1,0:T(1,128)S(1)} %bitcast.8), custom_call_target="tpu_custom_call" | custom-call | flops 1342177280 | bytes 3145728 | tf_op jit(solution)/shard_map/attend/pallas_call | solution.py:178
  161.9 0.7 constant_dynamic-slice_fusion
  162.7 0.7 collective-permute-start.11
  163.3 1.2 collective-permute-done.11.high_ref
  164.5 0.7 copy-done.15
  165.2 8.9 %out_project.1 = bf16[512,5376]{1,0:T(8,128)(2,1)} custom-call(bf16[512,256]{1,0:T(8,128)(2,1)} %get-tuple-element.8.low_ref, bf16[512,256]{1,0:T(8,128)(2,1)} %copy-done.15, bf16[5376,256]{1,0:T(8,128)(2,1)} %slice.52.wlow_ref, bf16[5376,256]{1,0:T(8,128)(2,1)} %collective-permute-done.12.whigh_ref), custom_call_target="tpu_custom_call" | custom-call | flops 2818572288 | bytes 12582912 | tf_op jit(solution)/shard_map/out_project/pallas_call | solution.py:199
  174.1 0.7 copy-done.18
  174.8 0.6 reshape.23.gain_ref
  175.4 58.6 %reduce-scatter.2.cloned.1.call-done.sum_ref = bf16[128,5376]{1,0:T(8,128)(2,1)} async-done(((bf16[512,5376]{1,0:T(8,128)(2,1)}), bf16[128,5376]{1,0:T(8,128)(2,1)}) %reduce-scatter.2.cloned.1.call-update) | async-done | bytes 1376272 | tf_op jit(solution)/shard_map/reduce_scatter | solution.py:313
  234.0 4.2 %final_norm.1 = bf16[128,5376]{1,0:T(8,128)(2,1)} custom-call(bf16[128,5376]{1,0:T(8,128)(2,1)} %reduce-scatter.2.cloned.1.call-done.sum_ref, bf16[128,5376]{1,0:T(8,128)(2,1)} %rows_ref.3, f32[1,5376]{1,0:T(1,128)} %reshape.23.gain_ref), custom_call_target="tpu_custom_call" | custom-call | tf_op jit(solution)/shard_map/final_norm/pallas_call | solution.py:228
  (48 shorter events, 0.2 us)
Async XLA Ops:
  6.5 4.4 %copy-start.17 = (f32[5376]{0:T(1024)S(1)}, f32[5376]{0:T(1024)}, u32[]{:S(2)}) copy-start(f32[5376]{0:T(1024)} %param.16) | copy-start | bytes 64516
  6.5 102.6 %all-gather.2.cloned.1.call-start = ((), (), s32[]{:S(2)}) async-start(), calls=%async_computation.1 | async-start | bytes 8515584 | tf_op jit(solution)/shard_map/all_gather | solution.py:277
  8.3 1.8 collective-permute-start.9
  10.9 223.1 %reduce-scatter.2.cloned.1.call-start = ((), (), s32[]{:S(2)}) async-start(), calls=%async_computation.2 | async-start | bytes 6881280 | tf_op jit(solution)/shard_map/reduce_scatter | solution.py:313
  15.4 32.8 %collective-permute-start.1 = (bf16[128,5376]{1,0:T(8,128)(2,1)}, bf16[128,5376]{1,0:T(8,128)(2,1)S(1)}, u32[]{:S(2)}, u32[]{:S(2)}) collective-permute-start(bf16[128,5376]{1,0:T(8,128)(2,1)} %input_norm.1.refs_0_), channel_id=1, source_target_pairs={{0,1},{1,2},{2,3},{3,0},{4,5},{5,6},{6,7},{7,4},{8,9},{9,10},{10,1... | collective-permute-start | bytes 4128776 | tf_op jit(solution)/shard_map/ppermute | solution.py:37
  16.6 31.9 %collective-permute-start = (bf16[128,5376]{1,0:T(8,128)(2,1)}, bf16[128,5376]{1,0:T(8,128)(2,1)}, u32[]{:S(2)}, u32[]{:S(2)}) collective-permute-start(bf16[128,5376]{1,0:T(8,128)(2,1)} %input_norm.1.refs_0_), channel_id=1, source_target_pairs={{0,3},{1,0},{2,1},{3,2},{4,7},{5,4},{6,5},{7,6},{8,11},{9,8},{10,9... | collective-permute-start | bytes 4128776 | tf_op jit(solution)/shard_map/ppermute | solution.py:37
  18.1 94.7 %collective-permute-start.4 = (bf16[128,5376]{1,0:T(8,128)(2,1)}, bf16[128,5376]{1,0:T(8,128)(2,1)S(1)}, u32[]{:S(2)}, u32[]{:S(2)}) collective-permute-start(bf16[128,5376]{1,0:T(8,128)(2,1)} %input_norm.1.refs_0_), channel_id=1, source_target_pairs={{0,4},{4,0},{8,12},{12,8},{16,20},{20,16},{24,28},{28,24},{32,36},... | collective-permute-start | bytes 4128776 | tf_op jit(solution)/shard_map/ppermute | solution.py:33
  48.3 67.3 %collective-permute-start.2 = (bf16[64,5376]{1,0:T(8,128)(2,1)S(1)}, bf16[64,5376]{1,0:T(8,128)(2,1)}, u32[]{:S(2)}, u32[]{:S(2)}) collective-permute-start(bf16[64,5376]{1,0:T(8,128)(2,1)S(1)} %slice.48), channel_id=1, source_target_pairs={{0,1},{1,2},{2,3},{3,0},{4,5},{5,6},{6,7},{7,4},{8,9},{9,10},{10,1... | collective-permute-start | bytes 2064392 | tf_op jit(solution)/shard_map/ppermute | solution.py:37
  50.5 65.2 %collective-permute-start.3 = (bf16[64,5376]{1,0:T(8,128)(2,1)}, bf16[64,5376]{1,0:T(8,128)(2,1)}, u32[]{:S(2)}, u32[]{:S(2)}) collective-permute-start(bf16[64,5376]{1,0:T(8,128)(2,1)} %slice.49), channel_id=1, source_target_pairs={{0,3},{1,0},{2,1},{3,2},{4,7},{5,4},{6,5},{7,6},{8,11},{9,8},{10,9... | collective-permute-start | bytes 2064392 | tf_op jit(solution)/shard_map/ppermute | solution.py:37
  53.1 68.8 %collective-permute-start.5 = (bf16[128,5376]{1,0:T(8,128)(2,1)}, bf16[128,5376]{1,0:T(8,128)(2,1)}, u32[]{:S(2)}, u32[]{:S(2)}) collective-permute-start(bf16[128,5376]{1,0:T(8,128)(2,1)} %collective-permute-done.refs_1_), channel_id=1, source_target_pairs={{0,4},{4,0},{8,12},{12,8},{16,20},{20,16},{24,28},{28,24},{32,36},... | collective-permute-start | bytes 4128776 | tf_op jit(solution)/shard_map/ppermute | solution.py:33
  54.8 67.0 %collective-permute-start.8 = (bf16[128,5376]{1,0:T(8,128)(2,1)S(1)}, bf16[128,5376]{1,0:T(8,128)(2,1)}, u32[]{:S(2)}, u32[]{:S(2)}) collective-permute-start(bf16[128,5376]{1,0:T(8,128)(2,1)S(1)} %collective-permute-done.1.refs_4_), channel_id=1, source_target_pairs={{0,4},{4,0},{8,12},{12,8},{16,20},{20,16},{24,28},{28,24},{32,36},... | collective-permute-start | bytes 4128776 | tf_op jit(solution)/shard_map/ppermute | solution.py:33
  109.2 5.8 %copy-start.16 = (s32[32768]{0:T(1024)S(1)}, s32[32768]{0:T(1024)}, u32[]{:S(2)}) copy-start(s32[32768]{0:T(1024)} %param.11) | copy-start | bytes 393220
  112.7 1.1 copy-start.1
  113.9 50.6 %collective-permute-start.12 = (bf16[5376,256]{1,0:T(8,128)(2,1)}, bf16[5376,256]{1,0:T(8,128)(2,1)}, u32[]{:S(2)}, u32[]{:S(2)}) collective-permute-start(bf16[5376,256]{1,0:T(8,128)(2,1)} %slice.52.wlow_ref), channel_id=1, source_target_pairs={{0,4},{4,0},{8,12},{12,8},{16,20},{20,16},{24,28},{28,24},{32,36},... | collective-permute-start | bytes 8257544 | tf_op jit(solution)/shard_map/ppermute | solution.py:33
  115.6 0.7 copy-start.13
  115.6 5.2 %collective-permute-start.6 = (bf16[64,5376]{1,0:T(8,128)(2,1)}, bf16[64,5376]{1,0:T(8,128)(2,1)S(1)}, u32[]{:S(2)}, u32[]{:S(2)}) collective-permute-start(bf16[64,5376]{1,0:T(8,128)(2,1)} %collective-permute-done.2.refs_2_), channel_id=1, source_target_pairs={{0,4},{4,0},{8,12},{12,8},{16,20},{20,16},{24,28},{28,24},{32,36},... | collective-permute-start | bytes 2064392 | tf_op jit(solution)/shard_map/ppermute | solution.py:33
  115.7 6.1 %collective-permute-start.7 = (bf16[64,5376]{1,0:T(8,128)(2,1)}, bf16[64,5376]{1,0:T(8,128)(2,1)S(1)}, u32[]{:S(2)}, u32[]{:S(2)}) collective-permute-start(bf16[64,5376]{1,0:T(8,128)(2,1)} %collective-permute-done.3.refs_3_), channel_id=1, source_target_pairs={{0,4},{4,0},{8,12},{12,8},{16,20},{20,16},{24,28},{28,24},{32,36},... | collective-permute-start | bytes 2064392 | tf_op jit(solution)/shard_map/ppermute | solution.py:33
  116.3 5.5 %copy-start.2 = (bf16[128,5376]{1,0:T(8,128)(2,1)S(1)}, bf16[128,5376]{1,0:T(8,128)(2,1)}, u32[]{:S(2)}) copy-start(bf16[128,5376]{1,0:T(8,128)(2,1)} %copy-done.1) | copy-start | bytes 4128772
  118.2 3.6 %copy-start = (bf16[128,5376]{1,0:T(8,128)(2,1)S(1)}, bf16[128,5376]{1,0:T(8,128)(2,1)}, u32[]{:S(2)}) copy-start(bf16[128,5376]{1,0:T(8,128)(2,1)} %input_norm.1.refs_0_) | copy-start | bytes 4128772
  118.2 3.6 %copy-start.11 = (f32[128]{0:T(128)S(1)}, f32[128]{0:T(128)}, u32[]{:S(2)}) copy-start(f32[128]{0:T(128)} %param.18) | copy-start | bytes 1540
  118.6 15.2 %copy-start.4 = (f32[1024,128]{1,0:T(8,128)}, f32[1024,128]{1,0:T(8,128)S(1)}, u32[]{:S(2)}) copy-start(f32[1024,128]{1,0:T(8,128)S(1)} %get-tuple-element.27.refs_13_) | copy-start | bytes 1572868
  120.9 13.0 %copy-start.6 = (bf16[64,5376]{1,0:T(8,128)(2,1)}, bf16[64,5376]{1,0:T(8,128)(2,1)S(1)}, u32[]{:S(2)}) copy-start(bf16[64,5376]{1,0:T(8,128)(2,1)S(1)} %collective-permute-done.6.refs_7_) | copy-start | bytes 2064388
  121.8 12.0 %copy-start.8 = (bf16[64,5376]{1,0:T(8,128)(2,1)}, bf16[64,5376]{1,0:T(8,128)(2,1)S(1)}, u32[]{:S(2)}) copy-start(bf16[64,5376]{1,0:T(8,128)(2,1)S(1)} %collective-permute-done.7.refs_8_) | copy-start | bytes 2064388
  121.9 16.5 %copy-start.14 = (s32[32768]{0:T(1024)S(1)}, s32[32768]{0:T(1024)}, u32[]{:S(2)}) copy-start(s32[32768]{0:T(1024)} %copy-done.13) | copy-start | bytes 393220
  121.9 16.5 %copy-start.12 = (f32[128]{0:T(128)S(1)}, f32[128]{0:T(128)}, u32[]{:S(2)}) copy-start(f32[128]{0:T(128)} %param.17) | copy-start | bytes 1540
  133.8 21.0 %collective-permute-start.10 = (bf16[2,1024,128]{2,1,0:T(8,128)(2,1)}, bf16[2,1024,128]{2,1,0:T(8,128)(2,1)}, u32[]{:S(2)}, u32[]{:S(2)}) collective-permute-start(bf16[2,1024,128]{2,1,0:T(8,128)(2,1)} %kv_project.1.own_ref), channel_id=1, source_target_pairs={{0,8},{4,12},{8,16},{12,20},{16,24},{20,28},{24,32},{28,36},{32,40... | collective-permute-start | bytes 1572872 | tf_op jit(solution)/shard_map/ppermute | solution.py:42
  138.4 1.3 copy-start.3
  139.7 1.0 copy-start.5
  140.8 1.1 copy-start.7
  141.9 1.1 copy-start.9
  143.0 11.8 %copy-start.10 = (s32[1024,1]{1,0:T(8,128)S(1)}, s32[1024,1]{1,0:T(8,128)}, u32[]{:S(2)}) copy-start(s32[1024,1]{1,0:T(8,128)} %copy.11.qoff_ref) | copy-start | bytes 12292
  162.7 1.8 collective-permute-start.11
  164.5 0.7 copy-start.15
  174.1 0.7 copy-start.18
Sparse Core Ops, SparseCore 0:
  11.0 98.1 all-gather.1
  174.2 59.7 reduce-scatter.1

commit v2 on v1

v2 whole, which is shorter than its diff:
```python
import functools

import jax
import jax.numpy as jnp
from jax import lax
from jax.experimental import pallas as pl
from jax.experimental.pallas import tpu as pltpu
from jax.sharding import PartitionSpec as P

HEAD_SIZE = 128
QS = 168
LOOKBACK_WINDOW = 1024
EPSILON = 1e-06
ROPE_BASE = 10000.0
Z, Y, C, X = 8, 4, 2, 4
BLOCK = 512
PAIR = 1024
VMEM = pltpu.VMEM
MIB = 1024 * 1024


def ctx_pairs(move):
    pairs = []
    for source in range(Z * Y * C):
        target = move(source // (Y * C), source // C % Y, source % C)
        if target is not None:
            z, y, c = target
            pairs.append((source, (z % Z) * Y * C + (y % Y) * C + c))
    return pairs


def swap_cores(value):
    return lax.ppermute(value, "ctx", ctx_pairs(lambda z, y, c: (z, y, 1 - c)))


def shift_x(value, steps):
    return lax.ppermute(value, "tp", [(x, (x + steps) % X) for x in range(X)])


def next_pair(value):
    pairs = [(source, source + C) for source in range(Z * Y * C - C)]
    return lax.ppermute(value, "ctx", pairs)


def shift_y(value, steps):
    return lax.ppermute(value, "ctx", ctx_pairs(lambda z, y, c: (z, y + steps, c)))


def shift_z(value, steps):
    return lax.ppermute(value, "ctx", ctx_pairs(lambda z, y, c: (z + steps, y, c)))


def trade_x_z(value):
    pairs = []
    for source in range(Z * Y * C * X):
        ctx, x = source // X, source % X
        z, rest = ctx // (Y * C), ctx % (Y * C)
        pairs.append((source, ((x * 2 + z % 2) * Y * C + rest) * X + z // 2))
    return lax.ppermute(value, ("ctx", "tp"), pairs)


def together(*values):
    return lax.optimization_barrier(values)


ROWS = [[z * Y * C + y * C + c for y in range(Y)] for z in range(Z) for c in range(C)]
COLUMNS = [[z * Y * C + y * C + c for z in range(Z)] for y in range(Y) for c in range(C)]


def norm_body(rows_ref, gain_ref, out_ref):
    rows = rows_ref[...].astype(jnp.float32)
    scale = lax.rsqrt(jnp.mean(rows * rows, axis=-1, keepdims=True) + EPSILON)
    out_ref[...] = (rows * scale * gain_ref[...]).astype(jnp.bfloat16)


def input_norm(rows, gain):
    count, width = rows.shape
    step = 32
    return pl.pallas_call(
        norm_body,
        grid=(count // step,),
        in_specs=[
            pl.BlockSpec((step, width), lambda i: (i, 0)),
            pl.BlockSpec((1, width), lambda i: (0, 0)),
        ],
        out_specs=pl.BlockSpec((step, width), lambda i: (i, 0)),
        out_shape=jax.ShapeDtypeStruct(rows.shape, jnp.bfloat16),
        name="input_norm",
    )(rows, gain.reshape(1, width))


def head_norm_rope(raw, gain, cosine, sine):
    scale = lax.rsqrt(jnp.mean(raw * raw, axis=-1, keepdims=True) + EPSILON)
    normed = raw * scale * gain
    return normed * cosine + pltpu.roll(normed, HEAD_SIZE // 2, 1) * sine


PARTS = 3


def project_body(
    mine, place_ref, rows_hbm, weight_hbm, gq_ref, gk_ref, cos_ref, sin_ref,
    q_ref, kv_ref, rows_ref, weight_ref, total_ref, sems,
):
    c = place_ref[3]
    start = pl.multiple_of((c if mine else 1 - c) * BLOCK, BLOCK)
    step = rows_ref.shape[1] // PARTS
    copies = []
    for k in range(PARTS):
        span = pl.ds(k * step, step)
        copies.append(
            (
                pltpu.make_async_copy(rows_hbm.at[:, span], rows_ref.at[:, span], sems.at[2 * k]),
                pltpu.make_async_copy(
                    weight_hbm.at[span], weight_ref.at[span], sems.at[2 * k + 1]
                ),
            )
        )
    for pair in copies:
        for copy in pair:
            copy.start()
    for k, pair in enumerate(copies):
        for copy in pair:
            copy.wait()
        span = slice(k * step, (k + 1) * step)
        part = jnp.dot(
            rows_ref[:, span], weight_ref[span, :], preferred_element_type=jnp.float32
        )
        if k == 0:
            total_ref[...] = part
        else:
            total_ref[...] += part
    cosine, sine = cos_ref[pl.ds(start, BLOCK), :], sin_ref[pl.ds(start, BLOCK), :]
    heads = [total_ref[:, h * HEAD_SIZE : (h + 1) * HEAD_SIZE] for h in range(4)]
    kv_ref[0] = head_norm_rope(heads[2], gk_ref[...], cosine, sine).astype(jnp.bfloat16)
    kv_ref[1] = heads[3].astype(jnp.bfloat16)
    for h in range(2):
        q_ref[h] = head_norm_rope(heads[h], gq_ref[...], cosine, sine).astype(jnp.bfloat16)


def whole(shape):
    return pl.BlockSpec(shape, lambda i, p: (0,) * len(shape))


SMEM = pl.BlockSpec(memory_space=pltpu.SMEM)
HBM = pl.BlockSpec(memory_space=pltpu.HBM)
HELD = pl.BlockSpec(memory_space=pltpu.VMEM)


def project(mine, place, rows, weights, tables, name):
    width = weights.shape[0]
    head = jax.ShapeDtypeStruct((2, BLOCK, HEAD_SIZE), jnp.bfloat16)
    return pl.pallas_call(
        functools.partial(project_body, mine),
        in_specs=[SMEM, HBM, HBM] + [HELD] * 4,
        out_specs=[HELD] * 2,
        out_shape=[head] * 2,
        scratch_shapes=[
            pltpu.VMEM((BLOCK, width), jnp.bfloat16),
            pltpu.VMEM((width, 512), jnp.bfloat16),
            pltpu.VMEM((BLOCK, 512), jnp.float32),
            pltpu.SemaphoreType.DMA((2 * PARTS,)),
        ],
        compiler_params=pltpu.CompilerParams(vmem_limit_bytes=60 * MIB),
        cost_estimate=pl.CostEstimate(
            flops=2 * BLOCK * width * 512, bytes_accessed=12 * MIB, transcendentals=0
        ),
        name=name,
    )(place, rows, weights, *tables)


def rows_body(place_ref, *refs):
    pieces, out_ref = refs[:5], refs[5]
    x = place_ref[0]
    quarter, half = BLOCK // X, BLOCK // X // 2
    plan = [(0, 0, quarter), (1, 0, quarter), (2, 0, half), (2, half, half), (3, 0, quarter)]
    for piece, (rel, shift, size) in zip(pieces, plan):
        at = pl.multiple_of(lax.rem(x + rel, X) * quarter + shift, half)
        out_ref[pl.ds(at, size), :] = piece[...]


def place_rows(place, pieces):
    width = pieces[0].shape[1]
    step = 768
    return pl.pallas_call(
        rows_body,
        grid_spec=pltpu.PrefetchScalarGridSpec(
            num_scalar_prefetch=1,
            grid=(width // step,),
            in_specs=[pl.BlockSpec((p.shape[0], step), lambda i, p: (0, i)) for p in pieces],
            out_specs=pl.BlockSpec((BLOCK, step), lambda i, p: (0, i)),
        ),
        out_shape=jax.ShapeDtypeStruct((BLOCK, width), jnp.bfloat16),
        cost_estimate=pl.CostEstimate(flops=0, bytes_accessed=11 * MIB, transcendentals=0),
        name="place_rows",
    )(place, *pieces)


TILE = 256
SPAN = PAIR + TILE


def attend_body(mine, place_ref, q_ref, first_ref, second_ref, pfirst_ref, psecond_ref, qoff_ref, koff_ref, out_ref, keys_ref, values_ref):
    c = place_ref[3]
    for base, refs in ((0, (pfirst_ref, psecond_ref)), (PAIR, (first_ref, second_ref))):
        for block, ref in ((c, refs[0]), (1 - c, refs[1])):
            at = pl.multiple_of(base + block * BLOCK, BLOCK)
            keys_ref[pl.ds(at, BLOCK), :] = ref[0]
            values_ref[pl.ds(at, BLOCK), :] = ref[1]
    block = c if mine else 1 - c
    for tile in range(BLOCK // TILE):
        first, last = tile * TILE, (tile + 1) * TILE
        at = pl.multiple_of(block * BLOCK + first, TILE)
        keys = keys_ref[pl.ds(at, SPAN), :]
        values = values_ref[pl.ds(at, SPAN), :]
        gap = qoff_ref[pl.ds(at, TILE), :] - koff_ref[pl.ds(block * (BLOCK // TILE) + tile, 1), :]
        allowed = (gap >= 0) & (gap < LOOKBACK_WINDOW)
        for h in range(2):
            scores = lax.dot_general(
                q_ref[h, first:last],
                keys,
                (((1,), (1,)), ((), ())),
                preferred_element_type=jnp.float32,
            ) * QS ** (-0.5)
            scores = jnp.where(allowed, scores, -1e30)
            row_max = jnp.max(scores, axis=-1, keepdims=True)
            weights = jnp.exp(scores - row_max)
            totals = jnp.sum(weights, axis=-1, keepdims=True)
            mixed = jnp.dot(
                weights.astype(jnp.bfloat16), values, preferred_element_type=jnp.float32
            )
            out_ref[first:last, h * HEAD_SIZE : (h + 1) * HEAD_SIZE] = (mixed / totals).astype(
                jnp.bfloat16
            )


def attend(mine, place, queries, blocks, query_offsets, key_offsets, name):
    pair_block = whole((2, BLOCK, HEAD_SIZE))
    return pl.pallas_call(
        functools.partial(attend_body, mine),
        grid_spec=pltpu.PrefetchScalarGridSpec(
            num_scalar_prefetch=1,
            grid=(1,),
            in_specs=[pair_block] * 5
            + [whole((PAIR, 1)), whole((PAIR // TILE, SPAN))],
            out_specs=whole((BLOCK, 2 * HEAD_SIZE)),
            scratch_shapes=[pltpu.VMEM((2 * PAIR, HEAD_SIZE), jnp.bfloat16)] * 2,
        ),
        out_shape=jax.ShapeDtypeStruct((BLOCK, 2 * HEAD_SIZE), jnp.bfloat16),
        compiler_params=pltpu.CompilerParams(vmem_limit_bytes=32 * MIB),
        cost_estimate=pl.CostEstimate(
            flops=4 * BLOCK * SPAN * 256, bytes_accessed=3 * MIB, transcendentals=2 * BLOCK * SPAN
        ),
        name=name,
    )(place, queries, *blocks, query_offsets, key_offsets)


def out_body(place_ref, *refs):
    pieces, (own_ref, other_ref, *outs) = refs[:8], refs[8:]
    rows_ref, weight_ref, sems = outs[X:]
    x = place_ref[0]
    quarter = BLOCK // X
    count = own_ref.shape[0] // X
    copies = []
    for k in range(X):
        at = pl.multiple_of(lax.rem(x + k, X) * count, 16)
        for side, ref in enumerate((own_ref, other_ref)):
            slot = 2 * k + side
            copies.append(
                pltpu.make_async_copy(
                    ref.at[pl.ds(at, count)], weight_ref.at[slot], sems.at[slot]
                )
            )
    for copy in copies:
        copy.start()
    for k, piece in enumerate(pieces):
        for rel in range(X):
            at = pl.multiple_of(lax.rem(x + rel, X) * quarter, quarter)
            rows_ref[rel * quarter : (rel + 1) * quarter, k * 256 : (k + 1) * 256] = piece[
                pl.ds(at, quarter), :
            ]
    for copy in copies:
        copy.wait()
    weights = jnp.concatenate([weight_ref[k] for k in range(2 * X)], axis=1)
    total = lax.dot_general(
        rows_ref[...], weights, (((1,), (1,)), ((), ())), preferred_element_type=jnp.float32
    )
    for rel, out_ref in enumerate(outs[:X]):
        out_ref[...] = total[rel * quarter : (rel + 1) * quarter].astype(jnp.bfloat16)


def out_project(place, pieces, own, other):
    count = own.shape[0] // X
    chunk = jax.ShapeDtypeStruct((BLOCK // X, count), jnp.bfloat16)
    return pl.pallas_call(
        out_body,
        in_specs=[SMEM] + [HELD] * 8 + [HBM] * 2,
        out_specs=[HELD] * X,
        out_shape=[chunk] * X,
        scratch_shapes=[
            pltpu.VMEM((BLOCK, 2048), jnp.bfloat16),
            pltpu.VMEM((2 * X, count, 256), jnp.bfloat16),
            pltpu.SemaphoreType.DMA((2 * X,)),
        ],
        compiler_params=pltpu.CompilerParams(vmem_limit_bytes=60 * MIB),
        cost_estimate=pl.CostEstimate(
            flops=2 * BLOCK * count * 2048, bytes_accessed=9 * MIB, transcendentals=0
        ),
        name="out_project",
    )(place, *pieces, own, other)


def final_body(place_ref, *refs):
    pieces, (rows_ref, gain_ref, out_ref, stage_ref) = refs[:X], refs[X:]
    x = place_ref[0]
    for k, piece in enumerate(pieces):
        stage_ref[lax.rem(x + k, X)] = piece[...]
    step = 32
    for at in range(0, rows_ref.shape[0], step):
        summed = jnp.concatenate(
            [stage_ref[k, at : at + step].astype(jnp.float32) for k in range(X)], axis=1
        )
        scale = lax.rsqrt(jnp.mean(summed * summed, axis=-1, keepdims=True) + EPSILON)
        out = rows_ref[at : at + step].astype(jnp.float32) + summed * scale * gain_ref[...]
        out_ref[at : at + step] = out.astype(jnp.bfloat16)


def final_norm(place, pieces, rows, gain):
    width = rows.shape[1]
    return pl.pallas_call(
        final_body,
        in_specs=[SMEM] + [HELD] * (X + 2),
        out_specs=HELD,
        out_shape=jax.ShapeDtypeStruct(rows.shape, jnp.bfloat16),
        scratch_shapes=[pltpu.VMEM((X, rows.shape[0], width // X), jnp.bfloat16)],
        compiler_params=pltpu.CompilerParams(vmem_limit_bytes=32 * MIB),
        name="final_norm",
    )(place, *pieces, rows, gain.reshape(1, width))


def core_order(first, second, c):
    low = jnp.where(c == 0, first, second)
    high = jnp.where(c == 0, second, first)
    return low, high


def shards(
    tokens,
    positions,
    w_query,
    key_matrix,
    value_matrix,
    w_out,
    gain_in,
    gain_query,
    gain_key,
    gain_post,
):
    ctx = lax.axis_index("ctx")
    c, y, z, pair = ctx % C, ctx // C % Y, ctx // (Y * C), ctx // C
    x = lax.axis_index("tp")
    place = jnp.stack([x, y, z, c]).astype(jnp.int32)
    width = tokens.shape[1]

    out_rows = w_out.T
    sides = [
        jnp.concatenate(
            [
                w_query[:, side * 256 : side * 256 + 256],
                key_matrix[:, side * 128 : side * 128 + 128],
                value_matrix[:, side * 128 : side * 128 + 128],
                out_rows[:, side * 256 : side * 256 + 256],
            ],
            axis=1,
        )
        for side in range(2)
    ]
    mine, theirs = core_order(sides[0], sides[1], c)
    received = swap_cores(theirs)
    stacked = jnp.concatenate(core_order(mine, received, c), axis=0)
    part, part_out = stacked[:, :512], trade_x_z(stacked[:, 512:])
    part = lax.all_gather(part, "ctx", axis=0, tiled=True, axis_index_groups=ROWS)
    part, moving = together(part, tokens)
    weights = lax.all_gather(part, "ctx", axis=0, tiled=True, axis_index_groups=COLUMNS)

    start = pair * PAIR
    query_offsets = lax.dynamic_slice_in_dim(positions, start, PAIR, 0) - positions[0]
    before = lax.dynamic_slice_in_dim(positions, jnp.maximum(start - PAIR, 0), PAIR, 0)
    before = jnp.where(pair == 0, -(2**30), before - positions[0])
    key_offsets = jnp.concatenate([before, query_offsets])
    key_offsets = jnp.stack([key_offsets[at : at + SPAN] for at in range(0, PAIR, TILE)])
    half_dim = HEAD_SIZE // 2
    frequency = ROPE_BASE ** (-(jnp.arange(half_dim, dtype=jnp.float32) * 2.0) / HEAD_SIZE)
    angles = query_offsets.astype(jnp.float32)[:, None] * frequency[None, :]
    cosine, sine = jnp.cos(angles), jnp.sin(angles)
    cosine = jnp.concatenate([cosine, cosine], axis=1)
    sine = jnp.concatenate([-sine, sine], axis=1)
    query_offsets = query_offsets[:, None]

    rows = input_norm(moving, gain_in)
    from_low, from_high = shift_x(rows, 1), shift_x(rows, -1)
    part_out = lax.all_gather(part_out, "ctx", axis=0, tiled=True, axis_index_groups=ROWS)
    from_low, from_high, part_out, cosine, sine, query_offsets, key_offsets = together(
        from_low, from_high, part_out, cosine, sine, query_offsets, key_offsets
    )
    half = rows.shape[0] // 2
    far_low = shift_x(from_low[:half], 1)
    far_high = shift_x(from_high[half:], -1)
    own_rows = place_rows(place, [rows, from_high, far_low, far_high, from_low])
    other_rows = swap_cores(own_rows)

    tables = [gain_query.reshape(1, HEAD_SIZE), gain_key.reshape(1, HEAD_SIZE), cosine, sine]

    weights, part_out = together(weights, part_out)
    own_out = lax.all_gather(part_out, "ctx", axis=0, tiled=True, axis_index_groups=COLUMNS)
    q_own, kv_own = project(True, place, own_rows, weights, tables, "project_own")
    prev_own = next_pair(kv_own)
    q_other, kv_other = project(False, place, other_rows, weights, tables, "project_other")
    prev_other = next_pair(kv_other)
    blocks = [kv_own, kv_other, prev_own, prev_other]
    keep = attend(True, place, q_own, blocks, query_offsets, key_offsets, "attend_keep")
    q_other, keep = together(q_other, keep)
    give = attend(False, place, q_other, blocks, query_offsets, key_offsets, "attend_give")
    far_keep = [shift_x(keep, -1), shift_x(keep, 2), shift_x(keep, 1)]
    other = swap_cores(give)
    far_other = [shift_x(other, -1), shift_x(other, 2), shift_x(other, 1)]
    own_out, *far_keep = together(own_out, *far_keep)
    other_out = swap_cores(own_out)
    attended = [keep, other]
    for k in range(3):
        attended += [far_keep[k], far_other[k]]
    sums = out_project(place, attended, own_out, other_out)
    sums = [sums[0], shift_x(sums[3], -1), shift_x(sums[2], 2), shift_x(sums[1], 1)]
    return final_norm(place, sums, tokens, gain_post)


def solution(mesh):
    in_specs = (
        P(("ctx", "tp"), None),
        P(),
        P("ctx", "tp"),
        P("ctx", "tp"),
        P("ctx", "tp"),
        P("tp", "ctx"),
        P(),
        P(),
        P(),
        P(),
    )
    out_specs = P(("ctx", "tp"), None)
    return jax.shard_map(shards, mesh=mesh, in_specs=in_specs, out_specs=out_specs, check_vma=False)
```

time: 247 us -> 219 us (0.89)
  waiting for transfers between devices: 146 us -> 94.3 us
  blocking collectives: 0 us -> 22.4 us
  local copies, waits for them, and re-layouts: 18.7 us -> 7.43 us
  starting transfers between devices: 14.7 us -> 24.4 us
    reduce_scatter x1 -> x0, waiting for transfers between devices: 58.6 us -> none  [shards(): summed = lax.psum_scatter(projected, 'tp', scatter_dimension=0, tiled=True)]
    all_gather x1 -> x2, waiting for transfers between devices: 54.4 us -> 13.2 us  [the longest x1 13.2 us: shards(): lax.all_gather(part, 'ctx', axis=0, tiled=True, axis_index_groups=COLUMNS)]
    ppermute x4 -> x13, waiting for transfers between devices: 28 us -> 66.6 us  [shift_x(): return lax.ppermute(value, 'tp', [(x, (x + steps) % X) for x in range(X)])]
    all_gather x0 -> x2, blocking collectives: none -> 22.4 us  [the longest x1 11.4 us: shards(): lax.all_gather(part, 'ctx', axis=0, tiled=True, axis_index_groups=ROWS)]
    ppermute x1 -> x2, waiting for transfers between devices: 0.01 us -> 12 us  [next_pair(): return lax.ppermute(value, 'ctx', pairs)]
    ppermute x4 -> x13, starting transfers between devices: 5.43 us -> 10.7 us  [shift_x(): return lax.ppermute(value, 'tp', [(x, (x + steps) % X) for x in range(X)])]
    unnamed x38 -> x42, local copies, waits for them, and re-layouts: 7.13 us -> 2.68 us
    slice x2 -> x1, local copies, waits for them, and re-layouts: 4.78 us -> 1.26 us  [shards(): positions[0]]
  transfers between devices with their start and end apart: 15 -> 22, of which waited for: 7 -> 17; matrix products, arithmetic and copies ran while one was open for 5% -> 4% of each run, Pallas kernels for 14% -> 17%
where the time goes in v2:
time: 219 us; the launch traced here: 215 us
  waiting for transfers between devices  94.3 us (43%)
  Pallas kernels  47.6 us (22%)
  starting transfers between devices  24.4 us (11%)
  blocking collectives  22.4 us (10%)
  between operations  13.7 us (6%)
  local copies, waits for them, and re-layouts  7.43 us (3%)
  other arithmetic  5.58 us (3%)
    ppermute x13, waiting for transfers between devices, shift_x(): return lax.ppermute(value, 'tp', [(x, (x + steps) % X) for x in range(X)])  66.6 us
    pallas_call x2, Pallas kernels, project(): pl.pallas_call(functools.partial(project_body, mine), in_specs=[SMEM, HBM...  16.6 us
    all_gather x1, waiting for transfers between devices, shards(): lax.all_gather(part, 'ctx', axis=0, tiled=True, axis_index_groups=COLUMNS)  13.2 us
    ppermute x2, waiting for transfers between devices, next_pair(): return lax.ppermute(value, 'ctx', pairs)  12 us
    all_gather x1, blocking collectives, shards(): lax.all_gather(part, 'ctx', axis=0, tiled=True, axis_index_groups=ROWS)  11.4 us
    all_gather x1, blocking collectives, shards(): lax.all_gather(part_out, 'ctx', axis=0, tiled=True, axis_index_groups=ROWS)  11 us
    ppermute x13, starting transfers between devices, shift_x(): return lax.ppermute(value, 'tp', [(x, (x + steps) % X) for x in range(X)])  10.7 us
    ppermute x4, starting transfers between devices, swap_cores(): return lax.ppermute(value, 'ctx', ctx_pairs(lambda z, y, c: (z, y, 1 - c)))  8.73 us
  transfers between devices with their start and end apart: 22, of which 17 were waited for; matrix products, arithmetic and copies ran while one was open for 4% of the time, Pallas kernels for 17%

profile of v2, /device:TPU:25, one launch (start us, length us, event | category | flops | bytes accessed | tf_op | source)
XLA Modules:
  0.0 215.5 jit_solution(5544325496575852005)
XLA Ops:
  6.5 0.9 fusion.6
  7.4 0.8 fusion.8
  8.3 0.8 collective-permute-start
  9.0 1.0 collective-permute-done
  10.1 11.4 %all_gather.12 = bf16[672,512]{1,0:T(8,128)(2,1)} all-gather(bf16[168,512]{1,0:T(8,128)(2,1)S(1)} %fusion), channel_id=1, replica_groups={{0,8,16,24},{4,12,20,28},{32,40,48,56},{36,44,52,60},{64,72,80,88},{68,..., dimensions={0}, use_global_device_ids=true | all-gather | bytes 860160 | tf_op jit(solution)/shard_map/all_gather | solution.py:382
  22.2 3.9 %input_norm.1.refs_0_ = bf16[128,5376]{1,0:T(8,128)(2,1)} custom-call(bf16[128,5376]{1,0:T(8,128)(2,1)} %refs_4_.1, f32[1,5376]{1,0:T(1,128)} %reshape.20.gain_ref), custom_call_target="tpu_custom_call" | custom-call | tf_op jit(solution)/shard_map/input_norm/pallas_call | solution.py:79
  26.1 1.2 collective-permute-start.1
  27.3 1.5 collective-permute-start.2
  28.7 1.3 slice.62
  30.0 1.5 fusion.5
  31.6 1.9 fusion.1
  33.6 0.7 collective-permute-start.3
  34.2 1.4 pad_maximum_fusion
  35.6 11.0 %all_gather.13 = bf16[672,256]{1,0:T(8,128)(2,1)} all-gather(bf16[168,256]{1,0:T(8,128)(2,1)S(1)} %collective-permute-done.3), channel_id=1, replica_groups={{0,8,16,24},{4,12,20,28},{32,40,48,56},{36,44,52,60},{64,72,80,88},{68,..., dimensions={0}, use_global_device_ids=true | all-gather | bytes 430080 | tf_op jit(solution)/shard_map/all_gather | solution.py:402
  46.6 10.4 %collective-permute-done.1.refs_4_ = bf16[128,5376]{1,0:T(8,128)(2,1)S(1)} collective-permute-done((bf16[128,5376]{1,0:T(8,128)(2,1)}, bf16[128,5376]{1,0:T(8,128)(2,1)S(1)}, u32[]{:S(2)}, u32[]{:S(2)}) %collective-permute-start.1) | collective-permute-done | bytes 1376288 | tf_op jit(solution)/shard_map/ppermute | solution.py:37
  57.1 2.3 %collective-permute-start.4 = (bf16[64,5376]{1,0:T(8,128)(2,1)S(1)}, bf16[64,5376]{1,0:T(8,128)(2,1)}, u32[]{:S(2)}, u32[]{:S(2)}) collective-permute-start(bf16[64,5376]{1,0:T(8,128)(2,1)S(1)} %slice.67), channel_id=1, source_target_pairs={{0,1},{1,2},{2,3},{3,0},{4,5},{5,6},{6,7},{7,4},{8,9},{9,10},{10,1... | collective-permute-start | bytes 2064392 | tf_op jit(solution)/shard_map/ppermute | solution.py:37
  59.4 0.9 slice.68
  60.3 1.2 collective-permute-start.5
  62.1 8.9 %collective-permute-done.4.refs_2_ = bf16[64,5376]{1,0:T(8,128)(2,1)} collective-permute-done((bf16[64,5376]{1,0:T(8,128)(2,1)S(1)}, bf16[64,5376]{1,0:T(8,128)(2,1)}, u32[]{:S(2)}, u32[]{:S(2)}) %collective-permute-start.4) | collective-permute-done | bytes 688160 | tf_op jit(solution)/shard_map/ppermute | solution.py:37
  71.1 8.3 %place_rows.1.rows_hbm = bf16[512,5376]{1,0:T(8,128)(2,1)} custom-call(s32[4]{0:T(128)} %pad_add_fusion.2.place_ref, bf16[128,5376]{1,0:T(8,128)(2,1)} %input_norm.1.refs_0_, bf16[128,5376]{1,0:T(8,128)(2,1)} %copy-done.11, bf16[64,5376]{1,0:T(8,128)(2,1)} %collective-permute-done.4.refs_2_, bf16[64,5376]{1,0:T(8,128)(2,1)} %collective-permute-done.5.refs_3_, ...), custom_call_target="tpu_custom_call" | custom-call | bytes 11534336 | tf_op jit(solution)/shard_map/place_rows/pallas_call | solution.py:185
  79.4 7.4 %collective-permute-start.6 = (bf16[512,5376]{1,0:T(8,128)(2,1)}, bf16[512,5376]{1,0:T(8,128)(2,1)}, u32[]{:S(2)}, u32[]{:S(2)}) collective-permute-start(bf16[512,5376]{1,0:T(8,128)(2,1)} %place_rows.1.rows_hbm), channel_id=1, source_target_pairs={{0,4},{4,0},{8,12},{12,8},{16,20},{20,16},{24,28},{28,24},{32,36},... | collective-permute-start | bytes 16515080 | tf_op jit(solution)/shard_map/ppermute | solution.py:33
  86.8 13.2 %all-gather.3.cloned.1.call-done.weight_hbm = bf16[5376,512]{1,0:T(8,128)(2,1)} async-done(((bf16[672,512]{1,0:T(8,128)(2,1)}), bf16[5376,512]{1,0:T(8,128)(2,1)}) %all-gather.3.cloned.1.call-update) | async-done | bytes 5505040 | tf_op jit(solution)/shard_map/all_gather | solution.py:384
  100.0 8.3 %project_own.1 = (bf16[2,512,128]{2,1,0:T(8,128)(2,1)}, bf16[2,512,128]{2,1,0:T(8,128)(2,1)}) custom-call(s32[4]{0:T(128)} %pad_add_fusion.2.place_ref, bf16[512,5376]{1,0:T(8,128)(2,1)} %place_rows.1.rows_hbm, bf16[5376,512]{1,0:T(8,128)(2,1)} %all-gather.3.cloned.1.call-done.weight_hbm, f32[1,128]{1,0:T(1,128)} %bitcast.11, f32[1,128]{1,0:T(1,128)} %bitcast.13, ...), custom_call_target="tpu_custom_call" | custom-call | flops 2818572288 | bytes 12582912 | tf_op jit(solution)/shard_map/project_own/pallas_call | solution.py:153
  108.3 2.1 collective-permute-start.7
  110.4 8.3 %project_other.1 = (bf16[2,512,128]{2,1,0:T(8,128)(2,1)}, bf16[2,512,128]{2,1,0:T(8,128)(2,1)}) custom-call(s32[4]{0:T(128)} %pad_add_fusion.2.place_ref, bf16[512,5376]{1,0:T(8,128)(2,1)} %collective-permute-done.6.rows_hbm, bf16[5376,512]{1,0:T(8,128)(2,1)} %all-gather.3.cloned.1.call-done.weight_hbm, f32[1,128]{1,0:T(1,128)} %bitcast.12, ...), custom_call_target="tpu_custom_call" | custom-call | flops 2818572288 | bytes 12582912 | tf_op jit(solution)/shard_map/project_other/pallas_call | solution.py:153
  118.8 2.2 %collective-permute-start.8 = (bf16[2,512,128]{2,1,0:T(8,128)(2,1)}, bf16[2,512,128]{2,1,0:T(8,128)(2,1)S(1)}, u32[]{:S(2)}, u32[]{:S(2)}) collective-permute-start(bf16[2,512,128]{2,1,0:T(8,128)(2,1)} %get-tuple-element.41.second_ref), channel_id=1, source_target_pairs={{0,8},{4,12},{8,16},{12,20},{16,24},{20,28},{24,32},{28,36},{32,40... | collective-permute-start | bytes 786440 | tf_op jit(solution)/shard_map/ppermute | solution.py:42
  121.2 0.8 collective-permute-done.7.pfirst_ref
  122.0 11.2 %collective-permute-done.8.psecond_ref = bf16[2,512,128]{2,1,0:T(8,128)(2,1)S(1)} collective-permute-done((bf16[2,512,128]{2,1,0:T(8,128)(2,1)}, bf16[2,512,128]{2,1,0:T(8,128)(2,1)S(1)}, u32[]{:S(2)}, u32[]{:S(2)}) %collective-permute-start.8) | collective-permute-done | bytes 262176 | tf_op jit(solution)/shard_map/ppermute | solution.py:42
  133.2 0.9 copy-done.7
  134.2 3.7 %attend_keep.1.refs_0_ = bf16[512,256]{1,0:T(8,128)(2,1)S(1)} custom-call(s32[4]{0:T(128)S(1)} %copy-done.2, bf16[2,512,128]{2,1,0:T(8,128)(2,1)S(1)} %copy-done.9, bf16[2,512,128]{2,1,0:T(8,128)(2,1)S(1)} %copy-done.5, bf16[2,512,128]{2,1,0:T(8,128)(2,1)S(1)} %copy-done.7, bf16[2,512,128]{2,1,0:T(8,128)(2,1)S(1)} %collective-permute-done.7.pfirst_ref, ...), custom_call_target="tpu_custom_call" | custom-call | flops 671088640 | bytes 3145728 | tf_op jit(solution)/shard_map/attend_keep/pallas_call | solution.py:239
  138.1 1.4 collective-permute-start.12
  139.4 5.6 %collective-permute-done.10.refs_2_ = bf16[512,256]{1,0:T(8,128)(2,1)S(1)} collective-permute-done((bf16[512,256]{1,0:T(8,128)(2,1)S(1)}, bf16[512,256]{1,0:T(8,128)(2,1)S(1)}, u32[]{:S(2)}, u32[]{:S(2)}) %collective-permute-start.10) | collective-permute-done | bytes 262176 | tf_op jit(solution)/shard_map/ppermute | solution.py:37
  145.0 1.5 collective-permute-done.11.refs_4_
  146.6 6.8 %collective-permute-done.12.refs_6_ = bf16[512,256]{1,0:T(8,128)(2,1)S(1)} collective-permute-done((bf16[512,256]{1,0:T(8,128)(2,1)S(1)}, bf16[512,256]{1,0:T(8,128)(2,1)S(1)}, u32[]{:S(2)}, u32[]{:S(2)}) %collective-permute-start.12) | collective-permute-done | bytes 262176 | tf_op jit(solution)/shard_map/ppermute | solution.py:37
  153.9 3.7 %attend_give.1 = bf16[512,256]{1,0:T(8,128)(2,1)S(1)} custom-call(s32[4]{0:T(128)S(1)} %copy-done.2, bf16[2,512,128]{2,1,0:T(8,128)(2,1)S(1)} %copy-done.6, bf16[2,512,128]{2,1,0:T(8,128)(2,1)S(1)} %copy-done.5, bf16[2,512,128]{2,1,0:T(8,128)(2,1)S(1)} %copy-done.8, bf16[2,512,128]{2,1,0:T(8,128)(2,1)S(1)} %collective-permute-done.7.pfirst_ref, ...), custom_call_target="tpu_custom_call" | custom-call | flops 671088640 | bytes 3145728 | tf_op jit(solution)/shard_map/attend_give/pallas_call | solution.py:239
  157.8 1.5 collective-permute-done.9.refs_1_
  159.3 0.9 collective-permute-start.13
  160.8 6.3 %collective-permute-done.13.refs_3_ = bf16[512,256]{1,0:T(8,128)(2,1)S(1)} collective-permute-done((bf16[512,256]{1,0:T(8,128)(2,1)S(1)}, bf16[512,256]{1,0:T(8,128)(2,1)S(1)}, u32[]{:S(2)}, u32[]{:S(2)}) %collective-permute-start.13) | collective-permute-done | bytes 262176 | tf_op jit(solution)/shard_map/ppermute | solution.py:37
  167.0 2.1 collective-permute-done.14.refs_5_
  169.2 6.3 %collective-permute-done.15.refs_7_ = bf16[512,256]{1,0:T(8,128)(2,1)S(1)} collective-permute-done((bf16[512,256]{1,0:T(8,128)(2,1)S(1)}, bf16[512,256]{1,0:T(8,128)(2,1)S(1)}, u32[]{:S(2)}, u32[]{:S(2)}) %collective-permute-start.15) | collective-permute-done | bytes 262176 | tf_op jit(solution)/shard_map/ppermute | solution.py:37
  175.6 0.7 copy-done.20
  176.2 8.6 %out_project.1 = (bf16[128,1344]{1,0:T(8,128)(2,1)}, bf16[128,1344]{1,0:T(8,128)(2,1)}, bf16[128,1344]{1,0:T(8,128)(2,1)}, bf16[128,1344]{1,0:T(8,128)(2,1)}) custom-call(s32[4]{0:T(128)} %pad_add_fusion.2.place_ref, bf16[512,256]{1,0:T(8,128)(2,1)} %copy-done.4, bf16[512,256]{1,0:T(8,128)(2,1)} %copy-done.17, bf16[512,256]{1,0:T(8,128)(2,1)} %copy-done.14, ...), custom_call_target="tpu_custom_call" | custom-call | flops 2818572288 | bytes 9437184 | tf_op jit(solution)/shard_map/out_project/pallas_call | solution.py:295
  185.0 1.3 collective-permute-start.19
  186.4 8.2 %collective-permute-done.17.refs_1_ = bf16[128,1344]{1,0:T(8,128)(2,1)S(1)} collective-permute-done((bf16[128,1344]{1,0:T(8,128)(2,1)}, bf16[128,1344]{1,0:T(8,128)(2,1)S(1)}, u32[]{:S(2)}, u32[]{:S(2)}) %collective-permute-start.17) | collective-permute-done | bytes 344096 | tf_op jit(solution)/shard_map/ppermute | solution.py:37
  194.6 1.1 collective-permute-done.18.refs_2_
  195.6 9.1 %collective-permute-done.19.refs_3_ = bf16[128,1344]{1,0:T(8,128)(2,1)S(1)} collective-permute-done((bf16[128,1344]{1,0:T(8,128)(2,1)}, bf16[128,1344]{1,0:T(8,128)(2,1)S(1)}, u32[]{:S(2)}, u32[]{:S(2)}) %collective-permute-start.19) | collective-permute-done | bytes 344096 | tf_op jit(solution)/shard_map/ppermute | solution.py:37
  204.8 1.0 copy-done.1
  205.8 2.9 %final_norm.1 = bf16[128,5376]{1,0:T(8,128)(2,1)} custom-call(s32[4]{0:T(128)S(1)} %copy-done.3, bf16[128,1344]{1,0:T(8,128)(2,1)S(1)} %copy-done.1, bf16[128,1344]{1,0:T(8,128)(2,1)S(1)} %collective-permute-done.17.refs_1_, bf16[128,1344]{1,0:T(8,128)(2,1)S(1)} %collective-permute-done.18.refs_2_, bf16[128,1344]{1,0:T(8,128)(2,1)S(1)} %collective-permute-done.19.refs_3_, ...), custom_call_target="tpu_custom_call" | custom-call | tf_op jit(solution)/shard_map/final_norm/pallas_call | solution.py:330
  (73 shorter events, 3.6 us)
Async XLA Ops:
  6.5 15.1 %copy-start.12 = (f32[5376]{0:T(1024)S(1)}, f32[5376]{0:T(1024)}, u32[]{:S(2)}) copy-start(f32[5376]{0:T(1024)} %param.16) | copy-start | bytes 64516
  6.5 93.4 %all-gather.3.cloned.1.call-start = ((), (), s32[]{:S(2)}) async-start(), calls=%async_computation | async-start | bytes 6193152 | tf_op jit(solution)/shard_map/all_gather | solution.py:384
  8.3 1.8 collective-permute-start
  21.5 131.9 %all-gather.5.cloned.1.call-start = ((), (), s32[]{:S(2)}) async-start(), calls=%async_computation.1 | async-start | bytes 3096576 | tf_op jit(solution)/shard_map/all_gather | solution.py:415
  26.1 31.0 %collective-permute-start.1 = (bf16[128,5376]{1,0:T(8,128)(2,1)}, bf16[128,5376]{1,0:T(8,128)(2,1)S(1)}, u32[]{:S(2)}, u32[]{:S(2)}) collective-permute-start(bf16[128,5376]{1,0:T(8,128)(2,1)} %input_norm.1.refs_0_), channel_id=1, source_target_pairs={{0,1},{1,2},{2,3},{3,0},{4,5},{5,6},{6,7},{7,4},{8,9},{9,10},{10,1... | collective-permute-start | bytes 4128776 | tf_op jit(solution)/shard_map/ppermute | solution.py:37
  27.3 29.8 %collective-permute-start.2 = (bf16[128,5376]{1,0:T(8,128)(2,1)}, bf16[128,5376]{1,0:T(8,128)(2,1)S(1)}, u32[]{:S(2)}, u32[]{:S(2)}) collective-permute-start(bf16[128,5376]{1,0:T(8,128)(2,1)} %input_norm.1.refs_0_), channel_id=1, source_target_pairs={{0,3},{1,0},{2,1},{3,2},{4,7},{5,4},{6,5},{7,6},{8,11},{9,8},{10,9... | collective-permute-start | bytes 4128776 | tf_op jit(solution)/shard_map/ppermute | solution.py:37
  33.6 2.0 collective-permute-start.3
  57.1 14.1 %copy-start.10 = (bf16[128,5376]{1,0:T(8,128)(2,1)}, bf16[128,5376]{1,0:T(8,128)(2,1)S(1)}, u32[]{:S(2)}) copy-start(bf16[128,5376]{1,0:T(8,128)(2,1)S(1)} %collective-permute-done.1.refs_4_) | copy-start | bytes 4128772
  57.1 14.1 %copy-start.11 = (bf16[128,5376]{1,0:T(8,128)(2,1)}, bf16[128,5376]{1,0:T(8,128)(2,1)S(1)}, u32[]{:S(2)}) copy-start(bf16[128,5376]{1,0:T(8,128)(2,1)S(1)} %collective-permute-done.2.refs_1_) | copy-start | bytes 4128772
  57.1 13.8 %collective-permute-start.4 = (bf16[64,5376]{1,0:T(8,128)(2,1)S(1)}, bf16[64,5376]{1,0:T(8,128)(2,1)}, u32[]{:S(2)}, u32[]{:S(2)}) collective-permute-start(bf16[64,5376]{1,0:T(8,128)(2,1)S(1)} %slice.67), channel_id=1, source_target_pairs={{0,1},{1,2},{2,3},{3,0},{4,5},{5,6},{6,7},{7,4},{8,9},{9,10},{10,1... | collective-permute-start | bytes 2064392 | tf_op jit(solution)/shard_map/ppermute | solution.py:37
  60.3 10.8 %collective-permute-start.5 = (bf16[64,5376]{1,0:T(8,128)(2,1)}, bf16[64,5376]{1,0:T(8,128)(2,1)}, u32[]{:S(2)}, u32[]{:S(2)}) collective-permute-start(bf16[64,5376]{1,0:T(8,128)(2,1)} %slice.68), channel_id=1, source_target_pairs={{0,3},{1,0},{2,1},{3,2},{4,7},{5,4},{6,5},{7,6},{8,11},{9,8},{10,9... | collective-permute-start | bytes 2064392 | tf_op jit(solution)/shard_map/ppermute | solution.py:37
  79.4 31.0 %collective-permute-start.6 = (bf16[512,5376]{1,0:T(8,128)(2,1)}, bf16[512,5376]{1,0:T(8,128)(2,1)}, u32[]{:S(2)}, u32[]{:S(2)}) collective-permute-start(bf16[512,5376]{1,0:T(8,128)(2,1)} %place_rows.1.rows_hbm), channel_id=1, source_target_pairs={{0,4},{4,0},{8,12},{12,8},{16,20},{20,16},{24,28},{28,24},{32,36},... | collective-permute-start | bytes 16515080 | tf_op jit(solution)/shard_map/ppermute | solution.py:33
  108.3 24.9 %copy-start.2 = (s32[4]{0:T(128)S(1)}, s32[4]{0:T(128)}, u32[]{:S(2)}) copy-start(s32[4]{0:T(128)} %pad_add_fusion.2.place_ref) | copy-start | bytes 52
  108.3 24.9 %copy-start.5 = (bf16[2,512,128]{2,1,0:T(8,128)(2,1)S(1)}, bf16[2,512,128]{2,1,0:T(8,128)(2,1)}, u32[]{:S(2)}) copy-start(bf16[2,512,128]{2,1,0:T(8,128)(2,1)} %get-tuple-element.40.first_ref) | copy-start | bytes 786436
  108.3 24.9 %copy-start.9 = (bf16[2,512,128]{2,1,0:T(8,128)(2,1)S(1)}, bf16[2,512,128]{2,1,0:T(8,128)(2,1)}, u32[]{:S(2)}) copy-start(bf16[2,512,128]{2,1,0:T(8,128)(2,1)} %get-tuple-element.39.q_ref) | copy-start | bytes 786436
  108.3 13.6 %collective-permute-start.7 = (bf16[2,512,128]{2,1,0:T(8,128)(2,1)}, bf16[2,512,128]{2,1,0:T(8,128)(2,1)S(1)}, u32[]{:S(2)}, u32[]{:S(2)}) collective-permute-start(bf16[2,512,128]{2,1,0:T(8,128)(2,1)} %get-tuple-element.40.first_ref), channel_id=1, source_target_pairs={{0,8},{4,12},{8,16},{12,20},{16,24},{20,28},{24,32},{28,36},{32,40... | collective-permute-start | bytes 786440 | tf_op jit(solution)/shard_map/ppermute | solution.py:42
  118.8 35.2 %copy-start.6 = (bf16[2,512,128]{2,1,0:T(8,128)(2,1)S(1)}, bf16[2,512,128]{2,1,0:T(8,128)(2,1)}, u32[]{:S(2)}) copy-start(bf16[2,512,128]{2,1,0:T(8,128)(2,1)} %get-tuple-element.45.q_ref) | copy-start | bytes 786436
  118.8 35.2 %copy-start.8 = (bf16[2,512,128]{2,1,0:T(8,128)(2,1)S(1)}, bf16[2,512,128]{2,1,0:T(8,128)(2,1)}, u32[]{:S(2)}) copy-start(bf16[2,512,128]{2,1,0:T(8,128)(2,1)} %get-tuple-element.41.second_ref) | copy-start | bytes 786436
  118.8 14.5 %collective-permute-start.8 = (bf16[2,512,128]{2,1,0:T(8,128)(2,1)}, bf16[2,512,128]{2,1,0:T(8,128)(2,1)S(1)}, u32[]{:S(2)}, u32[]{:S(2)}) collective-permute-start(bf16[2,512,128]{2,1,0:T(8,128)(2,1)} %get-tuple-element.41.second_ref), channel_id=1, source_target_pairs={{0,8},{4,12},{8,16},{12,20},{16,24},{20,28},{24,32},{28,36},{32,40... | collective-permute-start | bytes 786440 | tf_op jit(solution)/shard_map/ppermute | solution.py:42
  133.2 1.0 copy-start.7
  137.9 37.6 %copy-start.4 = (bf16[512,256]{1,0:T(8,128)(2,1)}, bf16[512,256]{1,0:T(8,128)(2,1)S(1)}, u32[]{:S(2)}) copy-start(bf16[512,256]{1,0:T(8,128)(2,1)S(1)} %attend_keep.1.refs_0_) | copy-start | bytes 786436
  137.9 7.1 %collective-permute-start.10 = (bf16[512,256]{1,0:T(8,128)(2,1)S(1)}, bf16[512,256]{1,0:T(8,128)(2,1)S(1)}, u32[]{:S(2)}, u32[]{:S(2)}) collective-permute-start(bf16[512,256]{1,0:T(8,128)(2,1)S(1)} %attend_keep.1.refs_0_), channel_id=1, source_target_pairs={{0,3},{1,0},{2,1},{3,2},{4,7},{5,4},{6,5},{7,6},{8,11},{9,8},{10,9... | collective-permute-start | bytes 786440 | tf_op jit(solution)/shard_map/ppermute | solution.py:37
  138.0 8.6 %collective-permute-start.11 = (bf16[512,256]{1,0:T(8,128)(2,1)S(1)}, bf16[512,256]{1,0:T(8,128)(2,1)S(1)}, u32[]{:S(2)}, u32[]{:S(2)}) collective-permute-start(bf16[512,256]{1,0:T(8,128)(2,1)S(1)} %attend_keep.1.refs_0_), channel_id=1, source_target_pairs={{0,2},{1,3},{2,0},{3,1},{4,6},{5,7},{6,4},{7,5},{8,10},{9,11},{10,... | collective-permute-start | bytes 786440 | tf_op jit(solution)/shard_map/ppermute | solution.py:37
  138.1 15.3 %collective-permute-start.12 = (bf16[512,256]{1,0:T(8,128)(2,1)S(1)}, bf16[512,256]{1,0:T(8,128)(2,1)S(1)}, u32[]{:S(2)}, u32[]{:S(2)}) collective-permute-start(bf16[512,256]{1,0:T(8,128)(2,1)S(1)} %attend_keep.1.refs_0_), channel_id=1, source_target_pairs={{0,1},{1,2},{2,3},{3,0},{4,5},{5,6},{6,7},{7,4},{8,9},{9,10},{10,1... | collective-permute-start | bytes 786440 | tf_op jit(solution)/shard_map/ppermute | solution.py:37
  145.0 30.5 %copy-start.14 = (bf16[512,256]{1,0:T(8,128)(2,1)}, bf16[512,256]{1,0:T(8,128)(2,1)S(1)}, u32[]{:S(2)}) copy-start(bf16[512,256]{1,0:T(8,128)(2,1)S(1)} %collective-permute-done.10.refs_2_) | copy-start | bytes 786436
  146.6 28.9 %copy-start.15 = (bf16[512,256]{1,0:T(8,128)(2,1)}, bf16[512,256]{1,0:T(8,128)(2,1)S(1)}, u32[]{:S(2)}) copy-start(bf16[512,256]{1,0:T(8,128)(2,1)S(1)} %collective-permute-done.11.refs_4_) | copy-start | bytes 786436
  153.4 22.1 %copy-start.16 = (bf16[512,256]{1,0:T(8,128)(2,1)}, bf16[512,256]{1,0:T(8,128)(2,1)S(1)}, u32[]{:S(2)}) copy-start(bf16[512,256]{1,0:T(8,128)(2,1)S(1)} %collective-permute-done.12.refs_6_) | copy-start | bytes 786436
  153.4 22.1 %collective-permute-start.16 = (bf16[5376,256]{1,0:T(8,128)(2,1)}, bf16[5376,256]{1,0:T(8,128)(2,1)}, u32[]{:S(2)}, u32[]{:S(2)}) collective-permute-start(bf16[5376,256]{1,0:T(8,128)(2,1)} %all-gather.5.cloned.1.call-done.refs_8_), channel_id=1, source_target_pairs={{0,4},{4,0},{8,12},{12,8},{16,20},{20,16},{24,28},{28,24},{32,36},... | collective-permute-start | bytes 8257544 | tf_op jit(solution)/shard_map/ppermute | solution.py:33
  157.6 28.8 %copy-start.13 = (f32[5376]{0:T(1024)S(1)}, f32[5376]{0:T(1024)}, u32[]{:S(2)}) copy-start(f32[5376]{0:T(1024)} %param.19) | copy-start | bytes 64516
  157.6 47.2 %copy-start = (bf16[128,5376]{1,0:T(8,128)(2,1)S(1)}, bf16[128,5376]{1,0:T(8,128)(2,1)}, u32[]{:S(2)}) copy-start(bf16[128,5376]{1,0:T(8,128)(2,1)} %refs_4_.1) | copy-start | bytes 4128772
  157.6 47.1 %copy-start.3 = (s32[4]{0:T(128)S(1)}, s32[4]{0:T(128)}, u32[]{:S(2)}) copy-start(s32[4]{0:T(128)} %pad_add_fusion.2.place_ref) | copy-start | bytes 52
  157.7 1.6 collective-permute-start.9
  159.3 16.3 %copy-start.17 = (bf16[512,256]{1,0:T(8,128)(2,1)}, bf16[512,256]{1,0:T(8,128)(2,1)S(1)}, u32[]{:S(2)}) copy-start(bf16[512,256]{1,0:T(8,128)(2,1)S(1)} %collective-permute-done.9.refs_1_) | copy-start | bytes 786436
  159.3 7.8 %collective-permute-start.13 = (bf16[512,256]{1,0:T(8,128)(2,1)S(1)}, bf16[512,256]{1,0:T(8,128)(2,1)S(1)}, u32[]{:S(2)}, u32[]{:S(2)}) collective-permute-start(bf16[512,256]{1,0:T(8,128)(2,1)S(1)} %collective-permute-done.9.refs_1_), channel_id=1, source_target_pairs={{0,3},{1,0},{2,1},{3,2},{4,7},{5,4},{6,5},{7,6},{8,11},{9,8},{10,9... | collective-permute-start | bytes 786440 | tf_op jit(solution)/shard_map/ppermute | solution.py:37
  160.2 9.0 %collective-permute-start.14 = (bf16[512,256]{1,0:T(8,128)(2,1)S(1)}, bf16[512,256]{1,0:T(8,128)(2,1)S(1)}, u32[]{:S(2)}, u32[]{:S(2)}) collective-permute-start(bf16[512,256]{1,0:T(8,128)(2,1)S(1)} %collective-permute-done.9.refs_1_), channel_id=1, source_target_pairs={{0,2},{1,3},{2,0},{3,1},{4,6},{5,7},{6,4},{7,5},{8,10},{9,11},{10,... | collective-permute-start | bytes 786440 | tf_op jit(solution)/shard_map/ppermute | solution.py:37
  160.2 15.3 %collective-permute-start.15 = (bf16[512,256]{1,0:T(8,128)(2,1)S(1)}, bf16[512,256]{1,0:T(8,128)(2,1)S(1)}, u32[]{:S(2)}, u32[]{:S(2)}) collective-permute-start(bf16[512,256]{1,0:T(8,128)(2,1)S(1)} %collective-permute-done.9.refs_1_), channel_id=1, source_target_pairs={{0,1},{1,2},{2,3},{3,0},{4,5},{5,6},{6,7},{7,4},{8,9},{9,10},{10,1... | collective-permute-start | bytes 786440 | tf_op jit(solution)/shard_map/ppermute | solution.py:37
  167.0 8.5 %copy-start.18 = (bf16[512,256]{1,0:T(8,128)(2,1)}, bf16[512,256]{1,0:T(8,128)(2,1)S(1)}, u32[]{:S(2)}) copy-start(bf16[512,256]{1,0:T(8,128)(2,1)S(1)} %collective-permute-done.13.refs_3_) | copy-start | bytes 786436
  169.2 6.4 %copy-start.19 = (bf16[512,256]{1,0:T(8,128)(2,1)}, bf16[512,256]{1,0:T(8,128)(2,1)S(1)}, u32[]{:S(2)}) copy-start(bf16[512,256]{1,0:T(8,128)(2,1)S(1)} %collective-permute-done.14.refs_5_) | copy-start | bytes 786436
  175.5 0.7 copy-start.20
  184.8 9.8 %collective-permute-start.17 = (bf16[128,1344]{1,0:T(8,128)(2,1)}, bf16[128,1344]{1,0:T(8,128)(2,1)S(1)}, u32[]{:S(2)}, u32[]{:S(2)}) collective-permute-start(bf16[128,1344]{1,0:T(8,128)(2,1)} %get-tuple-element.52), channel_id=1, source_target_pairs={{0,3},{1,0},{2,1},{3,2},{4,7},{5,4},{6,5},{7,6},{8,11},{9,8},{10,9... | collective-permute-start | bytes 1032200 | tf_op jit(solution)/shard_map/ppermute | solution.py:37
  184.9 10.7 %collective-permute-start.18 = (bf16[128,1344]{1,0:T(8,128)(2,1)}, bf16[128,1344]{1,0:T(8,128)(2,1)S(1)}, u32[]{:S(2)}, u32[]{:S(2)}) collective-permute-start(bf16[128,1344]{1,0:T(8,128)(2,1)} %get-tuple-element.53), channel_id=1, source_target_pairs={{0,2},{1,3},{2,0},{3,1},{4,6},{5,7},{6,4},{7,5},{8,10},{9,11},{10,... | collective-permute-start | bytes 1032200 | tf_op jit(solution)/shard_map/ppermute | solution.py:37
  185.0 19.7 %collective-permute-start.19 = (bf16[128,1344]{1,0:T(8,128)(2,1)}, bf16[128,1344]{1,0:T(8,128)(2,1)S(1)}, u32[]{:S(2)}, u32[]{:S(2)}) collective-permute-start(bf16[128,1344]{1,0:T(8,128)(2,1)} %get-tuple-element.54), channel_id=1, source_target_pairs={{0,1},{1,2},{2,3},{3,0},{4,5},{5,6},{6,7},{7,4},{8,9},{9,10},{10,1... | collective-permute-start | bytes 1032200 | tf_op jit(solution)/shard_map/ppermute | solution.py:37
  204.8 1.0 copy-start.1
Sparse Core Ops, SparseCore 0:
  21.7 78.2 all-gather.2
  101.8 47.6 all-gather.4

commit v3 on v2

--- a/solution.py
+++ b/solution.py
@@ -116,12 +116,15 @@
                 ),
             )
         )
-    for pair in copies:
+    for pair in copies[:2]:
         for copy in pair:
             copy.start()
     for k, pair in enumerate(copies):
         for copy in pair:
             copy.wait()
+        if k + 2 < PARTS:
+            for copy in copies[k + 2]:
+                copy.start()
         span = slice(k * step, (k + 1) * step)
         part = jnp.dot(
             rows_ref[:, span], weight_ref[span, :], preferred_element_type=jnp.float32
@@ -200,88 +203,84 @@
 SPAN = PAIR + TILE
 
 
-def attend_body(mine, place_ref, q_ref, first_ref, second_ref, pfirst_ref, psecond_ref, qoff_ref, koff_ref, out_ref, keys_ref, values_ref):
+def attend_body(
+    place_ref, qmine_ref, qother_ref, mine_ref, other_ref, pmine_ref, pother_ref,
+    qoff_ref, koff_ref, keep_ref, give_ref, keys_ref, values_ref,
+):
     c = place_ref[3]
-    for base, refs in ((0, (pfirst_ref, psecond_ref)), (PAIR, (first_ref, second_ref))):
+    for base, refs in ((0, (pmine_ref, pother_ref)), (PAIR, (mine_ref, other_ref))):
         for block, ref in ((c, refs[0]), (1 - c, refs[1])):
             at = pl.multiple_of(base + block * BLOCK, BLOCK)
             keys_ref[pl.ds(at, BLOCK), :] = ref[0]
             values_ref[pl.ds(at, BLOCK), :] = ref[1]
-    block = c if mine else 1 - c
-    for tile in range(BLOCK // TILE):
-        first, last = tile * TILE, (tile + 1) * TILE
-        at = pl.multiple_of(block * BLOCK + first, TILE)
-        keys = keys_ref[pl.ds(at, SPAN), :]
-        values = values_ref[pl.ds(at, SPAN), :]
-        gap = qoff_ref[pl.ds(at, TILE), :] - koff_ref[pl.ds(block * (BLOCK // TILE) + tile, 1), :]
-        allowed = (gap >= 0) & (gap < LOOKBACK_WINDOW)
-        for h in range(2):
-            scores = lax.dot_general(
-                q_ref[h, first:last],
-                keys,
-                (((1,), (1,)), ((), ())),
-                preferred_element_type=jnp.float32,
-            ) * QS ** (-0.5)
-            scores = jnp.where(allowed, scores, -1e30)
-            row_max = jnp.max(scores, axis=-1, keepdims=True)
-            weights = jnp.exp(scores - row_max)
-            totals = jnp.sum(weights, axis=-1, keepdims=True)
-            mixed = jnp.dot(
-                weights.astype(jnp.bfloat16), values, preferred_element_type=jnp.float32
+    for block, q_ref, out_ref in ((1 - c, qother_ref, give_ref), (c, qmine_ref, keep_ref)):
+        for tile in range(BLOCK // TILE):
+            first, last = tile * TILE, (tile + 1) * TILE
+            at = pl.multiple_of(block * BLOCK + first, TILE)
+            keys = keys_ref[pl.ds(at, SPAN), :]
+            values = values_ref[pl.ds(at, SPAN), :]
+            gap = (
+                qoff_ref[pl.ds(at, TILE), :]
+                - koff_ref[pl.ds(block * (BLOCK // TILE) + tile, 1), :]
             )
-            out_ref[first:last, h * HEAD_SIZE : (h + 1) * HEAD_SIZE] = (mixed / totals).astype(
-                jnp.bfloat16
-            )
-
-
-def attend(mine, place, queries, blocks, query_offsets, key_offsets, name):
-    pair_block = whole((2, BLOCK, HEAD_SIZE))
-    return pl.pallas_call(
-        functools.partial(attend_body, mine),
-        grid_spec=pltpu.PrefetchScalarGridSpec(
-            num_scalar_prefetch=1,
-            grid=(1,),
-            in_specs=[pair_block] * 5
-            + [whole((PAIR, 1)), whole((PAIR // TILE, SPAN))],
-            out_specs=whole((BLOCK, 2 * HEAD_SIZE)),
-            scratch_shapes=[pltpu.VMEM((2 * PAIR, HEAD_SIZE), jnp.bfloat16)] * 2,
-        ),
-        out_shape=jax.ShapeDtypeStruct((BLOCK, 2 * HEAD_SIZE), jnp.bfloat16),
+            allowed = (gap >= 0) & (gap < LOOKBACK_WINDOW)
+            for h in range(2):
+                scores = lax.dot_general(
+                    q_ref[h, first:last],
+                    keys,
+                    (((1,), (1,)), ((), ())),
+                    preferred_element_type=jnp.float32,
+                ) * QS ** (-0.5)
+                scores = jnp.where(allowed, scores, -1e30)
+                row_max = jnp.max(scores, axis=-1, keepdims=True)
+                weights = jnp.exp(scores - row_max)
+                totals = jnp.sum(weights, axis=-1, keepdims=True)
+                mixed = jnp.dot(
+                    weights.astype(jnp.bfloat16), values, preferred_element_type=jnp.float32
+                )
+                out_ref[first:last, h * HEAD_SIZE : (h + 1) * HEAD_SIZE] = (
+                    mixed / totals
+                ).astype(jnp.bfloat16)
+
+
+def attend(place, queries, blocks, query_offsets, key_offsets):
+    out = jax.ShapeDtypeStruct((BLOCK, 2 * HEAD_SIZE), jnp.bfloat16)
+    return pl.pallas_call(
+        attend_body,
+        in_specs=[SMEM] + [HELD] * 8,
+        out_specs=[HELD] * 2,
+        out_shape=[out] * 2,
+        scratch_shapes=[pltpu.VMEM((2 * PAIR, HEAD_SIZE), jnp.bfloat16)] * 2,
         compiler_params=pltpu.CompilerParams(vmem_limit_bytes=32 * MIB),
         cost_estimate=pl.CostEstimate(
-            flops=4 * BLOCK * SPAN * 256, bytes_accessed=3 * MIB, transcendentals=2 * BLOCK * SPAN
+            flops=4 * PAIR * SPAN * 256, bytes_accessed=3 * MIB, transcendentals=2 * PAIR * SPAN
         ),
-        name=name,
-    )(place, queries, *blocks, query_offsets, key_offsets)
+        name="attend",
+    )(place, *queries, *blocks, query_offsets, key_offsets)
 
 
 def out_body(place_ref, *refs):
-    pieces, (own_ref, other_ref, *outs) = refs[:8], refs[8:]
-    rows_ref, weight_ref, sems = outs[X:]
+    pieces, (own_ref, other_ref, *outs) = refs[:X], refs[X:]
+    rows_ref = outs[X]
     x = place_ref[0]
     quarter = BLOCK // X
     count = own_ref.shape[0] // X
-    copies = []
-    for k in range(X):
-        at = pl.multiple_of(lax.rem(x + k, X) * count, 16)
-        for side, ref in enumerate((own_ref, other_ref)):
-            slot = 2 * k + side
-            copies.append(
-                pltpu.make_async_copy(
-                    ref.at[pl.ds(at, count)], weight_ref.at[slot], sems.at[slot]
-                )
-            )
-    for copy in copies:
-        copy.start()
+    weights = jnp.concatenate(
+        [
+            ref[pl.ds(pl.multiple_of(lax.rem(x + k, X) * count, 16), count), :]
+            for k in range(X)
+            for ref in (own_ref, other_ref)
+        ],
+        axis=1,
+    )
     for k, piece in enumerate(pieces):
-        for rel in range(X):
-            at = pl.multiple_of(lax.rem(x + rel, X) * quarter, quarter)
-            rows_ref[rel * quarter : (rel + 1) * quarter, k * 256 : (k + 1) * 256] = piece[
-                pl.ds(at, quarter), :
-            ]
-    for copy in copies:
-        copy.wait()
-    weights = jnp.concatenate([weight_ref[k] for k in range(2 * X)], axis=1)
+        for side in range(2):
+            slot = (2 * k + side) * 256
+            for rel in range(X):
+                at = pl.multiple_of(lax.rem(x + rel, X) * quarter, quarter)
+                rows_ref[rel * quarter : (rel + 1) * quarter, slot : slot + 256] = piece[
+                    side, pl.ds(at, quarter), :
+                ]
     total = lax.dot_general(
         rows_ref[...], weights, (((1,), (1,)), ((), ())), preferred_element_type=jnp.float32
     )
@@ -294,15 +293,13 @@
     chunk = jax.ShapeDtypeStruct((BLOCK // X, count), jnp.bfloat16)
     return pl.pallas_call(
         out_body,
-        in_specs=[SMEM] + [HELD] * 8 + [HBM] * 2,
+        in_specs=[SMEM] + [HELD] * (X + 2),
         out_specs=[HELD] * X,
         out_shape=[chunk] * X,
         scratch_shapes=[
             pltpu.VMEM((BLOCK, 2048), jnp.bfloat16),
-            pltpu.VMEM((2 * X, count, 256), jnp.bfloat16),
-            pltpu.SemaphoreType.DMA((2 * X,)),
         ],
-        compiler_params=pltpu.CompilerParams(vmem_limit_bytes=60 * MIB),
+        compiler_params=pltpu.CompilerParams(vmem_limit_bytes=28 * MIB),
         cost_estimate=pl.CostEstimate(
             flops=2 * BLOCK * count * 2048, bytes_accessed=9 * MIB, transcendentals=0
         ),
@@ -418,17 +415,12 @@
     q_other, kv_other = project(False, place, other_rows, weights, tables, "project_other")
     prev_other = next_pair(kv_other)
     blocks = [kv_own, kv_other, prev_own, prev_other]
-    keep = attend(True, place, q_own, blocks, query_offsets, key_offsets, "attend_keep")
-    q_other, keep = together(q_other, keep)
-    give = attend(False, place, q_other, blocks, query_offsets, key_offsets, "attend_give")
-    far_keep = [shift_x(keep, -1), shift_x(keep, 2), shift_x(keep, 1)]
+    keep, give = attend(place, [q_own, q_other], blocks, query_offsets, key_offsets)
     other = swap_cores(give)
-    far_other = [shift_x(other, -1), shift_x(other, 2), shift_x(other, 1)]
-    own_out, *far_keep = together(own_out, *far_keep)
+    other, own_out = together(other, own_out)
+    both = jnp.stack([keep, other])
+    attended = [both, shift_x(both, -1), shift_x(both, 2), shift_x(both, 1)]
     other_out = swap_cores(own_out)
-    attended = [keep, other]
-    for k in range(3):
-        attended += [far_keep[k], far_other[k]]
     sums = out_project(place, attended, own_out, other_out)
     sums = [sums[0], shift_x(sums[3], -1), shift_x(sums[2], 2), shift_x(sums[1], 1)]
     return final_norm(place, sums, tokens, gain_post)

time: 219 us -> 217 us (level); the launches traced: 215 us -> 216 us
  Pallas kernels: 47.6 us -> 42.6 us
  starting transfers between devices: 24.4 us -> 26.7 us
    all_gather x1, waiting for transfers between devices: 0.01 us -> 5.77 us  [shards(): lax.all_gather(part_out, 'ctx', axis=0, tiled=True, axis_index_groups=COL...]
    pallas_call x3 -> x2, Pallas kernels: 16 us -> 10.5 us  [the longest x1 6.49 us: attend(): pl.pallas_call(attend_body, in_specs=[SMEM] + [HELD] * 8, out_specs=[HELD...]
    ppermute x13 -> x10, waiting for transfers between devices: 66.6 us -> 63.2 us  [shift_x(): return lax.ppermute(value, 'tp', [(x, (x + steps) % X) for x in range(X)])]
    ppermute x13 -> x10, starting transfers between devices: 10.7 us -> 12.3 us  [shift_x(): return lax.ppermute(value, 'tp', [(x, (x + steps) % X) for x in range(X)])]
  transfers between devices with their start and end apart: 22 -> 19, of which waited for: 17 -> 14; matrix products, arithmetic and copies ran while one was open for 4% -> 4% of each run, Pallas kernels for 17% -> 17%
where the time goes in v3:
time: 217 us; the launch traced here: 216 us
  waiting for transfers between devices  96.4 us (44%)
  Pallas kernels  42.6 us (20%)
  starting transfers between devices  26.7 us (12%)
  blocking collectives  22.4 us (10%)
  between operations  13.6 us (6%)
  local copies, waits for them, and re-layouts  8.5 us (4%)
  other arithmetic  5.6 us (3%)
    ppermute x10, waiting for transfers between devices, shift_x(): return lax.ppermute(value, 'tp', [(x, (x + steps) % X) for x in range(X)])  63.2 us
    pallas_call x2, Pallas kernels, project(): pl.pallas_call(functools.partial(project_body, mine), in_specs=[SMEM, HBM...  17.2 us
    all_gather x1, waiting for transfers between devices, shards(): lax.all_gather(part, 'ctx', axis=0, tiled=True, axis_index_groups=COLUMNS)  13.1 us
    ppermute x10, starting transfers between devices, shift_x(): return lax.ppermute(value, 'tp', [(x, (x + steps) % X) for x in range(X)])  12.3 us
    ppermute x2, waiting for transfers between devices, next_pair(): return lax.ppermute(value, 'ctx', pairs)  12.1 us
    all_gather x1, blocking collectives, shards(): lax.all_gather(part, 'ctx', axis=0, tiled=True, axis_index_groups=ROWS)  11.4 us
    all_gather x1, blocking collectives, shards(): lax.all_gather(part_out, 'ctx', axis=0, tiled=True, axis_index_groups=ROWS)  11 us
    ppermute x4, starting transfers between devices, swap_cores(): return lax.ppermute(value, 'ctx', ctx_pairs(lambda z, y, c: (z, y, 1 - c)))  9.56 us
  transfers between devices with their start and end apart: 19, of which 14 were waited for; matrix products, arithmetic and copies ran while one was open for 4% of the time, Pallas kernels for 17%

profile of v3, /device:TPU:25, one launch (start us, length us, event | category | flops | bytes accessed | tf_op | source)
XLA Modules:
  0.0 215.9 jit_solution(13452387726207525532)
XLA Ops:
  6.5 0.9 fusion.6
  7.4 0.8 fusion.8
  8.3 0.8 collective-permute-start
  9.0 1.0 collective-permute-done
  10.1 11.4 %all_gather.12 = bf16[672,512]{1,0:T(8,128)(2,1)} all-gather(bf16[168,512]{1,0:T(8,128)(2,1)S(1)} %fusion), channel_id=1, replica_groups={{0,8,16,24},{4,12,20,28},{32,40,48,56},{36,44,52,60},{64,72,80,88},{68,..., dimensions={0}, use_global_device_ids=true | all-gather | bytes 860160 | tf_op jit(solution)/shard_map/all_gather | solution.py:379
  21.6 0.6 reshape.20.gain_ref
  22.2 3.9 %input_norm.1.refs_0_ = bf16[128,5376]{1,0:T(8,128)(2,1)} custom-call(bf16[128,5376]{1,0:T(8,128)(2,1)} %refs_4_.1, f32[1,5376]{1,0:T(1,128)} %reshape.20.gain_ref), custom_call_target="tpu_custom_call" | custom-call | tf_op jit(solution)/shard_map/input_norm/pallas_call | solution.py:79
  26.1 1.2 collective-permute-start.1
  27.3 1.5 collective-permute-start.2
  28.8 1.3 slice.62
  30.0 1.5 fusion.5
  31.6 1.9 fusion.1
  33.5 0.7 collective-permute-start.3
  34.2 1.3 pad_maximum_fusion
  35.5 11.0 %all_gather.13 = bf16[672,256]{1,0:T(8,128)(2,1)} all-gather(bf16[168,256]{1,0:T(8,128)(2,1)S(1)} %collective-permute-done.3), channel_id=1, replica_groups={{0,8,16,24},{4,12,20,28},{32,40,48,56},{36,44,52,60},{64,72,80,88},{68,..., dimensions={0}, use_global_device_ids=true | all-gather | bytes 430080 | tf_op jit(solution)/shard_map/all_gather | solution.py:399
  46.6 10.5 %collective-permute-done.1.refs_4_ = bf16[128,5376]{1,0:T(8,128)(2,1)S(1)} collective-permute-done((bf16[128,5376]{1,0:T(8,128)(2,1)}, bf16[128,5376]{1,0:T(8,128)(2,1)S(1)}, u32[]{:S(2)}, u32[]{:S(2)}) %collective-permute-start.1) | collective-permute-done | bytes 1376288 | tf_op jit(solution)/shard_map/ppermute | solution.py:37
  57.1 2.3 %collective-permute-start.4 = (bf16[64,5376]{1,0:T(8,128)(2,1)S(1)}, bf16[64,5376]{1,0:T(8,128)(2,1)}, u32[]{:S(2)}, u32[]{:S(2)}) collective-permute-start(bf16[64,5376]{1,0:T(8,128)(2,1)S(1)} %slice.67), channel_id=1, source_target_pairs={{0,1},{1,2},{2,3},{3,0},{4,5},{5,6},{6,7},{7,4},{8,9},{9,10},{10,1... | collective-permute-start | bytes 2064392 | tf_op jit(solution)/shard_map/ppermute | solution.py:37
  59.4 0.9 slice.68
  60.3 1.2 collective-permute-start.5
  61.5 0.7 pad_add_fusion.2.place_ref
  62.2 8.8 %collective-permute-done.4.refs_2_ = bf16[64,5376]{1,0:T(8,128)(2,1)} collective-permute-done((bf16[64,5376]{1,0:T(8,128)(2,1)S(1)}, bf16[64,5376]{1,0:T(8,128)(2,1)}, u32[]{:S(2)}, u32[]{:S(2)}) %collective-permute-start.4) | collective-permute-done | bytes 688160 | tf_op jit(solution)/shard_map/ppermute | solution.py:37
  71.2 8.3 %place_rows.1.rows_hbm = bf16[512,5376]{1,0:T(8,128)(2,1)} custom-call(s32[4]{0:T(128)} %pad_add_fusion.2.place_ref, bf16[128,5376]{1,0:T(8,128)(2,1)} %input_norm.1.refs_0_, bf16[128,5376]{1,0:T(8,128)(2,1)} %copy-done.8, bf16[64,5376]{1,0:T(8,128)(2,1)} %collective-permute-done.4.refs_2_, bf16[64,5376]{1,0:T(8,128)(2,1)} %collective-permute-done.5.refs_3_, ...), custom_call_target="tpu_custom_call" | custom-call | bytes 11534336 | tf_op jit(solution)/shard_map/place_rows/pallas_call | solution.py:188
  79.5 7.3 %collective-permute-start.6 = (bf16[512,5376]{1,0:T(8,128)(2,1)}, bf16[512,5376]{1,0:T(8,128)(2,1)}, u32[]{:S(2)}, u32[]{:S(2)}) collective-permute-start(bf16[512,5376]{1,0:T(8,128)(2,1)} %place_rows.1.rows_hbm), channel_id=1, source_target_pairs={{0,4},{4,0},{8,12},{12,8},{16,20},{20,16},{24,28},{28,24},{32,36},... | collective-permute-start | bytes 16515080 | tf_op jit(solution)/shard_map/ppermute | solution.py:33
  86.8 13.1 %all-gather.3.cloned.1.call-done.weight_hbm = bf16[5376,512]{1,0:T(8,128)(2,1)} async-done(((bf16[672,512]{1,0:T(8,128)(2,1)}), bf16[5376,512]{1,0:T(8,128)(2,1)}) %all-gather.3.cloned.1.call-update) | async-done | bytes 5505040 | tf_op jit(solution)/shard_map/all_gather | solution.py:381
  100.0 8.5 %project_own.1 = (bf16[2,512,128]{2,1,0:T(8,128)(2,1)}, bf16[2,512,128]{2,1,0:T(8,128)(2,1)}) custom-call(s32[4]{0:T(128)} %pad_add_fusion.2.place_ref, bf16[512,5376]{1,0:T(8,128)(2,1)} %place_rows.1.rows_hbm, bf16[5376,512]{1,0:T(8,128)(2,1)} %all-gather.3.cloned.1.call-done.weight_hbm, f32[1,128]{1,0:T(1,128)} %bitcast.15, f32[1,128]{1,0:T(1,128)} %bitcast.17, ...), custom_call_target="tpu_custom_call" | custom-call | flops 2818572288 | bytes 12582912 | tf_op jit(solution)/shard_map/project_own/pallas_call | solution.py:156
  108.6 2.1 collective-permute-start.7
  110.6 8.6 %project_other.1 = (bf16[2,512,128]{2,1,0:T(8,128)(2,1)}, bf16[2,512,128]{2,1,0:T(8,128)(2,1)}) custom-call(s32[4]{0:T(128)} %pad_add_fusion.2.place_ref, bf16[512,5376]{1,0:T(8,128)(2,1)} %collective-permute-done.6.rows_hbm, bf16[5376,512]{1,0:T(8,128)(2,1)} %all-gather.3.cloned.1.call-done.weight_hbm, f32[1,128]{1,0:T(1,128)} %bitcast.16, ...), custom_call_target="tpu_custom_call" | custom-call | flops 2818572288 | bytes 12582912 | tf_op jit(solution)/shard_map/project_other/pallas_call | solution.py:156
  119.3 2.1 collective-permute-start.8
  121.6 0.9 collective-permute-done.7.pmine_ref
  122.5 11.2 %collective-permute-done.8.pother_ref = bf16[2,512,128]{2,1,0:T(8,128)(2,1)S(1)} collective-permute-done((bf16[2,512,128]{2,1,0:T(8,128)(2,1)}, bf16[2,512,128]{2,1,0:T(8,128)(2,1)S(1)}, u32[]{:S(2)}, u32[]{:S(2)}) %collective-permute-start.8) | collective-permute-done | bytes 262176 | tf_op jit(solution)/shard_map/ppermute | solution.py:42
  133.8 0.9 copy-done.5
  134.7 0.9 copy-done.6
  135.6 6.5 %attend.1 = (bf16[512,256]{1,0:T(8,128)(2,1)S(1)}, bf16[512,256]{1,0:T(8,128)(2,1)S(1)}) custom-call(s32[4]{0:T(128)S(1)} %copy-done.1, bf16[2,512,128]{2,1,0:T(8,128)(2,1)S(1)} %copy-done.3, bf16[2,512,128]{2,1,0:T(8,128)(2,1)S(1)} %copy-done.5, bf16[2,512,128]{2,1,0:T(8,128)(2,1)S(1)} %copy-done.4, bf16[2,512,128]{2,1,0:T(8,128)(2,1)S(1)} %copy-done.6, ...), custom_call_target="tpu_custom_call" | custom-call | flops 1342177280 | bytes 3145728 | tf_op jit(solution)/shard_map/attend/pallas_call | solution.py:248
  142.1 0.7 collective-permute-start.9
  142.8 1.2 collective-permute-done.9
  144.0 5.8 %all-gather.5.cloned.1.call-done.refs_4_ = bf16[5376,256]{1,0:T(8,128)(2,1)} async-done(((bf16[672,256]{1,0:T(8,128)(2,1)}), bf16[5376,256]{1,0:T(8,128)(2,1)}) %all-gather.5.cloned.1.call-update) | async-done | bytes 2752528 | tf_op jit(solution)/shard_map/all_gather | solution.py:412
  149.7 0.8 collective-permute-start.13
  150.6 3.9 %collective-permute-start.10 = (bf16[2,512,256]{2,1,0:T(8,128)(2,1)S(1)}, bf16[2,512,256]{2,1,0:T(8,128)(2,1)S(1)}, u32[]{:S(2)}, u32[]{:S(2)}) collective-permute-start(bf16[2,512,256]{2,1,0:T(8,128)(2,1)S(1)} %pad_maximum_fusion.2.refs_0_), channel_id=1, source_target_pairs={{0,3},{1,0},{2,1},{3,2},{4,7},{5,4},{6,5},{7,6},{8,11},{9,8},{10,9... | collective-permute-start | bytes 1572872 | tf_op jit(solution)/shard_map/ppermute | solution.py:37
  154.5 0.7 collective-permute-start.12
  155.2 21.9 %collective-permute-done.10.refs_1_ = bf16[2,512,256]{2,1,0:T(8,128)(2,1)S(1)} collective-permute-done((bf16[2,512,256]{2,1,0:T(8,128)(2,1)S(1)}, bf16[2,512,256]{2,1,0:T(8,128)(2,1)S(1)}, u32[]{:S(2)}, u32[]{:S(2)}) %collective-permute-start.10) | collective-permute-done | bytes 524320 | tf_op jit(solution)/shard_map/ppermute | solution.py:37
  177.1 3.4 %collective-permute-done.12.refs_3_ = bf16[2,512,256]{2,1,0:T(8,128)(2,1)S(1)} collective-permute-done((bf16[2,512,256]{2,1,0:T(8,128)(2,1)S(1)}, bf16[2,512,256]{2,1,0:T(8,128)(2,1)S(1)}, u32[]{:S(2)}, u32[]{:S(2)}) %collective-permute-start.12) | collective-permute-done | bytes 524320 | tf_op jit(solution)/shard_map/ppermute | solution.py:37
  180.5 1.8 copy-done.2
  182.3 4.0 %out_project.1 = (bf16[128,1344]{1,0:T(8,128)(2,1)S(1)}, bf16[128,1344]{1,0:T(8,128)(2,1)S(1)}, bf16[128,1344]{1,0:T(8,128)(2,1)S(1)}, bf16[128,1344]{1,0:T(8,128)(2,1)S(1)}) custom-call(s32[4]{0:T(128)S(1)} %copy-done.1, bf16[2,512,256]{2,1,0:T(8,128)(2,1)S(1)} %pad_maximum_fusion.2.refs_0_, bf16[2,512,256]{2,1,0:T(8,128)(2,1)S(1)} %collective-permute-done.10.refs_1_, ...), custom_call_target="tpu_custom_call" | custom-call | flops 2818572288 | bytes 9437184 | tf_op jit(solution)/shard_map/out_project/pallas_call | solution.py:294
  187.0 0.8 collective-permute-start.16
  187.9 7.7 %collective-permute-done.14.refs_1_ = bf16[128,1344]{1,0:T(8,128)(2,1)S(1)} collective-permute-done((bf16[128,1344]{1,0:T(8,128)(2,1)S(1)}, bf16[128,1344]{1,0:T(8,128)(2,1)S(1)}, u32[]{:S(2)}, u32[]{:S(2)}) %collective-permute-start.14) | collective-permute-done | bytes 344096 | tf_op jit(solution)/shard_map/ppermute | solution.py:37
  195.6 1.1 collective-permute-done.15.refs_2_
  196.7 9.5 %collective-permute-done.16.refs_3_ = bf16[128,1344]{1,0:T(8,128)(2,1)S(1)} collective-permute-done((bf16[128,1344]{1,0:T(8,128)(2,1)S(1)}, bf16[128,1344]{1,0:T(8,128)(2,1)S(1)}, u32[]{:S(2)}, u32[]{:S(2)}) %collective-permute-start.16) | collective-permute-done | bytes 344096 | tf_op jit(solution)/shard_map/ppermute | solution.py:37
  206.2 2.9 %final_norm.1 = bf16[128,5376]{1,0:T(8,128)(2,1)} custom-call(s32[4]{0:T(128)S(1)} %copy-done.1, bf16[128,1344]{1,0:T(8,128)(2,1)S(1)} %get-tuple-element.47.refs_0_, bf16[128,1344]{1,0:T(8,128)(2,1)S(1)} %collective-permute-done.14.refs_1_, bf16[128,1344]{1,0:T(8,128)(2,1)S(1)} %collective-permute-done.15.refs_2_, ...), custom_call_target="tpu_custom_call" | custom-call | tf_op jit(solution)/shard_map/final_norm/pallas_call | solution.py:327
  (47 shorter events, 1.6 us)
Async XLA Ops:
  6.5 15.1 %copy-start.9 = (f32[5376]{0:T(1024)S(1)}, f32[5376]{0:T(1024)}, u32[]{:S(2)}) copy-start(f32[5376]{0:T(1024)} %param.16) | copy-start | bytes 64516
  6.5 93.4 %all-gather.3.cloned.1.call-start = ((), (), s32[]{:S(2)}) async-start(), calls=%async_computation | async-start | bytes 6193152 | tf_op jit(solution)/shard_map/all_gather | solution.py:381
  8.3 1.8 collective-permute-start
  21.5 128.2 %all-gather.5.cloned.1.call-start = ((), (), s32[]{:S(2)}) async-start(), calls=%async_computation.1 | async-start | bytes 3096576 | tf_op jit(solution)/shard_map/all_gather | solution.py:412
  26.1 31.0 %collective-permute-start.1 = (bf16[128,5376]{1,0:T(8,128)(2,1)}, bf16[128,5376]{1,0:T(8,128)(2,1)S(1)}, u32[]{:S(2)}, u32[]{:S(2)}) collective-permute-start(bf16[128,5376]{1,0:T(8,128)(2,1)} %input_norm.1.refs_0_), channel_id=1, source_target_pairs={{0,1},{1,2},{2,3},{3,0},{4,5},{5,6},{6,7},{7,4},{8,9},{9,10},{10,1... | collective-permute-start | bytes 4128776 | tf_op jit(solution)/shard_map/ppermute | solution.py:37
  27.3 29.8 %collective-permute-start.2 = (bf16[128,5376]{1,0:T(8,128)(2,1)}, bf16[128,5376]{1,0:T(8,128)(2,1)S(1)}, u32[]{:S(2)}, u32[]{:S(2)}) collective-permute-start(bf16[128,5376]{1,0:T(8,128)(2,1)} %input_norm.1.refs_0_), channel_id=1, source_target_pairs={{0,3},{1,0},{2,1},{3,2},{4,7},{5,4},{6,5},{7,6},{8,11},{9,8},{10,9... | collective-permute-start | bytes 4128776 | tf_op jit(solution)/shard_map/ppermute | solution.py:37
  33.5 2.0 collective-permute-start.3
  57.1 14.1 %copy-start.7 = (bf16[128,5376]{1,0:T(8,128)(2,1)}, bf16[128,5376]{1,0:T(8,128)(2,1)S(1)}, u32[]{:S(2)}) copy-start(bf16[128,5376]{1,0:T(8,128)(2,1)S(1)} %collective-permute-done.1.refs_4_) | copy-start | bytes 4128772
  57.1 14.1 %copy-start.8 = (bf16[128,5376]{1,0:T(8,128)(2,1)}, bf16[128,5376]{1,0:T(8,128)(2,1)S(1)}, u32[]{:S(2)}) copy-start(bf16[128,5376]{1,0:T(8,128)(2,1)S(1)} %collective-permute-done.2.refs_1_) | copy-start | bytes 4128772
  57.1 13.8 %collective-permute-start.4 = (bf16[64,5376]{1,0:T(8,128)(2,1)S(1)}, bf16[64,5376]{1,0:T(8,128)(2,1)}, u32[]{:S(2)}, u32[]{:S(2)}) collective-permute-start(bf16[64,5376]{1,0:T(8,128)(2,1)S(1)} %slice.67), channel_id=1, source_target_pairs={{0,1},{1,2},{2,3},{3,0},{4,5},{5,6},{6,7},{7,4},{8,9},{9,10},{10,1... | collective-permute-start | bytes 2064392 | tf_op jit(solution)/shard_map/ppermute | solution.py:37
  60.3 10.9 %collective-permute-start.5 = (bf16[64,5376]{1,0:T(8,128)(2,1)}, bf16[64,5376]{1,0:T(8,128)(2,1)}, u32[]{:S(2)}, u32[]{:S(2)}) collective-permute-start(bf16[64,5376]{1,0:T(8,128)(2,1)} %slice.68), channel_id=1, source_target_pairs={{0,3},{1,0},{2,1},{3,2},{4,7},{5,4},{6,5},{7,6},{8,11},{9,8},{10,9... | collective-permute-start | bytes 2064392 | tf_op jit(solution)/shard_map/ppermute | solution.py:37
  79.5 31.1 %collective-permute-start.6 = (bf16[512,5376]{1,0:T(8,128)(2,1)}, bf16[512,5376]{1,0:T(8,128)(2,1)}, u32[]{:S(2)}, u32[]{:S(2)}) collective-permute-start(bf16[512,5376]{1,0:T(8,128)(2,1)} %place_rows.1.rows_hbm), channel_id=1, source_target_pairs={{0,4},{4,0},{8,12},{12,8},{16,20},{20,16},{24,28},{28,24},{32,36},... | collective-permute-start | bytes 16515080 | tf_op jit(solution)/shard_map/ppermute | solution.py:33
  108.5 25.2 %copy-start.1 = (s32[4]{0:T(128)S(1)}, s32[4]{0:T(128)}, u32[]{:S(2)}) copy-start(s32[4]{0:T(128)} %pad_add_fusion.2.place_ref) | copy-start | bytes 52
  108.5 25.2 %copy-start.3 = (bf16[2,512,128]{2,1,0:T(8,128)(2,1)S(1)}, bf16[2,512,128]{2,1,0:T(8,128)(2,1)}, u32[]{:S(2)}) copy-start(bf16[2,512,128]{2,1,0:T(8,128)(2,1)} %get-tuple-element.36.qmine_ref) | copy-start | bytes 786436
  108.5 25.2 %copy-start.4 = (bf16[2,512,128]{2,1,0:T(8,128)(2,1)S(1)}, bf16[2,512,128]{2,1,0:T(8,128)(2,1)}, u32[]{:S(2)}) copy-start(bf16[2,512,128]{2,1,0:T(8,128)(2,1)} %get-tuple-element.38.mine_ref) | copy-start | bytes 786436
  108.6 13.9 %collective-permute-start.7 = (bf16[2,512,128]{2,1,0:T(8,128)(2,1)}, bf16[2,512,128]{2,1,0:T(8,128)(2,1)S(1)}, u32[]{:S(2)}, u32[]{:S(2)}) collective-permute-start(bf16[2,512,128]{2,1,0:T(8,128)(2,1)} %get-tuple-element.38.mine_ref), channel_id=1, source_target_pairs={{0,8},{4,12},{8,16},{12,20},{16,24},{20,28},{24,32},{28,36},{32,40... | collective-permute-start | bytes 786440 | tf_op jit(solution)/shard_map/ppermute | solution.py:42
  119.3 14.5 %collective-permute-start.8 = (bf16[2,512,128]{2,1,0:T(8,128)(2,1)}, bf16[2,512,128]{2,1,0:T(8,128)(2,1)S(1)}, u32[]{:S(2)}, u32[]{:S(2)}) collective-permute-start(bf16[2,512,128]{2,1,0:T(8,128)(2,1)} %get-tuple-element.39.other_ref), channel_id=1, source_target_pairs={{0,8},{4,12},{8,16},{12,20},{16,24},{20,28},{24,32},{28,36},{32,40... | collective-permute-start | bytes 786440 | tf_op jit(solution)/shard_map/ppermute | solution.py:42
  133.7 1.0 copy-start.5
  134.7 1.0 copy-start.6
  142.1 1.8 collective-permute-start.9
  149.7 30.8 %collective-permute-start.13 = (bf16[5376,256]{1,0:T(8,128)(2,1)}, bf16[5376,256]{1,0:T(8,128)(2,1)S(1)}, u32[]{:S(2)}, u32[]{:S(2)}) collective-permute-start(bf16[5376,256]{1,0:T(8,128)(2,1)} %all-gather.5.cloned.1.call-done.refs_4_), channel_id=1, source_target_pairs={{0,4},{4,0},{8,12},{12,8},{16,20},{20,16},{24,28},{28,24},{32,36},... | collective-permute-start | bytes 8257544 | tf_op jit(solution)/shard_map/ppermute | solution.py:33
  150.6 37.3 %copy-start.10 = (f32[5376]{0:T(1024)S(1)}, f32[5376]{0:T(1024)}, u32[]{:S(2)}) copy-start(f32[5376]{0:T(1024)} %param.19) | copy-start | bytes 64516
  150.6 55.6 %copy-start = (bf16[128,5376]{1,0:T(8,128)(2,1)S(1)}, bf16[128,5376]{1,0:T(8,128)(2,1)}, u32[]{:S(2)}) copy-start(bf16[128,5376]{1,0:T(8,128)(2,1)} %refs_4_.1) | copy-start | bytes 4128772
  150.6 26.5 %collective-permute-start.10 = (bf16[2,512,256]{2,1,0:T(8,128)(2,1)S(1)}, bf16[2,512,256]{2,1,0:T(8,128)(2,1)S(1)}, u32[]{:S(2)}, u32[]{:S(2)}) collective-permute-start(bf16[2,512,256]{2,1,0:T(8,128)(2,1)S(1)} %pad_maximum_fusion.2.refs_0_), channel_id=1, source_target_pairs={{0,3},{1,0},{2,1},{3,2},{4,7},{5,4},{6,5},{7,6},{8,11},{9,8},{10,9... | collective-permute-start | bytes 1572872 | tf_op jit(solution)/shard_map/ppermute | solution.py:37
  154.5 22.6 %collective-permute-start.11 = (bf16[2,512,256]{2,1,0:T(8,128)(2,1)S(1)}, bf16[2,512,256]{2,1,0:T(8,128)(2,1)S(1)}, u32[]{:S(2)}, u32[]{:S(2)}) collective-permute-start(bf16[2,512,256]{2,1,0:T(8,128)(2,1)S(1)} %pad_maximum_fusion.2.refs_0_), channel_id=1, source_target_pairs={{0,2},{1,3},{2,0},{3,1},{4,6},{5,7},{6,4},{7,5},{8,10},{9,11},{10,... | collective-permute-start | bytes 1572872 | tf_op jit(solution)/shard_map/ppermute | solution.py:37
  154.5 26.0 %collective-permute-start.12 = (bf16[2,512,256]{2,1,0:T(8,128)(2,1)S(1)}, bf16[2,512,256]{2,1,0:T(8,128)(2,1)S(1)}, u32[]{:S(2)}, u32[]{:S(2)}) collective-permute-start(bf16[2,512,256]{2,1,0:T(8,128)(2,1)S(1)} %pad_maximum_fusion.2.refs_0_), channel_id=1, source_target_pairs={{0,1},{1,2},{2,3},{3,0},{4,5},{5,6},{6,7},{7,4},{8,9},{9,10},{10,1... | collective-permute-start | bytes 1572872 | tf_op jit(solution)/shard_map/ppermute | solution.py:37
  180.5 1.8 copy-start.2
  186.3 9.3 %collective-permute-start.14 = (bf16[128,1344]{1,0:T(8,128)(2,1)S(1)}, bf16[128,1344]{1,0:T(8,128)(2,1)S(1)}, u32[]{:S(2)}, u32[]{:S(2)}) collective-permute-start(bf16[128,1344]{1,0:T(8,128)(2,1)S(1)} %get-tuple-element.48), channel_id=1, source_target_pairs={{0,3},{1,0},{2,1},{3,2},{4,7},{5,4},{6,5},{7,6},{8,11},{9,8},{10,9... | collective-permute-start | bytes 1032200 | tf_op jit(solution)/shard_map/ppermute | solution.py:37
  186.6 10.1 %collective-permute-start.15 = (bf16[128,1344]{1,0:T(8,128)(2,1)S(1)}, bf16[128,1344]{1,0:T(8,128)(2,1)S(1)}, u32[]{:S(2)}, u32[]{:S(2)}) collective-permute-start(bf16[128,1344]{1,0:T(8,128)(2,1)S(1)} %get-tuple-element.49), channel_id=1, source_target_pairs={{0,2},{1,3},{2,0},{3,1},{4,6},{5,7},{6,4},{7,5},{8,10},{9,11},{10,... | collective-permute-start | bytes 1032200 | tf_op jit(solution)/shard_map/ppermute | solution.py:37
  187.0 19.2 %collective-permute-start.16 = (bf16[128,1344]{1,0:T(8,128)(2,1)S(1)}, bf16[128,1344]{1,0:T(8,128)(2,1)S(1)}, u32[]{:S(2)}, u32[]{:S(2)}) collective-permute-start(bf16[128,1344]{1,0:T(8,128)(2,1)S(1)} %get-tuple-element.50), channel_id=1, source_target_pairs={{0,1},{1,2},{2,3},{3,0},{4,5},{5,6},{6,7},{7,4},{8,9},{9,10},{10,1... | collective-permute-start | bytes 1032200 | tf_op jit(solution)/shard_map/ppermute | solution.py:37
Sparse Core Ops, SparseCore 0:
  21.7 78.2 all-gather.2
  101.7 47.9 all-gather.4

commit v4 on v3

--- a/solution.py
+++ b/solution.py
@@ -99,8 +99,8 @@
 
 
 def project_body(
-    mine, place_ref, rows_hbm, weight_hbm, gq_ref, gk_ref, cos_ref, sin_ref,
-    q_ref, kv_ref, rows_ref, weight_ref, total_ref, sems,
+    mine, place_ref, rows_hbm, weight_ref, gq_ref, gk_ref, cos_ref, sin_ref,
+    q_ref, kv_ref, rows_ref, total_ref, sems,
 ):
     c = place_ref[3]
     start = pl.multiple_of((c if mine else 1 - c) * BLOCK, BLOCK)
@@ -109,22 +109,12 @@
     for k in range(PARTS):
         span = pl.ds(k * step, step)
         copies.append(
-            (
-                pltpu.make_async_copy(rows_hbm.at[:, span], rows_ref.at[:, span], sems.at[2 * k]),
-                pltpu.make_async_copy(
-                    weight_hbm.at[span], weight_ref.at[span], sems.at[2 * k + 1]
-                ),
-            )
+            pltpu.make_async_copy(rows_hbm.at[:, span], rows_ref.at[:, span], sems.at[k])
         )
-    for pair in copies[:2]:
-        for copy in pair:
-            copy.start()
-    for k, pair in enumerate(copies):
-        for copy in pair:
-            copy.wait()
-        if k + 2 < PARTS:
-            for copy in copies[k + 2]:
-                copy.start()
+    for copy in copies:
+        copy.start()
+    for k, copy in enumerate(copies):
+        copy.wait()
         span = slice(k * step, (k + 1) * step)
         part = jnp.dot(
             rows_ref[:, span], weight_ref[span, :], preferred_element_type=jnp.float32
@@ -155,16 +145,15 @@
     head = jax.ShapeDtypeStruct((2, BLOCK, HEAD_SIZE), jnp.bfloat16)
     return pl.pallas_call(
         functools.partial(project_body, mine),
-        in_specs=[SMEM, HBM, HBM] + [HELD] * 4,
+        in_specs=[SMEM, HBM] + [HELD] * 5,
         out_specs=[HELD] * 2,
         out_shape=[head] * 2,
         scratch_shapes=[
             pltpu.VMEM((BLOCK, width), jnp.bfloat16),
-            pltpu.VMEM((width, 512), jnp.bfloat16),
             pltpu.VMEM((BLOCK, 512), jnp.float32),
-            pltpu.SemaphoreType.DMA((2 * PARTS,)),
+            pltpu.SemaphoreType.DMA((PARTS,)),
         ],
-        compiler_params=pltpu.CompilerParams(vmem_limit_bytes=60 * MIB),
+        compiler_params=pltpu.CompilerParams(vmem_limit_bytes=50 * MIB),
         cost_estimate=pl.CostEstimate(
             flops=2 * BLOCK * width * 512, bytes_accessed=12 * MIB, transcendentals=0
         ),

time: 217 us -> 216 us (level)
  transfers between devices with their start and end apart: 19 -> 19, of which waited for: 14 -> 13; matrix products, arithmetic and copies ran while one was open for 4% -> 4% of each run, Pallas kernels for 17% -> 16%
where the time goes in v4:
time: 216 us; the launch traced here: 215 us
  waiting for transfers between devices  97.5 us (45%)
  Pallas kernels  41.9 us (19%)
  starting transfers between devices  27.4 us (13%)
  blocking collectives  22.4 us (10%)
  between operations  13.6 us (6%)
  local copies, waits for them, and re-layouts  7.64 us (4%)
  other arithmetic  4.61 us (2%)
    ppermute x10, waiting for transfers between devices, shift_x(): return lax.ppermute(value, 'tp', [(x, (x + steps) % X) for x in range(X)])  64.3 us
    pallas_call x2, Pallas kernels, project(): pl.pallas_call(functools.partial(project_body, mine), in_specs=[SMEM, HBM...  16.3 us
    ppermute x10, starting transfers between devices, shift_x(): return lax.ppermute(value, 'tp', [(x, (x + steps) % X) for x in range(X)])  12.2 us
    all_gather x1, waiting for transfers between devices, shards(): lax.all_gather(part, 'ctx', axis=0, tiled=True, axis_index_groups=COLUMNS)  11.9 us
    all_gather x1, blocking collectives, shards(): lax.all_gather(part, 'ctx', axis=0, tiled=True, axis_index_groups=ROWS)  11.4 us
    ppermute x2, waiting for transfers between devices, next_pair(): return lax.ppermute(value, 'ctx', pairs)  11.3 us
    all_gather x1, blocking collectives, shards(): lax.all_gather(part_out, 'ctx', axis=0, tiled=True, axis_index_groups=ROWS)  11 us
    ppermute x4, starting transfers between devices, swap_cores(): return lax.ppermute(value, 'ctx', ctx_pairs(lambda z, y, c: (z, y, 1 - c)))  10.5 us
  transfers between devices with their start and end apart: 19, of which 13 were waited for; matrix products, arithmetic and copies ran while one was open for 4% of the time, Pallas kernels for 16%

profile of v4, /device:TPU:25, one launch (start us, length us, event | category | flops | bytes accessed | tf_op | source)
XLA Modules:
  0.0 215.1 jit_solution(16226490161775869110)
XLA Ops:
  6.5 0.9 fusion.6
  7.4 0.8 fusion.8
  8.3 0.8 collective-permute-start
  9.0 1.0 collective-permute-done
  10.1 11.4 %all_gather.12 = bf16[672,512]{1,0:T(8,128)(2,1)} all-gather(bf16[168,512]{1,0:T(8,128)(2,1)S(1)} %fusion), channel_id=1, replica_groups={{0,8,16,24},{4,12,20,28},{32,40,48,56},{36,44,52,60},{64,72,80,88},{68,..., dimensions={0}, use_global_device_ids=true | all-gather | bytes 860160 | tf_op jit(solution)/shard_map/all_gather | solution.py:368
  21.6 0.6 reshape.20.gain_ref
  22.2 3.9 %input_norm.1.refs_0_ = bf16[128,5376]{1,0:T(8,128)(2,1)} custom-call(bf16[128,5376]{1,0:T(8,128)(2,1)} %refs_4_.1, f32[1,5376]{1,0:T(1,128)} %reshape.20.gain_ref), custom_call_target="tpu_custom_call" | custom-call | tf_op jit(solution)/shard_map/input_norm/pallas_call | solution.py:79
  26.1 1.2 collective-permute-start.1
  27.3 1.5 collective-permute-start.2
  28.7 1.2 slice.62
  30.0 1.5 fusion.5
  31.5 1.9 fusion.1
  33.5 0.7 collective-permute-start.3
  34.1 0.3 pad_maximum_fusion
  34.5 11.0 %all_gather.13 = bf16[672,256]{1,0:T(8,128)(2,1)} all-gather(bf16[168,256]{1,0:T(8,128)(2,1)S(1)} %collective-permute-done.3), channel_id=1, replica_groups={{0,8,16,24},{4,12,20,28},{32,40,48,56},{36,44,52,60},{64,72,80,88},{68,..., dimensions={0}, use_global_device_ids=true | all-gather | bytes 430080 | tf_op jit(solution)/shard_map/all_gather | solution.py:388
  45.5 11.5 %collective-permute-done.1.refs_4_ = bf16[128,5376]{1,0:T(8,128)(2,1)S(1)} collective-permute-done((bf16[128,5376]{1,0:T(8,128)(2,1)}, bf16[128,5376]{1,0:T(8,128)(2,1)S(1)}, u32[]{:S(2)}, u32[]{:S(2)}) %collective-permute-start.1) | collective-permute-done | bytes 1376288 | tf_op jit(solution)/shard_map/ppermute | solution.py:37
  57.1 2.3 %collective-permute-start.4 = (bf16[64,5376]{1,0:T(8,128)(2,1)S(1)}, bf16[64,5376]{1,0:T(8,128)(2,1)}, u32[]{:S(2)}, u32[]{:S(2)}) collective-permute-start(bf16[64,5376]{1,0:T(8,128)(2,1)S(1)} %slice.67), channel_id=1, source_target_pairs={{0,1},{1,2},{2,3},{3,0},{4,5},{5,6},{6,7},{7,4},{8,9},{9,10},{10,1... | collective-permute-start | bytes 2064392 | tf_op jit(solution)/shard_map/ppermute | solution.py:37
  59.4 2.0 slice.68
  61.4 1.0 collective-permute-start.5
  62.5 0.6 pad_add_fusion.2.place_ref
  63.1 7.8 %collective-permute-done.4.refs_2_ = bf16[64,5376]{1,0:T(8,128)(2,1)} collective-permute-done((bf16[64,5376]{1,0:T(8,128)(2,1)S(1)}, bf16[64,5376]{1,0:T(8,128)(2,1)}, u32[]{:S(2)}, u32[]{:S(2)}) %collective-permute-start.4) | collective-permute-done | bytes 688160 | tf_op jit(solution)/shard_map/ppermute | solution.py:37
  71.0 1.4 collective-permute-done.5.refs_3_
  72.4 8.3 %place_rows.1.rows_hbm = bf16[512,5376]{1,0:T(8,128)(2,1)} custom-call(s32[4]{0:T(128)} %pad_add_fusion.2.place_ref, bf16[128,5376]{1,0:T(8,128)(2,1)} %input_norm.1.refs_0_, bf16[128,5376]{1,0:T(8,128)(2,1)} %collective-permute-done.2.refs_1_, bf16[64,5376]{1,0:T(8,128)(2,1)} %collective-permute-done.4.refs_2_, ...), custom_call_target="tpu_custom_call" | custom-call | bytes 11534336 | tf_op jit(solution)/shard_map/place_rows/pallas_call | solution.py:177
  80.7 7.3 %collective-permute-start.6 = (bf16[512,5376]{1,0:T(8,128)(2,1)}, bf16[512,5376]{1,0:T(8,128)(2,1)}, u32[]{:S(2)}, u32[]{:S(2)}) collective-permute-start(bf16[512,5376]{1,0:T(8,128)(2,1)} %place_rows.1.rows_hbm), channel_id=1, source_target_pairs={{0,4},{4,0},{8,12},{12,8},{16,20},{20,16},{24,28},{28,24},{32,36},... | collective-permute-start | bytes 16515080 | tf_op jit(solution)/shard_map/ppermute | solution.py:33
  88.0 11.9 %all-gather.3.cloned.1.call-done.weight_ref = bf16[5376,512]{1,0:T(8,128)(2,1)} async-done(((bf16[672,512]{1,0:T(8,128)(2,1)}), bf16[5376,512]{1,0:T(8,128)(2,1)}) %all-gather.3.cloned.1.call-update) | async-done | bytes 5505040 | tf_op jit(solution)/shard_map/all_gather | solution.py:370
  100.0 8.1 %project_own.1 = (bf16[2,512,128]{2,1,0:T(8,128)(2,1)S(1)}, bf16[2,512,128]{2,1,0:T(8,128)(2,1)S(1)}) custom-call(s32[4]{0:T(128)S(1)} %copy-done.1, bf16[512,5376]{1,0:T(8,128)(2,1)} %place_rows.1.rows_hbm, bf16[5376,512]{1,0:T(8,128)(2,1)} %all-gather.3.cloned.1.call-done.weight_ref, f32[1,128]{1,0:T(1,128)S(1)} %bitcast.12, f32[1,128]{1,0:T(1,128)S(1)} %bitcast.14, ...), custom_call_target="tpu_custom_call" | custom-call | flops 2818572288 | bytes 12582912 | tf_op jit(solution)/shard_map/project_own/pallas_call | solution.py:146
  108.1 1.9 collective-permute-start.7
  110.0 8.2 %project_other.1 = (bf16[2,512,128]{2,1,0:T(8,128)(2,1)S(1)}, bf16[2,512,128]{2,1,0:T(8,128)(2,1)S(1)}) custom-call(s32[4]{0:T(128)S(1)} %copy-done.1, bf16[512,5376]{1,0:T(8,128)(2,1)} %collective-permute-done.6.rows_hbm, bf16[5376,512]{1,0:T(8,128)(2,1)} %all-gather.3.cloned.1.call-done.weight_ref, f32[1,128]{1,0:T(1,128)S(1)} %bitcast.13, ...), custom_call_target="tpu_custom_call" | custom-call | flops 2818572288 | bytes 12582912 | tf_op jit(solution)/shard_map/project_other/pallas_call | solution.py:146
  118.3 2.1 collective-permute-start.8
  120.6 11.3 %collective-permute-done.8.pother_ref = bf16[2,512,128]{2,1,0:T(8,128)(2,1)S(1)} collective-permute-done((bf16[2,512,128]{2,1,0:T(8,128)(2,1)S(1)}, bf16[2,512,128]{2,1,0:T(8,128)(2,1)S(1)}, u32[]{:S(2)}, u32[]{:S(2)}) %collective-permute-start.8) | collective-permute-done | bytes 262176 | tf_op jit(solution)/shard_map/ppermute | solution.py:42
  131.9 6.5 %attend.1 = (bf16[512,256]{1,0:T(8,128)(2,1)S(1)}, bf16[512,256]{1,0:T(8,128)(2,1)S(1)}) custom-call(s32[4]{0:T(128)S(1)} %copy-done.1, bf16[2,512,128]{2,1,0:T(8,128)(2,1)S(1)} %get-tuple-element.36.qmine_ref, bf16[2,512,128]{2,1,0:T(8,128)(2,1)S(1)} %get-tuple-element.37.qother_ref, bf16[2,512,128]{2,1,0:T(8,128)(2,1)S(1)} %get-tuple-element.38.mine_ref, ...), custom_call_target="tpu_custom_call" | custom-call | flops 1342177280 | bytes 3145728 | tf_op jit(solution)/shard_map/attend/pallas_call | solution.py:237
  138.3 1.5 collective-permute-start.9
  139.8 1.2 collective-permute-done.9
  141.0 7.8 %all-gather.5.cloned.1.call-done.refs_4_ = bf16[5376,256]{1,0:T(8,128)(2,1)} async-done(((bf16[672,256]{1,0:T(8,128)(2,1)}), bf16[5376,256]{1,0:T(8,128)(2,1)}) %all-gather.5.cloned.1.call-update) | async-done | bytes 2752528 | tf_op jit(solution)/shard_map/all_gather | solution.py:401
  148.8 1.0 collective-permute-start.13
  149.9 3.9 %collective-permute-start.10 = (bf16[2,512,256]{2,1,0:T(8,128)(2,1)S(1)}, bf16[2,512,256]{2,1,0:T(8,128)(2,1)S(1)}, u32[]{:S(2)}, u32[]{:S(2)}) collective-permute-start(bf16[2,512,256]{2,1,0:T(8,128)(2,1)S(1)} %pad_maximum_fusion.2.refs_0_), channel_id=1, source_target_pairs={{0,3},{1,0},{2,1},{3,2},{4,7},{5,4},{6,5},{7,6},{8,11},{9,8},{10,9... | collective-permute-start | bytes 1572872 | tf_op jit(solution)/shard_map/ppermute | solution.py:37
  153.8 0.8 collective-permute-start.12
  154.5 21.8 %collective-permute-done.10.refs_1_ = bf16[2,512,256]{2,1,0:T(8,128)(2,1)S(1)} collective-permute-done((bf16[2,512,256]{2,1,0:T(8,128)(2,1)S(1)}, bf16[2,512,256]{2,1,0:T(8,128)(2,1)S(1)}, u32[]{:S(2)}, u32[]{:S(2)}) %collective-permute-start.10) | collective-permute-done | bytes 524320 | tf_op jit(solution)/shard_map/ppermute | solution.py:37
  176.3 3.5 %collective-permute-done.12.refs_3_ = bf16[2,512,256]{2,1,0:T(8,128)(2,1)S(1)} collective-permute-done((bf16[2,512,256]{2,1,0:T(8,128)(2,1)S(1)}, bf16[2,512,256]{2,1,0:T(8,128)(2,1)S(1)}, u32[]{:S(2)}, u32[]{:S(2)}) %collective-permute-start.12) | collective-permute-done | bytes 524320 | tf_op jit(solution)/shard_map/ppermute | solution.py:37
  179.9 1.8 copy-done.4
  181.6 4.0 %out_project.1 = (bf16[128,1344]{1,0:T(8,128)(2,1)S(1)}, bf16[128,1344]{1,0:T(8,128)(2,1)S(1)}, bf16[128,1344]{1,0:T(8,128)(2,1)S(1)}, bf16[128,1344]{1,0:T(8,128)(2,1)S(1)}) custom-call(s32[4]{0:T(128)S(1)} %copy-done.1, bf16[2,512,256]{2,1,0:T(8,128)(2,1)S(1)} %pad_maximum_fusion.2.refs_0_, bf16[2,512,256]{2,1,0:T(8,128)(2,1)S(1)} %collective-permute-done.10.refs_1_, ...), custom_call_target="tpu_custom_call" | custom-call | flops 2818572288 | bytes 9437184 | tf_op jit(solution)/shard_map/out_project/pallas_call | solution.py:283
  185.6 0.3 collective-permute-start.14
  185.9 0.4 collective-permute-start.15
  186.3 0.9 collective-permute-start.16
  187.2 7.8 %collective-permute-done.14.refs_1_ = bf16[128,1344]{1,0:T(8,128)(2,1)S(1)} collective-permute-done((bf16[128,1344]{1,0:T(8,128)(2,1)S(1)}, bf16[128,1344]{1,0:T(8,128)(2,1)S(1)}, u32[]{:S(2)}, u32[]{:S(2)}) %collective-permute-start.14) | collective-permute-done | bytes 344096 | tf_op jit(solution)/shard_map/ppermute | solution.py:37
  194.9 1.0 collective-permute-done.15.refs_2_
  196.0 9.5 %collective-permute-done.16.refs_3_ = bf16[128,1344]{1,0:T(8,128)(2,1)S(1)} collective-permute-done((bf16[128,1344]{1,0:T(8,128)(2,1)S(1)}, bf16[128,1344]{1,0:T(8,128)(2,1)S(1)}, u32[]{:S(2)}, u32[]{:S(2)}) %collective-permute-start.16) | collective-permute-done | bytes 344096 | tf_op jit(solution)/shard_map/ppermute | solution.py:37
  205.4 2.9 %final_norm.1 = bf16[128,5376]{1,0:T(8,128)(2,1)} custom-call(s32[4]{0:T(128)S(1)} %copy-done.1, bf16[128,1344]{1,0:T(8,128)(2,1)S(1)} %get-tuple-element.47.refs_0_, bf16[128,1344]{1,0:T(8,128)(2,1)S(1)} %collective-permute-done.14.refs_1_, bf16[128,1344]{1,0:T(8,128)(2,1)S(1)} %collective-permute-done.15.refs_2_, ...), custom_call_target="tpu_custom_call" | custom-call | tf_op jit(solution)/shard_map/final_norm/pallas_call | solution.py:316
  (41 shorter events, 0.7 us)
Async XLA Ops:
  6.5 15.1 %copy-start.6 = (f32[5376]{0:T(1024)S(1)}, f32[5376]{0:T(1024)}, u32[]{:S(2)}) copy-start(f32[5376]{0:T(1024)} %param.16) | copy-start | bytes 64516
  6.5 93.4 %all-gather.3.cloned.1.call-start = ((), (), s32[]{:S(2)}) async-start(), calls=%async_computation | async-start | bytes 6193152 | tf_op jit(solution)/shard_map/all_gather | solution.py:370
  8.3 1.8 collective-permute-start
  21.5 127.3 %all-gather.5.cloned.1.call-start = ((), (), s32[]{:S(2)}) async-start(), calls=%async_computation.1 | async-start | bytes 3096576 | tf_op jit(solution)/shard_map/all_gather | solution.py:401
  26.1 31.0 %collective-permute-start.1 = (bf16[128,5376]{1,0:T(8,128)(2,1)}, bf16[128,5376]{1,0:T(8,128)(2,1)S(1)}, u32[]{:S(2)}, u32[]{:S(2)}) collective-permute-start(bf16[128,5376]{1,0:T(8,128)(2,1)} %input_norm.1.refs_0_), channel_id=1, source_target_pairs={{0,1},{1,2},{2,3},{3,0},{4,5},{5,6},{6,7},{7,4},{8,9},{9,10},{10,1... | collective-permute-start | bytes 4128776 | tf_op jit(solution)/shard_map/ppermute | solution.py:37
  27.3 29.8 %collective-permute-start.2 = (bf16[128,5376]{1,0:T(8,128)(2,1)}, bf16[128,5376]{1,0:T(8,128)(2,1)}, u32[]{:S(2)}, u32[]{:S(2)}) collective-permute-start(bf16[128,5376]{1,0:T(8,128)(2,1)} %input_norm.1.refs_0_), channel_id=1, source_target_pairs={{0,3},{1,0},{2,1},{3,2},{4,7},{5,4},{6,5},{7,6},{8,11},{9,8},{10,9... | collective-permute-start | bytes 4128776 | tf_op jit(solution)/shard_map/ppermute | solution.py:37
  33.5 1.0 collective-permute-start.3
  57.1 15.3 %copy-start.5 = (bf16[128,5376]{1,0:T(8,128)(2,1)}, bf16[128,5376]{1,0:T(8,128)(2,1)S(1)}, u32[]{:S(2)}) copy-start(bf16[128,5376]{1,0:T(8,128)(2,1)S(1)} %collective-permute-done.1.refs_4_) | copy-start | bytes 4128772
  57.1 13.8 %collective-permute-start.4 = (bf16[64,5376]{1,0:T(8,128)(2,1)S(1)}, bf16[64,5376]{1,0:T(8,128)(2,1)}, u32[]{:S(2)}, u32[]{:S(2)}) collective-permute-start(bf16[64,5376]{1,0:T(8,128)(2,1)S(1)} %slice.67), channel_id=1, source_target_pairs={{0,1},{1,2},{2,3},{3,0},{4,5},{5,6},{6,7},{7,4},{8,9},{9,10},{10,1... | collective-permute-start | bytes 2064392 | tf_op jit(solution)/shard_map/ppermute | solution.py:37
  61.4 10.9 %collective-permute-start.5 = (bf16[64,5376]{1,0:T(8,128)(2,1)}, bf16[64,5376]{1,0:T(8,128)(2,1)}, u32[]{:S(2)}, u32[]{:S(2)}) collective-permute-start(bf16[64,5376]{1,0:T(8,128)(2,1)} %slice.68), channel_id=1, source_target_pairs={{0,3},{1,0},{2,1},{3,2},{4,7},{5,4},{6,5},{7,6},{8,11},{9,8},{10,9... | collective-permute-start | bytes 2064392 | tf_op jit(solution)/shard_map/ppermute | solution.py:37
  63.1 36.8 %copy-start.1 = (s32[4]{0:T(128)S(1)}, s32[4]{0:T(128)}, u32[]{:S(2)}) copy-start(s32[4]{0:T(128)} %pad_add_fusion.2.place_ref) | copy-start | bytes 52
  63.1 36.8 %copy-start.2 = (f32[128]{0:T(128)S(1)}, f32[128]{0:T(128)}, u32[]{:S(2)}) copy-start(f32[128]{0:T(128)} %param.17) | copy-start | bytes 1540
  63.1 36.8 %copy-start.3 = (f32[128]{0:T(128)S(1)}, f32[128]{0:T(128)}, u32[]{:S(2)}) copy-start(f32[128]{0:T(128)} %param.18) | copy-start | bytes 1540
  80.7 29.3 %collective-permute-start.6 = (bf16[512,5376]{1,0:T(8,128)(2,1)}, bf16[512,5376]{1,0:T(8,128)(2,1)}, u32[]{:S(2)}, u32[]{:S(2)}) collective-permute-start(bf16[512,5376]{1,0:T(8,128)(2,1)} %place_rows.1.rows_hbm), channel_id=1, source_target_pairs={{0,4},{4,0},{8,12},{12,8},{16,20},{20,16},{24,28},{28,24},{32,36},... | collective-permute-start | bytes 16515080 | tf_op jit(solution)/shard_map/ppermute | solution.py:33
  108.1 12.5 %collective-permute-start.7 = (bf16[2,512,128]{2,1,0:T(8,128)(2,1)S(1)}, bf16[2,512,128]{2,1,0:T(8,128)(2,1)S(1)}, u32[]{:S(2)}, u32[]{:S(2)}) collective-permute-start(bf16[2,512,128]{2,1,0:T(8,128)(2,1)S(1)} %get-tuple-element.38.mine_ref), channel_id=1, source_target_pairs={{0,8},{4,12},{8,16},{12,20},{16,24},{20,28},{24,32},{28,36},{32,40... | collective-permute-start | bytes 786440 | tf_op jit(solution)/shard_map/ppermute | solution.py:42
  118.3 13.6 %collective-permute-start.8 = (bf16[2,512,128]{2,1,0:T(8,128)(2,1)S(1)}, bf16[2,512,128]{2,1,0:T(8,128)(2,1)S(1)}, u32[]{:S(2)}, u32[]{:S(2)}) collective-permute-start(bf16[2,512,128]{2,1,0:T(8,128)(2,1)S(1)} %get-tuple-element.39.other_ref), channel_id=1, source_target_pairs={{0,8},{4,12},{8,16},{12,20},{16,24},{20,28},{24,32},{28,36},{32,40... | collective-permute-start | bytes 786440 | tf_op jit(solution)/shard_map/ppermute | solution.py:42
  138.3 2.7 %collective-permute-start.9 = (bf16[512,256]{1,0:T(8,128)(2,1)S(1)}, bf16[512,256]{1,0:T(8,128)(2,1)S(1)}, u32[]{:S(2)}, u32[]{:S(2)}) collective-permute-start(bf16[512,256]{1,0:T(8,128)(2,1)S(1)} %get-tuple-element.43), channel_id=1, source_target_pairs={{0,4},{4,0},{8,12},{12,8},{16,20},{20,16},{24,28},{28,24},{32,36},... | collective-permute-start | bytes 786440 | tf_op jit(solution)/shard_map/ppermute | solution.py:33
  148.8 31.0 %collective-permute-start.13 = (bf16[5376,256]{1,0:T(8,128)(2,1)}, bf16[5376,256]{1,0:T(8,128)(2,1)S(1)}, u32[]{:S(2)}, u32[]{:S(2)}) collective-permute-start(bf16[5376,256]{1,0:T(8,128)(2,1)} %all-gather.5.cloned.1.call-done.refs_4_), channel_id=1, source_target_pairs={{0,4},{4,0},{8,12},{12,8},{16,20},{20,16},{24,28},{28,24},{32,36},... | collective-permute-start | bytes 8257544 | tf_op jit(solution)/shard_map/ppermute | solution.py:33
  149.8 37.4 %copy-start.7 = (f32[5376]{0:T(1024)S(1)}, f32[5376]{0:T(1024)}, u32[]{:S(2)}) copy-start(f32[5376]{0:T(1024)} %param.19) | copy-start | bytes 64516
  149.9 55.6 %copy-start = (bf16[128,5376]{1,0:T(8,128)(2,1)S(1)}, bf16[128,5376]{1,0:T(8,128)(2,1)}, u32[]{:S(2)}) copy-start(bf16[128,5376]{1,0:T(8,128)(2,1)} %refs_4_.1) | copy-start | bytes 4128772
  149.9 26.5 %collective-permute-start.10 = (bf16[2,512,256]{2,1,0:T(8,128)(2,1)S(1)}, bf16[2,512,256]{2,1,0:T(8,128)(2,1)S(1)}, u32[]{:S(2)}, u32[]{:S(2)}) collective-permute-start(bf16[2,512,256]{2,1,0:T(8,128)(2,1)S(1)} %pad_maximum_fusion.2.refs_0_), channel_id=1, source_target_pairs={{0,3},{1,0},{2,1},{3,2},{4,7},{5,4},{6,5},{7,6},{8,11},{9,8},{10,9... | collective-permute-start | bytes 1572872 | tf_op jit(solution)/shard_map/ppermute | solution.py:37
  153.7 22.6 %collective-permute-start.11 = (bf16[2,512,256]{2,1,0:T(8,128)(2,1)S(1)}, bf16[2,512,256]{2,1,0:T(8,128)(2,1)S(1)}, u32[]{:S(2)}, u32[]{:S(2)}) collective-permute-start(bf16[2,512,256]{2,1,0:T(8,128)(2,1)S(1)} %pad_maximum_fusion.2.refs_0_), channel_id=1, source_target_pairs={{0,2},{1,3},{2,0},{3,1},{4,6},{5,7},{6,4},{7,5},{8,10},{9,11},{10,... | collective-permute-start | bytes 1572872 | tf_op jit(solution)/shard_map/ppermute | solution.py:37
  153.8 26.1 %collective-permute-start.12 = (bf16[2,512,256]{2,1,0:T(8,128)(2,1)S(1)}, bf16[2,512,256]{2,1,0:T(8,128)(2,1)S(1)}, u32[]{:S(2)}, u32[]{:S(2)}) collective-permute-start(bf16[2,512,256]{2,1,0:T(8,128)(2,1)S(1)} %pad_maximum_fusion.2.refs_0_), channel_id=1, source_target_pairs={{0,1},{1,2},{2,3},{3,0},{4,5},{5,6},{6,7},{7,4},{8,9},{9,10},{10,1... | collective-permute-start | bytes 1572872 | tf_op jit(solution)/shard_map/ppermute | solution.py:37
  179.9 1.8 copy-start.4
  185.6 9.3 %collective-permute-start.14 = (bf16[128,1344]{1,0:T(8,128)(2,1)S(1)}, bf16[128,1344]{1,0:T(8,128)(2,1)S(1)}, u32[]{:S(2)}, u32[]{:S(2)}) collective-permute-start(bf16[128,1344]{1,0:T(8,128)(2,1)S(1)} %get-tuple-element.48), channel_id=1, source_target_pairs={{0,3},{1,0},{2,1},{3,2},{4,7},{5,4},{6,5},{7,6},{8,11},{9,8},{10,9... | collective-permute-start | bytes 1032200 | tf_op jit(solution)/shard_map/ppermute | solution.py:37
  185.9 10.1 %collective-permute-start.15 = (bf16[128,1344]{1,0:T(8,128)(2,1)S(1)}, bf16[128,1344]{1,0:T(8,128)(2,1)S(1)}, u32[]{:S(2)}, u32[]{:S(2)}) collective-permute-start(bf16[128,1344]{1,0:T(8,128)(2,1)S(1)} %get-tuple-element.49), channel_id=1, source_target_pairs={{0,2},{1,3},{2,0},{3,1},{4,6},{5,7},{6,4},{7,5},{8,10},{9,11},{10,... | collective-permute-start | bytes 1032200 | tf_op jit(solution)/shard_map/ppermute | solution.py:37
  186.3 19.1 %collective-permute-start.16 = (bf16[128,1344]{1,0:T(8,128)(2,1)S(1)}, bf16[128,1344]{1,0:T(8,128)(2,1)S(1)}, u32[]{:S(2)}, u32[]{:S(2)}) collective-permute-start(bf16[128,1344]{1,0:T(8,128)(2,1)S(1)} %get-tuple-element.50), channel_id=1, source_target_pairs={{0,1},{1,2},{2,3},{3,0},{4,5},{5,6},{6,7},{7,4},{8,9},{9,10},{10,1... | collective-permute-start | bytes 1032200 | tf_op jit(solution)/shard_map/ppermute | solution.py:37
Sparse Core Ops, SparseCore 0:
  21.7 78.2 all-gather.2
  101.7 47.1 all-gather.4

commit v5 on v4

--- a/solution.py
+++ b/solution.py
@@ -406,9 +406,9 @@
     blocks = [kv_own, kv_other, prev_own, prev_other]
     keep, give = attend(place, [q_own, q_other], blocks, query_offsets, key_offsets)
     other = swap_cores(give)
-    other, own_out = together(other, own_out)
     both = jnp.stack([keep, other])
     attended = [both, shift_x(both, -1), shift_x(both, 2), shift_x(both, 1)]
+    own_out, *attended[1:] = together(own_out, *attended[1:])
     other_out = swap_cores(own_out)
     sums = out_project(place, attended, own_out, other_out)
     sums = [sums[0], shift_x(sums[3], -1), shift_x(sums[2], 2), shift_x(sums[1], 1)]

time: 216 us -> 213 us (0.986); the launches traced: 215 us -> 209 us
  starting transfers between devices: 27.4 us -> 23.9 us
  waiting for transfers between devices: 97.5 us -> 95.1 us
    all_gather x1, waiting for transfers between devices: 7.83 us -> 0.01 us  [shards(): lax.all_gather(part_out, 'ctx', axis=0, tiled=True, axis_index_groups=COL...]
    ppermute x4, waiting for transfers between devices: 2.16 us -> 7.09 us  [swap_cores(): return lax.ppermute(value, 'ctx', ctx_pairs(lambda z, y, c: (z, y, 1 - c)))]
    ppermute x10, starting transfers between devices: 12.2 us -> 9.16 us  [shift_x(): return lax.ppermute(value, 'tp', [(x, (x + steps) % X) for x in range(X)])]
  transfers between devices with their start and end apart: 19 -> 19, of which waited for: 13 -> 14; matrix products, arithmetic and copies ran while one was open for 4% -> 4% of each run, Pallas kernels for 16% -> 17%
where the time goes in v5:
time: 213 us; the launch traced here: 209 us
  waiting for transfers between devices  95.1 us (45%)
  Pallas kernels  41.9 us (20%)
  starting transfers between devices  23.9 us (11%)
  blocking collectives  22.4 us (11%)
  between operations  13.6 us (6%)
  local copies, waits for them, and re-layouts  7.64 us (4%)
  other arithmetic  4.61 us (2%)
    ppermute x10, waiting for transfers between devices, shift_x(): return lax.ppermute(value, 'tp', [(x, (x + steps) % X) for x in range(X)])  64.8 us
    pallas_call x2, Pallas kernels, project(): pl.pallas_call(functools.partial(project_body, mine), in_specs=[SMEM, HBM...  16.3 us
    all_gather x1, waiting for transfers between devices, shards(): lax.all_gather(part, 'ctx', axis=0, tiled=True, axis_index_groups=COLUMNS)  11.9 us
    all_gather x1, blocking collectives, shards(): lax.all_gather(part, 'ctx', axis=0, tiled=True, axis_index_groups=ROWS)  11.4 us
    ppermute x2, waiting for transfers between devices, next_pair(): return lax.ppermute(value, 'ctx', pairs)  11.3 us
    all_gather x1, blocking collectives, shards(): lax.all_gather(part_out, 'ctx', axis=0, tiled=True, axis_index_groups=ROWS)  11 us
    ppermute x4, starting transfers between devices, swap_cores(): return lax.ppermute(value, 'ctx', ctx_pairs(lambda z, y, c: (z, y, 1 - c)))  10.1 us
    ppermute x10, starting transfers between devices, shift_x(): return lax.ppermute(value, 'tp', [(x, (x + steps) % X) for x in range(X)])  9.16 us
  transfers between devices with their start and end apart: 19, of which 14 were waited for; matrix products, arithmetic and copies ran while one was open for 4% of the time, Pallas kernels for 17%

profile of v5, /device:TPU:25, one launch (start us, length us, event | category | flops | bytes accessed | tf_op | source)
XLA Modules:
  0.0 209.2 jit_solution(2841271627005697202)
XLA Ops:
  6.5 0.9 fusion.6
  7.4 0.8 fusion.8
  8.3 0.8 collective-permute-start
  9.0 1.0 collective-permute-done
  10.1 11.4 %all_gather.12 = bf16[672,512]{1,0:T(8,128)(2,1)} all-gather(bf16[168,512]{1,0:T(8,128)(2,1)S(1)} %fusion), channel_id=1, replica_groups={{0,8,16,24},{4,12,20,28},{32,40,48,56},{36,44,52,60},{64,72,80,88},{68,..., dimensions={0}, use_global_device_ids=true | all-gather | bytes 860160 | tf_op jit(solution)/shard_map/all_gather | solution.py:368
  21.6 0.6 reshape.20.gain_ref
  22.2 3.9 %input_norm.1.refs_0_ = bf16[128,5376]{1,0:T(8,128)(2,1)} custom-call(bf16[128,5376]{1,0:T(8,128)(2,1)} %refs_4_.1, f32[1,5376]{1,0:T(1,128)} %reshape.20.gain_ref), custom_call_target="tpu_custom_call" | custom-call | tf_op jit(solution)/shard_map/input_norm/pallas_call | solution.py:79
  26.1 1.2 collective-permute-start.1
  27.3 1.5 collective-permute-start.2
  28.7 1.2 slice.62
  30.0 1.5 fusion.5
  31.5 1.9 fusion.1
  33.5 0.7 collective-permute-start.3
  34.1 0.3 pad_maximum_fusion
  34.5 11.0 %all_gather.13 = bf16[672,256]{1,0:T(8,128)(2,1)} all-gather(bf16[168,256]{1,0:T(8,128)(2,1)S(1)} %collective-permute-done.3), channel_id=1, replica_groups={{0,8,16,24},{4,12,20,28},{32,40,48,56},{36,44,52,60},{64,72,80,88},{68,..., dimensions={0}, use_global_device_ids=true | all-gather | bytes 430080 | tf_op jit(solution)/shard_map/all_gather | solution.py:388
  45.5 11.5 %collective-permute-done.1.refs_4_ = bf16[128,5376]{1,0:T(8,128)(2,1)S(1)} collective-permute-done((bf16[128,5376]{1,0:T(8,128)(2,1)}, bf16[128,5376]{1,0:T(8,128)(2,1)S(1)}, u32[]{:S(2)}, u32[]{:S(2)}) %collective-permute-start.1) | collective-permute-done | bytes 1376288 | tf_op jit(solution)/shard_map/ppermute | solution.py:37
  57.1 2.3 %collective-permute-start.4 = (bf16[64,5376]{1,0:T(8,128)(2,1)S(1)}, bf16[64,5376]{1,0:T(8,128)(2,1)}, u32[]{:S(2)}, u32[]{:S(2)}) collective-permute-start(bf16[64,5376]{1,0:T(8,128)(2,1)S(1)} %slice.67), channel_id=1, source_target_pairs={{0,1},{1,2},{2,3},{3,0},{4,5},{5,6},{6,7},{7,4},{8,9},{9,10},{10,1... | collective-permute-start | bytes 2064392 | tf_op jit(solution)/shard_map/ppermute | solution.py:37
  59.4 2.0 slice.68
  61.4 1.0 collective-permute-start.5
  62.5 0.6 pad_add_fusion.2.place_ref
  63.1 7.8 %collective-permute-done.4.refs_2_ = bf16[64,5376]{1,0:T(8,128)(2,1)} collective-permute-done((bf16[64,5376]{1,0:T(8,128)(2,1)S(1)}, bf16[64,5376]{1,0:T(8,128)(2,1)}, u32[]{:S(2)}, u32[]{:S(2)}) %collective-permute-start.4) | collective-permute-done | bytes 688160 | tf_op jit(solution)/shard_map/ppermute | solution.py:37
  71.0 1.4 collective-permute-done.5.refs_3_
  72.4 8.3 %place_rows.1.rows_hbm = bf16[512,5376]{1,0:T(8,128)(2,1)} custom-call(s32[4]{0:T(128)} %pad_add_fusion.2.place_ref, bf16[128,5376]{1,0:T(8,128)(2,1)} %input_norm.1.refs_0_, bf16[128,5376]{1,0:T(8,128)(2,1)} %collective-permute-done.2.refs_1_, bf16[64,5376]{1,0:T(8,128)(2,1)} %collective-permute-done.4.refs_2_, ...), custom_call_target="tpu_custom_call" | custom-call | bytes 11534336 | tf_op jit(solution)/shard_map/place_rows/pallas_call | solution.py:177
  80.7 7.3 %collective-permute-start.6 = (bf16[512,5376]{1,0:T(8,128)(2,1)}, bf16[512,5376]{1,0:T(8,128)(2,1)}, u32[]{:S(2)}, u32[]{:S(2)}) collective-permute-start(bf16[512,5376]{1,0:T(8,128)(2,1)} %place_rows.1.rows_hbm), channel_id=1, source_target_pairs={{0,4},{4,0},{8,12},{12,8},{16,20},{20,16},{24,28},{28,24},{32,36},... | collective-permute-start | bytes 16515080 | tf_op jit(solution)/shard_map/ppermute | solution.py:33
  88.0 11.9 %all-gather.3.cloned.1.call-done.weight_ref = bf16[5376,512]{1,0:T(8,128)(2,1)} async-done(((bf16[672,512]{1,0:T(8,128)(2,1)}), bf16[5376,512]{1,0:T(8,128)(2,1)}) %all-gather.3.cloned.1.call-update) | async-done | bytes 5505040 | tf_op jit(solution)/shard_map/all_gather | solution.py:370
  100.0 8.1 %project_own.1 = (bf16[2,512,128]{2,1,0:T(8,128)(2,1)S(1)}, bf16[2,512,128]{2,1,0:T(8,128)(2,1)S(1)}) custom-call(s32[4]{0:T(128)S(1)} %copy-done.1, bf16[512,5376]{1,0:T(8,128)(2,1)} %place_rows.1.rows_hbm, bf16[5376,512]{1,0:T(8,128)(2,1)} %all-gather.3.cloned.1.call-done.weight_ref, f32[1,128]{1,0:T(1,128)S(1)} %bitcast.12, f32[1,128]{1,0:T(1,128)S(1)} %bitcast.14, ...), custom_call_target="tpu_custom_call" | custom-call | flops 2818572288 | bytes 12582912 | tf_op jit(solution)/shard_map/project_own/pallas_call | solution.py:146
  108.1 1.9 collective-permute-start.7
  110.0 8.2 %project_other.1 = (bf16[2,512,128]{2,1,0:T(8,128)(2,1)S(1)}, bf16[2,512,128]{2,1,0:T(8,128)(2,1)S(1)}) custom-call(s32[4]{0:T(128)S(1)} %copy-done.1, bf16[512,5376]{1,0:T(8,128)(2,1)} %collective-permute-done.6.rows_hbm, bf16[5376,512]{1,0:T(8,128)(2,1)} %all-gather.3.cloned.1.call-done.weight_ref, f32[1,128]{1,0:T(1,128)S(1)} %bitcast.13, ...), custom_call_target="tpu_custom_call" | custom-call | flops 2818572288 | bytes 12582912 | tf_op jit(solution)/shard_map/project_other/pallas_call | solution.py:146
  118.3 2.1 %collective-permute-start.8 = (bf16[2,512,128]{2,1,0:T(8,128)(2,1)S(1)}, bf16[2,512,128]{2,1,0:T(8,128)(2,1)S(1)}, u32[]{:S(2)}, u32[]{:S(2)}) collective-permute-start(bf16[2,512,128]{2,1,0:T(8,128)(2,1)S(1)} %get-tuple-element.41.other_ref), channel_id=1, source_target_pairs={{0,8},{4,12},{8,16},{12,20},{16,24},{20,28},{24,32},{28,36},{32,40... | collective-permute-start | bytes 786440 | tf_op jit(solution)/shard_map/ppermute | solution.py:42
  120.6 11.3 %collective-permute-done.8.pother_ref = bf16[2,512,128]{2,1,0:T(8,128)(2,1)S(1)} collective-permute-done((bf16[2,512,128]{2,1,0:T(8,128)(2,1)S(1)}, bf16[2,512,128]{2,1,0:T(8,128)(2,1)S(1)}, u32[]{:S(2)}, u32[]{:S(2)}) %collective-permute-start.8) | collective-permute-done | bytes 262176 | tf_op jit(solution)/shard_map/ppermute | solution.py:42
  131.9 6.5 %attend.1 = (bf16[512,256]{1,0:T(8,128)(2,1)S(1)}, bf16[512,256]{1,0:T(8,128)(2,1)S(1)}) custom-call(s32[4]{0:T(128)S(1)} %copy-done.1, bf16[2,512,128]{2,1,0:T(8,128)(2,1)S(1)} %get-tuple-element.38.qmine_ref, bf16[2,512,128]{2,1,0:T(8,128)(2,1)S(1)} %get-tuple-element.39.qother_ref, bf16[2,512,128]{2,1,0:T(8,128)(2,1)S(1)} %get-tuple-element.40.mine_ref, ...), custom_call_target="tpu_custom_call" | custom-call | flops 1342177280 | bytes 3145728 | tf_op jit(solution)/shard_map/attend/pallas_call | solution.py:237
  138.4 1.5 collective-permute-start.9
  139.9 1.2 collective-permute-done.9
  141.2 0.8 collective-permute-start.11
  142.0 0.7 collective-permute-start.12
  142.7 11.7 %collective-permute-done.10.refs_1_ = bf16[2,512,256]{2,1,0:T(8,128)(2,1)S(1)} collective-permute-done((bf16[2,512,256]{2,1,0:T(8,128)(2,1)S(1)}, bf16[2,512,256]{2,1,0:T(8,128)(2,1)S(1)}, u32[]{:S(2)}, u32[]{:S(2)}) %collective-permute-start.10) | collective-permute-done | bytes 524320 | tf_op jit(solution)/shard_map/ppermute | solution.py:37
  154.3 1.6 collective-permute-done.11.refs_2_
  156.0 11.9 %collective-permute-done.12.refs_3_ = bf16[2,512,256]{2,1,0:T(8,128)(2,1)S(1)} collective-permute-done((bf16[2,512,256]{2,1,0:T(8,128)(2,1)S(1)}, bf16[2,512,256]{2,1,0:T(8,128)(2,1)S(1)}, u32[]{:S(2)}, u32[]{:S(2)}) %collective-permute-start.12) | collective-permute-done | bytes 524320 | tf_op jit(solution)/shard_map/ppermute | solution.py:37
  167.9 0.5 collective-permute-start.13
  168.4 4.9 %collective-permute-done.13.refs_5_ = bf16[5376,256]{1,0:T(8,128)(2,1)S(1)} collective-permute-done((bf16[5376,256]{1,0:T(8,128)(2,1)}, bf16[5376,256]{1,0:T(8,128)(2,1)S(1)}, u32[]{:S(2)}, u32[]{:S(2)}) %collective-permute-start.13) | collective-permute-done | bytes 2752544 | tf_op jit(solution)/shard_map/ppermute | solution.py:33
  173.3 1.8 copy-done.4
  175.1 4.0 %out_project.1 = (bf16[128,1344]{1,0:T(8,128)(2,1)S(1)}, bf16[128,1344]{1,0:T(8,128)(2,1)S(1)}, bf16[128,1344]{1,0:T(8,128)(2,1)S(1)}, bf16[128,1344]{1,0:T(8,128)(2,1)S(1)}) custom-call(s32[4]{0:T(128)S(1)} %copy-done.1, bf16[2,512,256]{2,1,0:T(8,128)(2,1)S(1)} %pad_maximum_fusion.2.refs_0_, bf16[2,512,256]{2,1,0:T(8,128)(2,1)S(1)} %collective-permute-done.10.refs_1_, ...), custom_call_target="tpu_custom_call" | custom-call | flops 2818572288 | bytes 9437184 | tf_op jit(solution)/shard_map/out_project/pallas_call | solution.py:283
  179.1 0.9 collective-permute-start.14
  180.2 0.5 collective-permute-start.16
  180.7 8.0 %collective-permute-done.14.refs_1_ = bf16[128,1344]{1,0:T(8,128)(2,1)S(1)} collective-permute-done((bf16[128,1344]{1,0:T(8,128)(2,1)S(1)}, bf16[128,1344]{1,0:T(8,128)(2,1)S(1)}, u32[]{:S(2)}, u32[]{:S(2)}) %collective-permute-start.14) | collective-permute-done | bytes 344096 | tf_op jit(solution)/shard_map/ppermute | solution.py:37
  188.8 2.0 collective-permute-done.15.refs_2_
  190.8 8.7 %collective-permute-done.16.refs_3_ = bf16[128,1344]{1,0:T(8,128)(2,1)S(1)} collective-permute-done((bf16[128,1344]{1,0:T(8,128)(2,1)S(1)}, bf16[128,1344]{1,0:T(8,128)(2,1)S(1)}, u32[]{:S(2)}, u32[]{:S(2)}) %collective-permute-start.16) | collective-permute-done | bytes 344096 | tf_op jit(solution)/shard_map/ppermute | solution.py:37
  199.5 2.9 %final_norm.1 = bf16[128,5376]{1,0:T(8,128)(2,1)} custom-call(s32[4]{0:T(128)S(1)} %copy-done.1, bf16[128,1344]{1,0:T(8,128)(2,1)S(1)} %get-tuple-element.51.refs_0_, bf16[128,1344]{1,0:T(8,128)(2,1)S(1)} %collective-permute-done.14.refs_1_, bf16[128,1344]{1,0:T(8,128)(2,1)S(1)} %collective-permute-done.15.refs_2_, ...), custom_call_target="tpu_custom_call" | custom-call | tf_op jit(solution)/shard_map/final_norm/pallas_call | solution.py:316
  (41 shorter events, 1.0 us)
Async XLA Ops:
  6.5 15.1 %copy-start.6 = (f32[5376]{0:T(1024)S(1)}, f32[5376]{0:T(1024)}, u32[]{:S(2)}) copy-start(f32[5376]{0:T(1024)} %param.16) | copy-start | bytes 64516
  6.5 93.4 %all-gather.3.cloned.1.call-start = ((), (), s32[]{:S(2)}) async-start(), calls=%async_computation | async-start | bytes 6193152 | tf_op jit(solution)/shard_map/all_gather | solution.py:370
  8.3 1.8 collective-permute-start
  21.5 146.3 %all-gather.5.cloned.1.call-start = ((), (), s32[]{:S(2)}) async-start(), calls=%async_computation.1 | async-start | bytes 3096576 | tf_op jit(solution)/shard_map/all_gather | solution.py:401
  26.1 31.0 %collective-permute-start.1 = (bf16[128,5376]{1,0:T(8,128)(2,1)}, bf16[128,5376]{1,0:T(8,128)(2,1)S(1)}, u32[]{:S(2)}, u32[]{:S(2)}) collective-permute-start(bf16[128,5376]{1,0:T(8,128)(2,1)} %input_norm.1.refs_0_), channel_id=1, source_target_pairs={{0,1},{1,2},{2,3},{3,0},{4,5},{5,6},{6,7},{7,4},{8,9},{9,10},{10,1... | collective-permute-start | bytes 4128776 | tf_op jit(solution)/shard_map/ppermute | solution.py:37
  27.3 29.8 %collective-permute-start.2 = (bf16[128,5376]{1,0:T(8,128)(2,1)}, bf16[128,5376]{1,0:T(8,128)(2,1)}, u32[]{:S(2)}, u32[]{:S(2)}) collective-permute-start(bf16[128,5376]{1,0:T(8,128)(2,1)} %input_norm.1.refs_0_), channel_id=1, source_target_pairs={{0,3},{1,0},{2,1},{3,2},{4,7},{5,4},{6,5},{7,6},{8,11},{9,8},{10,9... | collective-permute-start | bytes 4128776 | tf_op jit(solution)/shard_map/ppermute | solution.py:37
  33.5 1.0 collective-permute-start.3
  57.1 15.3 %copy-start.5 = (bf16[128,5376]{1,0:T(8,128)(2,1)}, bf16[128,5376]{1,0:T(8,128)(2,1)S(1)}, u32[]{:S(2)}) copy-start(bf16[128,5376]{1,0:T(8,128)(2,1)S(1)} %collective-permute-done.1.refs_4_) | copy-start | bytes 4128772
  57.1 13.8 %collective-permute-start.4 = (bf16[64,5376]{1,0:T(8,128)(2,1)S(1)}, bf16[64,5376]{1,0:T(8,128)(2,1)}, u32[]{:S(2)}, u32[]{:S(2)}) collective-permute-start(bf16[64,5376]{1,0:T(8,128)(2,1)S(1)} %slice.67), channel_id=1, source_target_pairs={{0,1},{1,2},{2,3},{3,0},{4,5},{5,6},{6,7},{7,4},{8,9},{9,10},{10,1... | collective-permute-start | bytes 2064392 | tf_op jit(solution)/shard_map/ppermute | solution.py:37
  61.4 10.9 %collective-permute-start.5 = (bf16[64,5376]{1,0:T(8,128)(2,1)}, bf16[64,5376]{1,0:T(8,128)(2,1)}, u32[]{:S(2)}, u32[]{:S(2)}) collective-permute-start(bf16[64,5376]{1,0:T(8,128)(2,1)} %slice.68), channel_id=1, source_target_pairs={{0,3},{1,0},{2,1},{3,2},{4,7},{5,4},{6,5},{7,6},{8,11},{9,8},{10,9... | collective-permute-start | bytes 2064392 | tf_op jit(solution)/shard_map/ppermute | solution.py:37
  63.1 36.8 %copy-start.1 = (s32[4]{0:T(128)S(1)}, s32[4]{0:T(128)}, u32[]{:S(2)}) copy-start(s32[4]{0:T(128)} %pad_add_fusion.2.place_ref) | copy-start | bytes 52
  63.1 36.8 %copy-start.2 = (f32[128]{0:T(128)S(1)}, f32[128]{0:T(128)}, u32[]{:S(2)}) copy-start(f32[128]{0:T(128)} %param.17) | copy-start | bytes 1540
  63.1 36.8 %copy-start.3 = (f32[128]{0:T(128)S(1)}, f32[128]{0:T(128)}, u32[]{:S(2)}) copy-start(f32[128]{0:T(128)} %param.18) | copy-start | bytes 1540
  80.7 29.3 %collective-permute-start.6 = (bf16[512,5376]{1,0:T(8,128)(2,1)}, bf16[512,5376]{1,0:T(8,128)(2,1)}, u32[]{:S(2)}, u32[]{:S(2)}) collective-permute-start(bf16[512,5376]{1,0:T(8,128)(2,1)} %place_rows.1.rows_hbm), channel_id=1, source_target_pairs={{0,4},{4,0},{8,12},{12,8},{16,20},{20,16},{24,28},{28,24},{32,36},... | collective-permute-start | bytes 16515080 | tf_op jit(solution)/shard_map/ppermute | solution.py:33
  108.1 12.5 %collective-permute-start.7 = (bf16[2,512,128]{2,1,0:T(8,128)(2,1)S(1)}, bf16[2,512,128]{2,1,0:T(8,128)(2,1)S(1)}, u32[]{:S(2)}, u32[]{:S(2)}) collective-permute-start(bf16[2,512,128]{2,1,0:T(8,128)(2,1)S(1)} %get-tuple-element.40.mine_ref), channel_id=1, source_target_pairs={{0,8},{4,12},{8,16},{12,20},{16,24},{20,28},{24,32},{28,36},{32,40... | collective-permute-start | bytes 786440 | tf_op jit(solution)/shard_map/ppermute | solution.py:42
  118.3 13.6 %collective-permute-start.8 = (bf16[2,512,128]{2,1,0:T(8,128)(2,1)S(1)}, bf16[2,512,128]{2,1,0:T(8,128)(2,1)S(1)}, u32[]{:S(2)}, u32[]{:S(2)}) collective-permute-start(bf16[2,512,128]{2,1,0:T(8,128)(2,1)S(1)} %get-tuple-element.41.other_ref), channel_id=1, source_target_pairs={{0,8},{4,12},{8,16},{12,20},{16,24},{20,28},{24,32},{28,36},{32,40... | collective-permute-start | bytes 786440 | tf_op jit(solution)/shard_map/ppermute | solution.py:42
  138.4 2.7 %collective-permute-start.9 = (bf16[512,256]{1,0:T(8,128)(2,1)S(1)}, bf16[512,256]{1,0:T(8,128)(2,1)S(1)}, u32[]{:S(2)}, u32[]{:S(2)}) collective-permute-start(bf16[512,256]{1,0:T(8,128)(2,1)S(1)} %get-tuple-element.45), channel_id=1, source_target_pairs={{0,4},{4,0},{8,12},{12,8},{16,20},{20,16},{24,28},{28,24},{32,36},... | collective-permute-start | bytes 786440 | tf_op jit(solution)/shard_map/ppermute | solution.py:33
  141.0 39.7 %copy-start.7 = (f32[5376]{0:T(1024)S(1)}, f32[5376]{0:T(1024)}, u32[]{:S(2)}) copy-start(f32[5376]{0:T(1024)} %param.19) | copy-start | bytes 64516
  141.1 58.4 %copy-start = (bf16[128,5376]{1,0:T(8,128)(2,1)S(1)}, bf16[128,5376]{1,0:T(8,128)(2,1)}, u32[]{:S(2)}) copy-start(bf16[128,5376]{1,0:T(8,128)(2,1)} %refs_4_.1) | copy-start | bytes 4128772
  141.1 13.2 %collective-permute-start.10 = (bf16[2,512,256]{2,1,0:T(8,128)(2,1)S(1)}, bf16[2,512,256]{2,1,0:T(8,128)(2,1)S(1)}, u32[]{:S(2)}, u32[]{:S(2)}) collective-permute-start(bf16[2,512,256]{2,1,0:T(8,128)(2,1)S(1)} %pad_maximum_fusion.2.refs_0_), channel_id=1, source_target_pairs={{0,3},{1,0},{2,1},{3,2},{4,7},{5,4},{6,5},{7,6},{8,11},{9,8},{10,9... | collective-permute-start | bytes 1572872 | tf_op jit(solution)/shard_map/ppermute | solution.py:37
  141.2 14.8 %collective-permute-start.11 = (bf16[2,512,256]{2,1,0:T(8,128)(2,1)S(1)}, bf16[2,512,256]{2,1,0:T(8,128)(2,1)S(1)}, u32[]{:S(2)}, u32[]{:S(2)}) collective-permute-start(bf16[2,512,256]{2,1,0:T(8,128)(2,1)S(1)} %pad_maximum_fusion.2.refs_0_), channel_id=1, source_target_pairs={{0,2},{1,3},{2,0},{3,1},{4,6},{5,7},{6,4},{7,5},{8,10},{9,11},{10,... | collective-permute-start | bytes 1572872 | tf_op jit(solution)/shard_map/ppermute | solution.py:37
  142.0 25.9 %collective-permute-start.12 = (bf16[2,512,256]{2,1,0:T(8,128)(2,1)S(1)}, bf16[2,512,256]{2,1,0:T(8,128)(2,1)S(1)}, u32[]{:S(2)}, u32[]{:S(2)}) collective-permute-start(bf16[2,512,256]{2,1,0:T(8,128)(2,1)S(1)} %pad_maximum_fusion.2.refs_0_), channel_id=1, source_target_pairs={{0,1},{1,2},{2,3},{3,0},{4,5},{5,6},{6,7},{7,4},{8,9},{9,10},{10,1... | collective-permute-start | bytes 1572872 | tf_op jit(solution)/shard_map/ppermute | solution.py:37
  167.9 5.4 %collective-permute-start.13 = (bf16[5376,256]{1,0:T(8,128)(2,1)}, bf16[5376,256]{1,0:T(8,128)(2,1)S(1)}, u32[]{:S(2)}, u32[]{:S(2)}) collective-permute-start(bf16[5376,256]{1,0:T(8,128)(2,1)} %all-gather.5.cloned.1.call-done.refs_4_), channel_id=1, source_target_pairs={{0,4},{4,0},{8,12},{12,8},{16,20},{20,16},{24,28},{28,24},{32,36},... | collective-permute-start | bytes 8257544 | tf_op jit(solution)/shard_map/ppermute | solution.py:33
  173.3 1.8 copy-start.4
  179.1 9.7 %collective-permute-start.14 = (bf16[128,1344]{1,0:T(8,128)(2,1)S(1)}, bf16[128,1344]{1,0:T(8,128)(2,1)S(1)}, u32[]{:S(2)}, u32[]{:S(2)}) collective-permute-start(bf16[128,1344]{1,0:T(8,128)(2,1)S(1)} %get-tuple-element.52), channel_id=1, source_target_pairs={{0,3},{1,0},{2,1},{3,2},{4,7},{5,4},{6,5},{7,6},{8,11},{9,8},{10,9... | collective-permute-start | bytes 1032200 | tf_op jit(solution)/shard_map/ppermute | solution.py:37
  179.9 10.8 %collective-permute-start.15 = (bf16[128,1344]{1,0:T(8,128)(2,1)S(1)}, bf16[128,1344]{1,0:T(8,128)(2,1)S(1)}, u32[]{:S(2)}, u32[]{:S(2)}) collective-permute-start(bf16[128,1344]{1,0:T(8,128)(2,1)S(1)} %get-tuple-element.53), channel_id=1, source_target_pairs={{0,2},{1,3},{2,0},{3,1},{4,6},{5,7},{6,4},{7,5},{8,10},{9,11},{10,... | collective-permute-start | bytes 1032200 | tf_op jit(solution)/shard_map/ppermute | solution.py:37
  180.2 19.3 %collective-permute-start.16 = (bf16[128,1344]{1,0:T(8,128)(2,1)S(1)}, bf16[128,1344]{1,0:T(8,128)(2,1)S(1)}, u32[]{:S(2)}, u32[]{:S(2)}) collective-permute-start(bf16[128,1344]{1,0:T(8,128)(2,1)S(1)} %get-tuple-element.54), channel_id=1, source_target_pairs={{0,1},{1,2},{2,3},{3,0},{4,5},{5,6},{6,7},{7,4},{8,9},{9,10},{10,1... | collective-permute-start | bytes 1032200 | tf_op jit(solution)/shard_map/ppermute | solution.py:37
Sparse Core Ops, SparseCore 0:
  21.7 78.2 all-gather.2
  101.7 47.1 all-gather.4

commit v6 on v5

--- a/solution.py
+++ b/solution.py
@@ -188,7 +188,7 @@
     )(place, *pieces)
 
 
-TILE = 256
+TILE = 128
 SPAN = PAIR + TILE
 
 

time: 213 us -> 214 us (level)
  no operation moved by 1% of the time
where the time goes in v6:
time: 214 us; the launch traced here: 211 us
  waiting for transfers between devices  95 us (44%)
  Pallas kernels  43 us (20%)
  starting transfers between devices  24.2 us (11%)
  blocking collectives  22.4 us (10%)
  between operations  13.7 us (6%)
  local copies, waits for them, and re-layouts  7.73 us (4%)
  other arithmetic  4.59 us (2%)
    ppermute x10, waiting for transfers between devices, shift_x(): return lax.ppermute(value, 'tp', [(x, (x + steps) % X) for x in range(X)])  64.7 us
    pallas_call x2, Pallas kernels, project(): pl.pallas_call(functools.partial(project_body, mine), in_specs=[SMEM, HBM...  16.3 us
    all_gather x1, waiting for transfers between devices, shards(): lax.all_gather(part, 'ctx', axis=0, tiled=True, axis_index_groups=COLUMNS)  12 us
    all_gather x1, blocking collectives, shards(): lax.all_gather(part, 'ctx', axis=0, tiled=True, axis_index_groups=ROWS)  11.4 us
    ppermute x2, waiting for transfers between devices, next_pair(): return lax.ppermute(value, 'ctx', pairs)  11.3 us
    all_gather x1, blocking collectives, shards(): lax.all_gather(part_out, 'ctx', axis=0, tiled=True, axis_index_groups=ROWS)  11 us
    ppermute x4, starting transfers between devices, swap_cores(): return lax.ppermute(value, 'ctx', ctx_pairs(lambda z, y, c: (z, y, 1 - c)))  10.2 us
    ppermute x10, starting transfers between devices, shift_x(): return lax.ppermute(value, 'tp', [(x, (x + steps) % X) for x in range(X)])  9.3 us
  transfers between devices with their start and end apart: 19, of which 14 were waited for; matrix products, arithmetic and copies ran while one was open for 4% of the time, Pallas kernels for 17%

profile of v6, /device:TPU:25, one launch (start us, length us, event | category | flops | bytes accessed | tf_op | source)
XLA Modules:
  0.0 210.7 jit_solution(12567353225783114114)
XLA Ops:
  6.5 0.9 fusion.10
  7.4 0.8 fusion.12
  8.3 0.8 collective-permute-start
  9.0 1.0 collective-permute-done
  10.1 11.4 %all_gather.12 = bf16[672,512]{1,0:T(8,128)(2,1)} all-gather(bf16[168,512]{1,0:T(8,128)(2,1)S(1)} %fusion), channel_id=1, replica_groups={{0,8,16,24},{4,12,20,28},{32,40,48,56},{36,44,52,60},{64,72,80,88},{68,..., dimensions={0}, use_global_device_ids=true | all-gather | bytes 860160 | tf_op jit(solution)/shard_map/all_gather | solution.py:368
  21.6 0.6 reshape.20.gain_ref
  22.2 3.9 %input_norm.1.refs_0_ = bf16[128,5376]{1,0:T(8,128)(2,1)} custom-call(bf16[128,5376]{1,0:T(8,128)(2,1)} %refs_4_.1, f32[1,5376]{1,0:T(1,128)} %reshape.20.gain_ref), custom_call_target="tpu_custom_call" | custom-call | tf_op jit(solution)/shard_map/input_norm/pallas_call | solution.py:79
  26.1 1.2 collective-permute-start.1
  27.3 1.5 collective-permute-start.2
  28.7 1.2 slice.74
  30.0 1.5 fusion.9
  31.6 1.9 fusion.1
  33.6 0.7 collective-permute-start.3
  34.2 0.3 pad_maximum_fusion
  34.6 11.0 %all_gather.13 = bf16[672,256]{1,0:T(8,128)(2,1)} all-gather(bf16[168,256]{1,0:T(8,128)(2,1)S(1)} %collective-permute-done.3), channel_id=1, replica_groups={{0,8,16,24},{4,12,20,28},{32,40,48,56},{36,44,52,60},{64,72,80,88},{68,..., dimensions={0}, use_global_device_ids=true | all-gather | bytes 430080 | tf_op jit(solution)/shard_map/all_gather | solution.py:388
  45.6 11.4 %collective-permute-done.1.refs_4_ = bf16[128,5376]{1,0:T(8,128)(2,1)S(1)} collective-permute-done((bf16[128,5376]{1,0:T(8,128)(2,1)}, bf16[128,5376]{1,0:T(8,128)(2,1)S(1)}, u32[]{:S(2)}, u32[]{:S(2)}) %collective-permute-start.1) | collective-permute-done | bytes 1376288 | tf_op jit(solution)/shard_map/ppermute | solution.py:37
  57.1 2.3 %collective-permute-start.4 = (bf16[64,5376]{1,0:T(8,128)(2,1)S(1)}, bf16[64,5376]{1,0:T(8,128)(2,1)}, u32[]{:S(2)}, u32[]{:S(2)}) collective-permute-start(bf16[64,5376]{1,0:T(8,128)(2,1)S(1)} %slice.83), channel_id=1, source_target_pairs={{0,1},{1,2},{2,3},{3,0},{4,5},{5,6},{6,7},{7,4},{8,9},{9,10},{10,1... | collective-permute-start | bytes 2064392 | tf_op jit(solution)/shard_map/ppermute | solution.py:37
  59.4 2.0 slice.84
  61.4 1.0 collective-permute-start.5
  62.5 0.6 pad_add_fusion.1.place_ref
  63.1 7.8 %collective-permute-done.4.refs_2_ = bf16[64,5376]{1,0:T(8,128)(2,1)} collective-permute-done((bf16[64,5376]{1,0:T(8,128)(2,1)S(1)}, bf16[64,5376]{1,0:T(8,128)(2,1)}, u32[]{:S(2)}, u32[]{:S(2)}) %collective-permute-start.4) | collective-permute-done | bytes 688160 | tf_op jit(solution)/shard_map/ppermute | solution.py:37
  71.0 1.3 collective-permute-done.5.refs_3_
  72.3 8.4 %place_rows.1.rows_hbm = bf16[512,5376]{1,0:T(8,128)(2,1)} custom-call(s32[4]{0:T(128)} %pad_add_fusion.1.place_ref, bf16[128,5376]{1,0:T(8,128)(2,1)} %input_norm.1.refs_0_, bf16[128,5376]{1,0:T(8,128)(2,1)} %collective-permute-done.2.refs_1_, bf16[64,5376]{1,0:T(8,128)(2,1)} %collective-permute-done.4.refs_2_, ...), custom_call_target="tpu_custom_call" | custom-call | bytes 11534336 | tf_op jit(solution)/shard_map/place_rows/pallas_call | solution.py:177
  80.6 7.3 %collective-permute-start.6 = (bf16[512,5376]{1,0:T(8,128)(2,1)}, bf16[512,5376]{1,0:T(8,128)(2,1)}, u32[]{:S(2)}, u32[]{:S(2)}) collective-permute-start(bf16[512,5376]{1,0:T(8,128)(2,1)} %place_rows.1.rows_hbm), channel_id=1, source_target_pairs={{0,4},{4,0},{8,12},{12,8},{16,20},{20,16},{24,28},{28,24},{32,36},... | collective-permute-start | bytes 16515080 | tf_op jit(solution)/shard_map/ppermute | solution.py:33
  88.0 12.0 %all-gather.3.cloned.1.call-done.weight_ref = bf16[5376,512]{1,0:T(8,128)(2,1)} async-done(((bf16[672,512]{1,0:T(8,128)(2,1)}), bf16[5376,512]{1,0:T(8,128)(2,1)}) %all-gather.3.cloned.1.call-update) | async-done | bytes 5505040 | tf_op jit(solution)/shard_map/all_gather | solution.py:370
  100.0 8.1 %project_own.1 = (bf16[2,512,128]{2,1,0:T(8,128)(2,1)S(1)}, bf16[2,512,128]{2,1,0:T(8,128)(2,1)S(1)}) custom-call(s32[4]{0:T(128)S(1)} %copy-done.1, bf16[512,5376]{1,0:T(8,128)(2,1)} %place_rows.1.rows_hbm, bf16[5376,512]{1,0:T(8,128)(2,1)} %all-gather.3.cloned.1.call-done.weight_ref, f32[1,128]{1,0:T(1,128)S(1)} %bitcast.12, f32[1,128]{1,0:T(1,128)S(1)} %bitcast.14, ...), custom_call_target="tpu_custom_call" | custom-call | flops 2818572288 | bytes 12582912 | tf_op jit(solution)/shard_map/project_own/pallas_call | solution.py:146
  108.2 1.9 collective-permute-start.7
  110.1 8.2 %project_other.1 = (bf16[2,512,128]{2,1,0:T(8,128)(2,1)S(1)}, bf16[2,512,128]{2,1,0:T(8,128)(2,1)S(1)}) custom-call(s32[4]{0:T(128)S(1)} %copy-done.1, bf16[512,5376]{1,0:T(8,128)(2,1)} %collective-permute-done.6.rows_hbm, bf16[5376,512]{1,0:T(8,128)(2,1)} %all-gather.3.cloned.1.call-done.weight_ref, f32[1,128]{1,0:T(1,128)S(1)} %bitcast.13, ...), custom_call_target="tpu_custom_call" | custom-call | flops 2818572288 | bytes 12582912 | tf_op jit(solution)/shard_map/project_other/pallas_call | solution.py:146
  118.3 2.1 collective-permute-start.8
  120.7 11.3 %collective-permute-done.8.pother_ref = bf16[2,512,128]{2,1,0:T(8,128)(2,1)S(1)} collective-permute-done((bf16[2,512,128]{2,1,0:T(8,128)(2,1)S(1)}, bf16[2,512,128]{2,1,0:T(8,128)(2,1)S(1)}, u32[]{:S(2)}, u32[]{:S(2)}) %collective-permute-start.8) | collective-permute-done | bytes 262176 | tf_op jit(solution)/shard_map/ppermute | solution.py:42
  132.0 7.5 %attend.1 = (bf16[512,256]{1,0:T(8,128)(2,1)S(1)}, bf16[512,256]{1,0:T(8,128)(2,1)S(1)}) custom-call(s32[4]{0:T(128)S(1)} %copy-done.1, bf16[2,512,128]{2,1,0:T(8,128)(2,1)S(1)} %get-tuple-element.38.qmine_ref, bf16[2,512,128]{2,1,0:T(8,128)(2,1)S(1)} %get-tuple-element.39.qother_ref, bf16[2,512,128]{2,1,0:T(8,128)(2,1)S(1)} %get-tuple-element.40.mine_ref, ...), custom_call_target="tpu_custom_call" | custom-call | flops 1207959552 | bytes 3145728 | tf_op jit(solution)/shard_map/attend/pallas_call | solution.py:237
  139.5 1.6 collective-permute-start.9
  141.1 1.2 collective-permute-done.9
  142.4 0.6 collective-permute-start.11
  143.0 0.8 collective-permute-start.12
  143.9 11.7 %collective-permute-done.10.refs_1_ = bf16[2,512,256]{2,1,0:T(8,128)(2,1)S(1)} collective-permute-done((bf16[2,512,256]{2,1,0:T(8,128)(2,1)S(1)}, bf16[2,512,256]{2,1,0:T(8,128)(2,1)S(1)}, u32[]{:S(2)}, u32[]{:S(2)}) %collective-permute-start.10) | collective-permute-done | bytes 524320 | tf_op jit(solution)/shard_map/ppermute | solution.py:37
  155.5 1.6 collective-permute-done.11.refs_2_
  157.2 11.9 %collective-permute-done.12.refs_3_ = bf16[2,512,256]{2,1,0:T(8,128)(2,1)S(1)} collective-permute-done((bf16[2,512,256]{2,1,0:T(8,128)(2,1)S(1)}, bf16[2,512,256]{2,1,0:T(8,128)(2,1)S(1)}, u32[]{:S(2)}, u32[]{:S(2)}) %collective-permute-start.12) | collective-permute-done | bytes 524320 | tf_op jit(solution)/shard_map/ppermute | solution.py:37
  169.1 0.5 collective-permute-start.13
  169.6 4.9 %collective-permute-done.13.refs_5_ = bf16[5376,256]{1,0:T(8,128)(2,1)S(1)} collective-permute-done((bf16[5376,256]{1,0:T(8,128)(2,1)}, bf16[5376,256]{1,0:T(8,128)(2,1)S(1)}, u32[]{:S(2)}, u32[]{:S(2)}) %collective-permute-start.13) | collective-permute-done | bytes 2752544 | tf_op jit(solution)/shard_map/ppermute | solution.py:33
  174.5 1.8 copy-done.4
  176.3 4.0 %out_project.1 = (bf16[128,1344]{1,0:T(8,128)(2,1)S(1)}, bf16[128,1344]{1,0:T(8,128)(2,1)S(1)}, bf16[128,1344]{1,0:T(8,128)(2,1)S(1)}, bf16[128,1344]{1,0:T(8,128)(2,1)S(1)}) custom-call(s32[4]{0:T(128)S(1)} %copy-done.1, bf16[2,512,256]{2,1,0:T(8,128)(2,1)S(1)} %pad_maximum_fusion.2.refs_0_, bf16[2,512,256]{2,1,0:T(8,128)(2,1)S(1)} %collective-permute-done.10.refs_1_, ...), custom_call_target="tpu_custom_call" | custom-call | flops 2818572288 | bytes 9437184 | tf_op jit(solution)/shard_map/out_project/pallas_call | solution.py:283
  180.3 1.1 collective-permute-start.14
  181.4 0.6 collective-permute-start.16
  182.1 8.1 %collective-permute-done.14.refs_1_ = bf16[128,1344]{1,0:T(8,128)(2,1)S(1)} collective-permute-done((bf16[128,1344]{1,0:T(8,128)(2,1)S(1)}, bf16[128,1344]{1,0:T(8,128)(2,1)S(1)}, u32[]{:S(2)}, u32[]{:S(2)}) %collective-permute-start.14) | collective-permute-done | bytes 344096 | tf_op jit(solution)/shard_map/ppermute | solution.py:37
  190.2 2.0 collective-permute-done.15.refs_2_
  192.2 8.7 %collective-permute-done.16.refs_3_ = bf16[128,1344]{1,0:T(8,128)(2,1)S(1)} collective-permute-done((bf16[128,1344]{1,0:T(8,128)(2,1)S(1)}, bf16[128,1344]{1,0:T(8,128)(2,1)S(1)}, u32[]{:S(2)}, u32[]{:S(2)}) %collective-permute-start.16) | collective-permute-done | bytes 344096 | tf_op jit(solution)/shard_map/ppermute | solution.py:37
  200.9 2.9 %final_norm.1 = bf16[128,5376]{1,0:T(8,128)(2,1)} custom-call(s32[4]{0:T(128)S(1)} %copy-done.1, bf16[128,1344]{1,0:T(8,128)(2,1)S(1)} %get-tuple-element.51.refs_0_, bf16[128,1344]{1,0:T(8,128)(2,1)S(1)} %collective-permute-done.14.refs_1_, bf16[128,1344]{1,0:T(8,128)(2,1)S(1)} %collective-permute-done.15.refs_2_, ...), custom_call_target="tpu_custom_call" | custom-call | tf_op jit(solution)/shard_map/final_norm/pallas_call | solution.py:316
  (45 shorter events, 0.9 us)
Async XLA Ops:
  6.5 15.1 %copy-start.6 = (f32[5376]{0:T(1024)S(1)}, f32[5376]{0:T(1024)}, u32[]{:S(2)}) copy-start(f32[5376]{0:T(1024)} %param.16) | copy-start | bytes 64516
  6.5 93.5 %all-gather.3.cloned.1.call-start = ((), (), s32[]{:S(2)}) async-start(), calls=%async_computation | async-start | bytes 6193152 | tf_op jit(solution)/shard_map/all_gather | solution.py:370
  8.3 1.8 collective-permute-start
  21.5 147.6 %all-gather.5.cloned.1.call-start = ((), (), s32[]{:S(2)}) async-start(), calls=%async_computation.1 | async-start | bytes 3096576 | tf_op jit(solution)/shard_map/all_gather | solution.py:401
  26.1 31.0 %collective-permute-start.1 = (bf16[128,5376]{1,0:T(8,128)(2,1)}, bf16[128,5376]{1,0:T(8,128)(2,1)S(1)}, u32[]{:S(2)}, u32[]{:S(2)}) collective-permute-start(bf16[128,5376]{1,0:T(8,128)(2,1)} %input_norm.1.refs_0_), channel_id=1, source_target_pairs={{0,1},{1,2},{2,3},{3,0},{4,5},{5,6},{6,7},{7,4},{8,9},{9,10},{10,1... | collective-permute-start | bytes 4128776 | tf_op jit(solution)/shard_map/ppermute | solution.py:37
  27.3 29.8 %collective-permute-start.2 = (bf16[128,5376]{1,0:T(8,128)(2,1)}, bf16[128,5376]{1,0:T(8,128)(2,1)}, u32[]{:S(2)}, u32[]{:S(2)}) collective-permute-start(bf16[128,5376]{1,0:T(8,128)(2,1)} %input_norm.1.refs_0_), channel_id=1, source_target_pairs={{0,3},{1,0},{2,1},{3,2},{4,7},{5,4},{6,5},{7,6},{8,11},{9,8},{10,9... | collective-permute-start | bytes 4128776 | tf_op jit(solution)/shard_map/ppermute | solution.py:37
  33.6 1.0 collective-permute-start.3
  57.1 15.2 %copy-start.5 = (bf16[128,5376]{1,0:T(8,128)(2,1)}, bf16[128,5376]{1,0:T(8,128)(2,1)S(1)}, u32[]{:S(2)}) copy-start(bf16[128,5376]{1,0:T(8,128)(2,1)S(1)} %collective-permute-done.1.refs_4_) | copy-start | bytes 4128772
  57.1 13.8 %collective-permute-start.4 = (bf16[64,5376]{1,0:T(8,128)(2,1)S(1)}, bf16[64,5376]{1,0:T(8,128)(2,1)}, u32[]{:S(2)}, u32[]{:S(2)}) collective-permute-start(bf16[64,5376]{1,0:T(8,128)(2,1)S(1)} %slice.83), channel_id=1, source_target_pairs={{0,1},{1,2},{2,3},{3,0},{4,5},{5,6},{6,7},{7,4},{8,9},{9,10},{10,1... | collective-permute-start | bytes 2064392 | tf_op jit(solution)/shard_map/ppermute | solution.py:37
  61.4 10.8 %collective-permute-start.5 = (bf16[64,5376]{1,0:T(8,128)(2,1)}, bf16[64,5376]{1,0:T(8,128)(2,1)}, u32[]{:S(2)}, u32[]{:S(2)}) collective-permute-start(bf16[64,5376]{1,0:T(8,128)(2,1)} %slice.84), channel_id=1, source_target_pairs={{0,3},{1,0},{2,1},{3,2},{4,7},{5,4},{6,5},{7,6},{8,11},{9,8},{10,9... | collective-permute-start | bytes 2064392 | tf_op jit(solution)/shard_map/ppermute | solution.py:37
  63.1 36.9 %copy-start.1 = (s32[4]{0:T(128)S(1)}, s32[4]{0:T(128)}, u32[]{:S(2)}) copy-start(s32[4]{0:T(128)} %pad_add_fusion.1.place_ref) | copy-start | bytes 52
  63.1 36.9 %copy-start.2 = (f32[128]{0:T(128)S(1)}, f32[128]{0:T(128)}, u32[]{:S(2)}) copy-start(f32[128]{0:T(128)} %param.17) | copy-start | bytes 1540
  63.1 36.9 %copy-start.3 = (f32[128]{0:T(128)S(1)}, f32[128]{0:T(128)}, u32[]{:S(2)}) copy-start(f32[128]{0:T(128)} %param.18) | copy-start | bytes 1540
  80.6 29.5 %collective-permute-start.6 = (bf16[512,5376]{1,0:T(8,128)(2,1)}, bf16[512,5376]{1,0:T(8,128)(2,1)}, u32[]{:S(2)}, u32[]{:S(2)}) collective-permute-start(bf16[512,5376]{1,0:T(8,128)(2,1)} %place_rows.1.rows_hbm), channel_id=1, source_target_pairs={{0,4},{4,0},{8,12},{12,8},{16,20},{20,16},{24,28},{28,24},{32,36},... | collective-permute-start | bytes 16515080 | tf_op jit(solution)/shard_map/ppermute | solution.py:33
  108.2 12.5 %collective-permute-start.7 = (bf16[2,512,128]{2,1,0:T(8,128)(2,1)S(1)}, bf16[2,512,128]{2,1,0:T(8,128)(2,1)S(1)}, u32[]{:S(2)}, u32[]{:S(2)}) collective-permute-start(bf16[2,512,128]{2,1,0:T(8,128)(2,1)S(1)} %get-tuple-element.40.mine_ref), channel_id=1, source_target_pairs={{0,8},{4,12},{8,16},{12,20},{16,24},{20,28},{24,32},{28,36},{32,40... | collective-permute-start | bytes 786440 | tf_op jit(solution)/shard_map/ppermute | solution.py:42
  118.3 13.6 %collective-permute-start.8 = (bf16[2,512,128]{2,1,0:T(8,128)(2,1)S(1)}, bf16[2,512,128]{2,1,0:T(8,128)(2,1)S(1)}, u32[]{:S(2)}, u32[]{:S(2)}) collective-permute-start(bf16[2,512,128]{2,1,0:T(8,128)(2,1)S(1)} %get-tuple-element.41.other_ref), channel_id=1, source_target_pairs={{0,8},{4,12},{8,16},{12,20},{16,24},{20,28},{24,32},{28,36},{32,40... | collective-permute-start | bytes 786440 | tf_op jit(solution)/shard_map/ppermute | solution.py:42
  139.5 2.8 %collective-permute-start.9 = (bf16[512,256]{1,0:T(8,128)(2,1)S(1)}, bf16[512,256]{1,0:T(8,128)(2,1)S(1)}, u32[]{:S(2)}, u32[]{:S(2)}) collective-permute-start(bf16[512,256]{1,0:T(8,128)(2,1)S(1)} %get-tuple-element.45), channel_id=1, source_target_pairs={{0,4},{4,0},{8,12},{12,8},{16,20},{20,16},{24,28},{28,24},{32,36},... | collective-permute-start | bytes 786440 | tf_op jit(solution)/shard_map/ppermute | solution.py:33
  142.3 39.8 %copy-start.7 = (f32[5376]{0:T(1024)S(1)}, f32[5376]{0:T(1024)}, u32[]{:S(2)}) copy-start(f32[5376]{0:T(1024)} %param.19) | copy-start | bytes 64516
  142.3 58.6 %copy-start = (bf16[128,5376]{1,0:T(8,128)(2,1)S(1)}, bf16[128,5376]{1,0:T(8,128)(2,1)}, u32[]{:S(2)}) copy-start(bf16[128,5376]{1,0:T(8,128)(2,1)} %refs_4_.1) | copy-start | bytes 4128772
  142.3 13.2 %collective-permute-start.10 = (bf16[2,512,256]{2,1,0:T(8,128)(2,1)S(1)}, bf16[2,512,256]{2,1,0:T(8,128)(2,1)S(1)}, u32[]{:S(2)}, u32[]{:S(2)}) collective-permute-start(bf16[2,512,256]{2,1,0:T(8,128)(2,1)S(1)} %pad_maximum_fusion.2.refs_0_), channel_id=1, source_target_pairs={{0,3},{1,0},{2,1},{3,2},{4,7},{5,4},{6,5},{7,6},{8,11},{9,8},{10,9... | collective-permute-start | bytes 1572872 | tf_op jit(solution)/shard_map/ppermute | solution.py:37
  142.4 14.8 %collective-permute-start.11 = (bf16[2,512,256]{2,1,0:T(8,128)(2,1)S(1)}, bf16[2,512,256]{2,1,0:T(8,128)(2,1)S(1)}, u32[]{:S(2)}, u32[]{:S(2)}) collective-permute-start(bf16[2,512,256]{2,1,0:T(8,128)(2,1)S(1)} %pad_maximum_fusion.2.refs_0_), channel_id=1, source_target_pairs={{0,2},{1,3},{2,0},{3,1},{4,6},{5,7},{6,4},{7,5},{8,10},{9,11},{10,... | collective-permute-start | bytes 1572872 | tf_op jit(solution)/shard_map/ppermute | solution.py:37
  143.0 26.1 %collective-permute-start.12 = (bf16[2,512,256]{2,1,0:T(8,128)(2,1)S(1)}, bf16[2,512,256]{2,1,0:T(8,128)(2,1)S(1)}, u32[]{:S(2)}, u32[]{:S(2)}) collective-permute-start(bf16[2,512,256]{2,1,0:T(8,128)(2,1)S(1)} %pad_maximum_fusion.2.refs_0_), channel_id=1, source_target_pairs={{0,1},{1,2},{2,3},{3,0},{4,5},{5,6},{6,7},{7,4},{8,9},{9,10},{10,1... | collective-permute-start | bytes 1572872 | tf_op jit(solution)/shard_map/ppermute | solution.py:37
  169.1 5.4 %collective-permute-start.13 = (bf16[5376,256]{1,0:T(8,128)(2,1)}, bf16[5376,256]{1,0:T(8,128)(2,1)S(1)}, u32[]{:S(2)}, u32[]{:S(2)}) collective-permute-start(bf16[5376,256]{1,0:T(8,128)(2,1)} %all-gather.5.cloned.1.call-done.refs_4_), channel_id=1, source_target_pairs={{0,4},{4,0},{8,12},{12,8},{16,20},{20,16},{24,28},{28,24},{32,36},... | collective-permute-start | bytes 8257544 | tf_op jit(solution)/shard_map/ppermute | solution.py:33
  174.5 1.8 copy-start.4
  180.3 9.9 %collective-permute-start.14 = (bf16[128,1344]{1,0:T(8,128)(2,1)S(1)}, bf16[128,1344]{1,0:T(8,128)(2,1)S(1)}, u32[]{:S(2)}, u32[]{:S(2)}) collective-permute-start(bf16[128,1344]{1,0:T(8,128)(2,1)S(1)} %get-tuple-element.52), channel_id=1, source_target_pairs={{0,3},{1,0},{2,1},{3,2},{4,7},{5,4},{6,5},{7,6},{8,11},{9,8},{10,9... | collective-permute-start | bytes 1032200 | tf_op jit(solution)/shard_map/ppermute | solution.py:37
  181.4 10.9 %collective-permute-start.15 = (bf16[128,1344]{1,0:T(8,128)(2,1)S(1)}, bf16[128,1344]{1,0:T(8,128)(2,1)S(1)}, u32[]{:S(2)}, u32[]{:S(2)}) collective-permute-start(bf16[128,1344]{1,0:T(8,128)(2,1)S(1)} %get-tuple-element.53), channel_id=1, source_target_pairs={{0,2},{1,3},{2,0},{3,1},{4,6},{5,7},{6,4},{7,5},{8,10},{9,11},{10,... | collective-permute-start | bytes 1032200 | tf_op jit(solution)/shard_map/ppermute | solution.py:37
  181.4 19.5 %collective-permute-start.16 = (bf16[128,1344]{1,0:T(8,128)(2,1)S(1)}, bf16[128,1344]{1,0:T(8,128)(2,1)S(1)}, u32[]{:S(2)}, u32[]{:S(2)}) collective-permute-start(bf16[128,1344]{1,0:T(8,128)(2,1)S(1)} %get-tuple-element.54), channel_id=1, source_target_pairs={{0,1},{1,2},{2,3},{3,0},{4,5},{5,6},{6,7},{7,4},{8,9},{9,10},{10,1... | collective-permute-start | bytes 1032200 | tf_op jit(solution)/shard_map/ppermute | solution.py:37
Sparse Core Ops, SparseCore 0:
  21.7 78.2 all-gather.2
  101.8 47.2 all-gather.4
